TPU v7x, 128 devices: a whole 4x4x4 slice. The times are simulated.
128 devices in a mesh: leaf: 128 (over y, z, x, core).
Axes of the slice: x: 4, y: 4, z: 4, core: 2. Of those that a mesh axis runs over, the one named last changes fastest.
Arguments:
- rhs: bfloat16 [16, 1048576], P(None, 'leaf'), may hold values from -6 to 6
- leaf_basis: bfloat16 [4096, 256, 64], P('leaf'), may hold values from -0.375 to 0.375
- near_tiles: bfloat16 [4096, 4, 256, 256], P('leaf'), may hold values from -0.375 to 0.375
- near_pairs: int32 [4096, 4], P('leaf'), may hold values from 0 to 4095, as said below
- local_transfer: bfloat16 [7936, 64, 64], P('leaf'), may hold values from -0.625 to 0.625
- local_coupling: bfloat16 [7936, 64, 64], P('leaf'), may hold values from -0.75 to 0.75
- upper_transfer: bfloat16 [252, 64, 64], replicated, may hold values from -0.625 to 0.625
- upper_coupling: bfloat16 [254, 64, 64], replicated, may hold values from -0.75 to 0.75
Outputs:
- product: float32 [16, 1048576], P(None, 'leaf')
Inputs may be any that keep to these rules, and one draw needn't show every extreme that they name: near_pairs[n, 0] is n; every entry lies within 32 leaves of n, and entry 1 lies exactly 32 leaves away.
All inputs are finite; a program needn't handle non-finite values.
Results may differ from a plain program's by a relative error of at most 0.0003.
Values may be sent and summed in bfloat16 or wider, within the bound.
No kernel may reach another device: no remote copies, remote signals or barrier semaphores. Data moves between devices by JAX's collectives and lax.ppermute only.
A program may use at most 128 MiB of HBM per device.

v0:
```python
import jax
import jax.numpy as jnp
from jax import lax
from jax.sharding import PartitionSpec as P


def padded(array, sides, width):
    for axis, dim in sides:
        peers, length = (lax.axis_size(axis), array.shape[dim])
        up = [(i, (i + 1) % peers) for i in range(peers - 1)]
        down = [(j, i) for i, j in up]
        last = lax.slice_in_dim(array, length - width, length, axis=dim)
        leading = lax.slice_in_dim(array, 0, width, axis=dim)
        before = lax.ppermute(last, axis, up)
        after = lax.ppermute(leading, axis, down)
        array = jnp.concatenate([before, array, after], axis=dim)
    return array


def swapped(value, axis, bit):
    mask = 2**bit
    pairs = [(source, source ^ mask) for source in range(lax.axis_size(axis))]
    return lax.ppermute(value, axis, pairs)


def transfer_batch(coefficients, matrices):
    return jnp.einsum("nrk,nkj->nrj", coefficients, matrices, precision=lax.Precision.HIGHEST)


def adjoint_batch(fields, matrices):
    return jnp.einsum("nrj,nkj->nrk", fields, matrices, precision=lax.Precision.HIGHEST)


def swap_siblings(values):
    return values.reshape((-1, 2) + values.shape[1:])[:, ::-1].reshape(values.shape)


def times_matrix(values, matrix):
    return jnp.dot(values, matrix.astype(jnp.float32), precision=lax.Precision.HIGHEST)


def local(
    rhs,
    leaf_basis,
    near_tiles,
    near_pairs,
    local_transfer,
    local_coupling,
    upper_transfer,
    upper_coupling,
):
    leaf_count = leaf_basis.shape[0]
    leaf_size = leaf_basis.shape[1]
    rhs_count = rhs.shape[0]
    device_count = lax.axis_size("leaf")
    tree_depth = device_count.bit_length() - 1
    local_depth = leaf_count.bit_length() - 1
    position = lax.axis_index("leaf")
    extended = padded(rhs, (("leaf", 1),), leaf_count * leaf_size)
    ext_blocks = extended.reshape(rhs_count, 3 * leaf_count, leaf_size)
    local_index = near_pairs - (position * leaf_count - leaf_count)
    sources = jnp.take(ext_blocks, local_index, axis=1)
    nearby = jnp.einsum("lpij,rlpj->rli", near_tiles, sources, preferred_element_type=jnp.float32)
    own_blocks = rhs.reshape(rhs_count, leaf_count, leaf_size)
    coefficients = jnp.einsum(
        "rni,nik->nrk", own_blocks, leaf_basis, preferred_element_type=jnp.float32
    )
    trans_local = local_transfer.astype(jnp.float32)
    coup_local = local_coupling.astype(jnp.float32)
    local_trans_list = []
    local_far = []
    current = coefficients
    for height in range(local_depth):
        offset = 2 * leaf_count - (2 * leaf_count >> height)
        span = leaf_count >> height
        trans_here = trans_local[offset : offset + span]
        local_trans_list.append(trans_here)
        local_far.append(transfer_batch(swap_siblings(current), coup_local[offset : offset + span]))
        carried = transfer_batch(current, trans_here)
        current = carried[0::2] + carried[1::2]
    root_coef = current[0]
    siblings = []
    current_root = root_coef
    for height in range(tree_depth):
        partner = swapped(current_root, "leaf", height)
        siblings.append(partner)
        if height + 1 < tree_depth:
            offset = 2 * device_count - (2 * device_count >> height)
            node_index = position >> height
            mine = times_matrix(current_root, upper_transfer[offset + node_index])
            theirs = times_matrix(partner, upper_transfer[offset + (node_index ^ 1)])
            current_root = mine + theirs
    top_offset = 2 * device_count - (2 * device_count >> tree_depth - 1)
    fields = times_matrix(
        siblings[tree_depth - 1], upper_coupling[top_offset + (position >> tree_depth - 1)]
    )
    for height in range(tree_depth - 2, -1, -1):
        offset = 2 * device_count - (2 * device_count >> height)
        node_index = position >> height
        coupled = times_matrix(siblings[height], upper_coupling[offset + node_index])
        fields = coupled + times_matrix(fields, upper_transfer[offset + node_index].T)
    fields = fields[None]
    for height in range(local_depth - 1, -1, -1):
        parent = jnp.repeat(fields, 2, axis=0)
        fields = local_far[height] + adjoint_batch(parent, local_trans_list[height])
    far_out = jnp.einsum(
        "nrk,nik->rni", fields, leaf_basis.astype(jnp.float32), precision=lax.Precision.HIGHEST
    )
    return (far_out + nearby).reshape(rhs_count, leaf_count * leaf_size)


def solution(mesh):
    return jax.shard_map(
        local,
        mesh=mesh,
        in_specs=(
            P(None, "leaf"),
            P("leaf", None, None),
            P("leaf", None, None, None),
            P("leaf", None),
            P("leaf", None, None),
            P("leaf", None, None),
            P(),
            P(),
        ),
        out_specs=P(None, "leaf"),
        check_vma=False,
    )
```

profile of v0, /device:TPU:0, one launch (start us, length us, event | category | flops | bytes accessed | tf_op | source)
XLA Modules:
  0.0 122.5 jit_solution(9880515750264457728)
XLA Ops:
  0.0 2.1 %collective-permute-start.7 = (bf16[16,8192]{1,0:T(8,128)(2,1)}, bf16[16,8192]{1,0:T(8,128)(2,1)}, u32[]{:S(2)}, u32[]{:S(2)}) collective-permute-start(bf16[16,8192]{1,0:T(8,128)(2,1)} %param.8), channel_id=1, source_target_pairs={{0,1},{1,2},{2,3},{3,4},{4,5},{5,6},{6,7},{7,8},{8,9},{9,10},{10,1... | collective-permute-start | bytes 786440 | tf_op jit(solution)/shard_map/ppermute | solution.py:14
  12.7 2.2 %collective-permute-start = (f32[16,64]{1,0:T(8,128)}, f32[16,64]{1,0:T(8,128)}, u32[]{:S(2)}, u32[]{:S(2)}) collective-permute-start(f32[16,64]{1,0:T(8,128)} %fusion.71), channel_id=1, source_target_pairs={{0,1},{1,0},{2,3},{3,2},{4,5},{5,4},{6,7},{7,6},{8,9},{9,8},{10,11... | collective-permute-start | bytes 12296 | tf_op jit(solution)/shard_map/ppermute | solution.py:23
  15.5 7.0 %constant_dynamic-slice_fusion.1 = (bf16[1,64,64]{0,2,1:T(8,128)(2,1)}, bf16[1,64,64]{0,2,1:T(8,128)(2,1)}, bf16[1,64,64]{0,2,1:T(8,128)(2,1)}, bf16[1,64,64]{0,...) fusion(bf16[252,64,64]{0,2,1:T(8,128)(2,1)S(1)} %copy-done.1, ...), kind=kLoop, calls=%fused_computation.102 | loop fusion | bytes 196656 | tf_op jit(solution)/shard_map/dynamic_slice | solution.py:91
  22.5 1.8 %copy.62 = bf16[1,64,64]{2,1,0:T(8,128)(2,1)S(1)} copy(bf16[1,64,64]{0,2,1:T(8,128)(2,1)} %get-tuple-element.25) | data formatting | bytes 16384
  31.8 1.8 %fusion.18 = f32[8,16,64]{2,1,0:T(8,128)} fusion(f32[8,16,64]{2,1,0:T(8,128)} %bitcast.158, bf16[62,64,64]{2,1,0:T(8,128)(2,1)} %param.13), kind=kOutput, calls=%fused_computation.40 | convolution fusion | flops 6291456 | bytes 229376 | tf_op jit(solution)/shard_map/nrk,nkj->nrj/dot_general | solution.py:27
  36.3 2.3 %fusion.5 = f32[32,16,64]{2,1,0:T(8,128)} fusion(f32[32,16,64]{2,1,0:T(8,128)} %bitcast.151, bf16[62,64,64]{2,1,0:T(8,128)(2,1)} %param.13), kind=kOutput, calls=%fused_computation.27 | convolution fusion | flops 25165824 | bytes 917504 | tf_op jit(solution)/shard_map/nrk,nkj->nrj/dot_general | solution.py:27
  38.6 5.2 %constant_dynamic-slice_fusion.18 = (bf16[1,64,64]{0,2,1:T(8,128)(2,1)}, bf16[1,64,64]{0,2,1:T(8,128)(2,1)}, bf16[1,64,64]{0,2,1:T(8,128)(2,1)}, bf16[1,64,64]{0...) fusion(bf16[254,64,64]{0,2,1:T(8,128)(2,1)S(1)} %copy-done.2, ...), kind=kLoop, calls=%fused_computation.119 | loop fusion | bytes 114716 | tf_op jit(solution)/shard_map/dynamic_slice | solution.py:100
  44.4 1.8 %copy.63 = bf16[1,64,64]{2,1,0:T(8,128)(2,1)S(1)} copy(bf16[1,64,64]{0,2,1:T(8,128)(2,1)} %get-tuple-element.24) | data formatting | bytes 16384
  46.1 1.8 %copy.65 = bf16[1,64,64]{2,1,0:T(8,128)(2,1)S(1)} copy(bf16[1,64,64]{0,2,1:T(8,128)(2,1)} %get-tuple-element.23) | data formatting | bytes 16384
  47.9 1.7 %copy.66 = bf16[1,64,64]{2,1,0:T(8,128)(2,1)S(1)} copy(bf16[1,64,64]{0,2,1:T(8,128)(2,1)} %get-tuple-element.22) | data formatting | bytes 16384
  49.6 1.7 %copy.68 = bf16[1,64,64]{2,1,0:T(8,128)(2,1)S(1)} copy(bf16[1,64,64]{0,2,1:T(8,128)(2,1)} %get-tuple-element.21) | data formatting | bytes 16384
  52.2 1.8 %copy.72 = bf16[1,64,64]{2,1,0:T(8,128)(2,1)S(1)} copy(bf16[1,64,64]{0,2,1:T(8,128)(2,1)} %get-tuple-element.18) | data formatting | bytes 16384
  54.0 1.7 %copy.74 = bf16[1,64,64]{2,1,0:T(8,128)(2,1)S(1)} copy(bf16[1,64,64]{0,2,1:T(8,128)(2,1)} %get-tuple-element.17) | data formatting | bytes 16384
  61.2 1.9 %collective-permute-done.1 = f32[16,64]{1,0:T(8,128)S(1)} collective-permute-done((f32[16,64]{1,0:T(8,128)S(1)}, f32[16,64]{1,0:T(8,128)S(1)}, u32[]{:S(2)}, u32[]{:S(2)}) %collective-permute-start.1) | collective-permute-done | bytes 4128 | tf_op jit(solution)/shard_map/ppermute | solution.py:23
  63.2 3.2 %collective-permute-start.2 = (f32[16,64]{1,0:T(8,128)S(1)}, f32[16,64]{1,0:T(8,128)S(1)}, u32[]{:S(2)}, u32[]{:S(2)}) collective-permute-start(f32[16,64]{1,0:T(8,128)S(1)} %convolution_add_fusion.14), channel_id=1, source_target_pairs={{0,4},{1,5},{2,6},{3,7},{4,0},{5,1},{6,2},{7,3},{8,12},{9,13},{10,... | collective-permute-start | bytes 12296 | tf_op jit(solution)/shard_map/ppermute | solution.py:23
  66.5 1.9 %collective-permute-done.2 = f32[16,64]{1,0:T(8,128)S(1)} collective-permute-done((f32[16,64]{1,0:T(8,128)S(1)}, f32[16,64]{1,0:T(8,128)S(1)}, u32[]{:S(2)}, u32[]{:S(2)}) %collective-permute-start.2) | collective-permute-done | bytes 4128 | tf_op jit(solution)/shard_map/ppermute | solution.py:23
  68.5 4.2 %collective-permute-start.3 = (f32[16,64]{1,0:T(8,128)S(1)}, f32[16,64]{1,0:T(8,128)S(1)}, u32[]{:S(2)}, u32[]{:S(2)}) collective-permute-start(f32[16,64]{1,0:T(8,128)S(1)} %convolution_add_fusion.12), channel_id=1, source_target_pairs={{0,8},{1,9},{2,10},{3,11},{4,12},{5,13},{6,14},{7,15},{8,0},{9,1},... | collective-permute-start | bytes 12296 | tf_op jit(solution)/shard_map/ppermute | solution.py:23
  74.4 4.1 %collective-permute-start.4 = (f32[16,64]{1,0:T(8,128)S(1)}, f32[16,64]{1,0:T(8,128)S(1)}, u32[]{:S(2)}, u32[]{:S(2)}) collective-permute-start(f32[16,64]{1,0:T(8,128)S(1)} %convolution_add_fusion.10), channel_id=1, source_target_pairs={{0,16},{1,17},{2,18},{3,19},{4,20},{5,21},{6,22},{7,23},{8,24},{9,... | collective-permute-start | bytes 12296 | tf_op jit(solution)/shard_map/ppermute | solution.py:23
  80.3 3.3 %collective-permute-start.5 = (f32[16,64]{1,0:T(8,128)S(1)}, f32[16,64]{1,0:T(8,128)S(1)}, u32[]{:S(2)}, u32[]{:S(2)}) collective-permute-start(f32[16,64]{1,0:T(8,128)S(1)} %convolution_add_fusion.8), channel_id=1, source_target_pairs={{0,32},{1,33},{2,34},{3,35},{4,36},{5,37},{6,38},{7,39},{8,40},{9,... | collective-permute-start | bytes 12296 | tf_op jit(solution)/shard_map/ppermute | solution.py:23
  86.1 3.6 %collective-permute-start.6 = (f32[16,64]{1,0:T(8,128)}, f32[16,64]{1,0:T(8,128)}, u32[]{:S(2)}, u32[]{:S(2)}) collective-permute-start(f32[16,64]{1,0:T(8,128)} %convolution_add_fusion.6), channel_id=1, source_target_pairs={{0,64},{1,65},{2,66},{3,67},{4,68},{5,69},{6,70},{7,71},{8,72},{9,... | collective-permute-start | bytes 12296 | tf_op jit(solution)/shard_map/ppermute | solution.py:23
  91.8 2.4 %copy.73 = bf16[1,64,64]{2,1,0:T(8,128)(2,1)} copy(bf16[1,64,64]{0,2,1:T(8,128)(2,1)} %get-tuple-element.9) | data formatting | bytes 16384
  95.9 1.7 %copy.67 = bf16[1,64,64]{2,1,0:T(8,128)(2,1)S(1)} copy(bf16[1,64,64]{0,2,1:T(8,128)(2,1)} %get-tuple-element.11) | data formatting | bytes 16384
  109.3 1.9 %convolution_add_fusion.1 = f32[32,16,64]{2,1,0:T(8,128)S(1)} fusion(f32[32,16,64]{2,1,0:T(8,128)} %fusion.5, f32[32,16,64]{2,1,0:T(8,128)S(1)} %bitcast.150, bf16[62,64,64]{2,1,0:T(8,128)(2,1)S(1)} %copy-done.11), kind=kOutput, calls=%fused_computation.4 | convolution fusion | flops 25198592 | bytes 1048576 | tf_op jit(solution)/shard_map/nrj,nkj->nrk/dot_general | solution.py:31
  113.0 8.1 %convolution_bitcast_fusion = f32[32,16,256]{2,1,0:T(8,128)S(1)} fusion(bf16[32,4,256,256]{3,2,1,0:T(8,128)(2,1)} %param.10, bf16[32,4,16,256]{3,2,1,0:T(8,128)(2,1)S(1)} %bitcast.146, pred[32,4]{1,0:T(8,128)(4,1)S(1)} %copy.56), kind=kOutput, calls=%fused_computation.1 | convolution fusion | flops 268959744 | bytes 18350208 | tf_op jit(solution)/shard_map/lpij,rlpj->rli/dot_general | solution.py:63
  (127 shorter events, 53.1 us)
Async XLA Ops:
  0.0 111.2 %collective-permute-start.7 = (bf16[16,8192]{1,0:T(8,128)(2,1)}, bf16[16,8192]{1,0:T(8,128)(2,1)}, u32[]{:S(2)}, u32[]{:S(2)}) collective-permute-start(bf16[16,8192]{1,0:T(8,128)(2,1)} %param.8), channel_id=1, source_target_pairs={{0,1},{1,2},{2,3},{3,4},{4,5},{5,6},{6,7},{7,8},{8,9},{9,10},{10,1... | collective-permute-start | bytes 786440 | tf_op jit(solution)/shard_map/ppermute | solution.py:14
  2.1 109.1 %collective-permute-start.8 = (bf16[16,8192]{1,0:T(8,128)(2,1)}, bf16[16,8192]{1,0:T(8,128)(2,1)}, u32[]{:S(2)}, u32[]{:S(2)}) collective-permute-start(bf16[16,8192]{1,0:T(8,128)(2,1)} %param.8), channel_id=1, source_target_pairs={{1,0},{2,1},{3,2},{4,3},{5,4},{6,5},{7,6},{8,7},{9,8},{10,9},{11,1... | collective-permute-start | bytes 786440 | tf_op jit(solution)/shard_map/ppermute | solution.py:15
  3.4 12.1 %copy-start.1 = (bf16[252,64,64]{0,2,1:T(8,128)(2,1)S(1)}, bf16[252,64,64]{0,2,1:T(8,128)(2,1)}, u32[]{:S(2)}) copy-start(bf16[252,64,64]{0,2,1:T(8,128)(2,1)} %param.14) | copy-start | bytes 6193156
  12.7 45.8 %collective-permute-start = (f32[16,64]{1,0:T(8,128)}, f32[16,64]{1,0:T(8,128)}, u32[]{:S(2)}, u32[]{:S(2)}) collective-permute-start(f32[16,64]{1,0:T(8,128)} %fusion.71), channel_id=1, source_target_pairs={{0,1},{1,0},{2,3},{3,2},{4,5},{5,4},{6,7},{7,6},{8,9},{9,8},{10,11... | collective-permute-start | bytes 12296 | tf_op jit(solution)/shard_map/ppermute | solution.py:23
  22.5 16.1 %copy-start.2 = (bf16[254,64,64]{0,2,1:T(8,128)(2,1)S(1)}, bf16[254,64,64]{0,2,1:T(8,128)(2,1)}, u32[]{:S(2)}) copy-start(bf16[254,64,64]{0,2,1:T(8,128)(2,1)} %param.15) | copy-start | bytes 6242308
  44.4 6.9 %copy-start.6 = (bf16[1,64,64]{0,2,1:T(8,128)(2,1)S(1)}, bf16[1,64,64]{0,2,1:T(8,128)(2,1)}, u32[]{:S(2)}) copy-start(bf16[1,64,64]{0,2,1:T(8,128)(2,1)} %get-tuple-element.20) | copy-start | bytes 24580
  57.8 31.9 %copy-start.10 = (bf16[1,64,64]{0,2,1:T(8,128)(2,1)S(1)}, bf16[1,64,64]{0,2,1:T(8,128)(2,1)}, u32[]{:S(2)}) copy-start(bf16[1,64,64]{0,2,1:T(8,128)(2,1)} %get-tuple-element.13) | copy-start | bytes 24580
  58.3 32.5 %copy-start.9 = (bf16[1,64,64]{0,2,1:T(8,128)(2,1)S(1)}, bf16[1,64,64]{0,2,1:T(8,128)(2,1)}, u32[]{:S(2)}) copy-start(bf16[1,64,64]{0,2,1:T(8,128)(2,1)} %get-tuple-element.8) | copy-start | bytes 24580
  59.4 3.7 %collective-permute-start.1 = (f32[16,64]{1,0:T(8,128)S(1)}, f32[16,64]{1,0:T(8,128)S(1)}, u32[]{:S(2)}, u32[]{:S(2)}) collective-permute-start(f32[16,64]{1,0:T(8,128)S(1)} %convolution_add_fusion.16), channel_id=1, source_target_pairs={{0,2},{1,3},{2,0},{3,1},{4,6},{5,7},{6,4},{7,5},{8,10},{9,11},{10,... | collective-permute-start | bytes 12296 | tf_op jit(solution)/shard_map/ppermute | solution.py:23
  63.2 5.2 %collective-permute-start.2 = (f32[16,64]{1,0:T(8,128)S(1)}, f32[16,64]{1,0:T(8,128)S(1)}, u32[]{:S(2)}, u32[]{:S(2)}) collective-permute-start(f32[16,64]{1,0:T(8,128)S(1)} %convolution_add_fusion.14), channel_id=1, source_target_pairs={{0,4},{1,5},{2,6},{3,7},{4,0},{5,1},{6,2},{7,3},{8,12},{9,13},{10,... | collective-permute-start | bytes 12296 | tf_op jit(solution)/shard_map/ppermute | solution.py:23
  68.4 25.8 %copy-start.17 = (f32[16,64]{1,0:T(8,128)}, f32[16,64]{1,0:T(8,128)S(1)}, u32[]{:S(2)}) copy-start(f32[16,64]{1,0:T(8,128)S(1)} %collective-permute-done.2) | copy-start | bytes 12292
  68.5 5.8 %collective-permute-start.3 = (f32[16,64]{1,0:T(8,128)S(1)}, f32[16,64]{1,0:T(8,128)S(1)}, u32[]{:S(2)}, u32[]{:S(2)}) collective-permute-start(f32[16,64]{1,0:T(8,128)S(1)} %convolution_add_fusion.12), channel_id=1, source_target_pairs={{0,8},{1,9},{2,10},{3,11},{4,12},{5,13},{6,14},{7,15},{8,0},{9,1},... | collective-permute-start | bytes 12296 | tf_op jit(solution)/shard_map/ppermute | solution.py:23
  74.3 19.9 %copy-start.18 = (f32[16,64]{1,0:T(8,128)}, f32[16,64]{1,0:T(8,128)S(1)}, u32[]{:S(2)}) copy-start(f32[16,64]{1,0:T(8,128)S(1)} %collective-permute-done.3) | copy-start | bytes 12292
  74.4 5.8 %collective-permute-start.4 = (f32[16,64]{1,0:T(8,128)S(1)}, f32[16,64]{1,0:T(8,128)S(1)}, u32[]{:S(2)}, u32[]{:S(2)}) collective-permute-start(f32[16,64]{1,0:T(8,128)S(1)} %convolution_add_fusion.10), channel_id=1, source_target_pairs={{0,16},{1,17},{2,18},{3,19},{4,20},{5,21},{6,22},{7,23},{8,24},{9,... | collective-permute-start | bytes 12296 | tf_op jit(solution)/shard_map/ppermute | solution.py:23
  80.2 14.0 %copy-start.19 = (f32[16,64]{1,0:T(8,128)}, f32[16,64]{1,0:T(8,128)S(1)}, u32[]{:S(2)}) copy-start(f32[16,64]{1,0:T(8,128)S(1)} %collective-permute-done.4) | copy-start | bytes 12292
  80.3 5.0 %collective-permute-start.5 = (f32[16,64]{1,0:T(8,128)S(1)}, f32[16,64]{1,0:T(8,128)S(1)}, u32[]{:S(2)}, u32[]{:S(2)}) collective-permute-start(f32[16,64]{1,0:T(8,128)S(1)} %convolution_add_fusion.8), channel_id=1, source_target_pairs={{0,32},{1,33},{2,34},{3,35},{4,36},{5,37},{6,38},{7,39},{8,40},{9,... | collective-permute-start | bytes 12296 | tf_op jit(solution)/shard_map/ppermute | solution.py:23
  85.3 8.9 %copy-start.20 = (f32[16,64]{1,0:T(8,128)}, f32[16,64]{1,0:T(8,128)S(1)}, u32[]{:S(2)}) copy-start(f32[16,64]{1,0:T(8,128)S(1)} %collective-permute-done.5) | copy-start | bytes 12292
  86.1 13.3 %collective-permute-start.6 = (f32[16,64]{1,0:T(8,128)}, f32[16,64]{1,0:T(8,128)}, u32[]{:S(2)}, u32[]{:S(2)}) collective-permute-start(f32[16,64]{1,0:T(8,128)} %convolution_add_fusion.6), channel_id=1, source_target_pairs={{0,64},{1,65},{2,66},{3,67},{4,68},{5,69},{6,70},{7,71},{8,72},{9,... | collective-permute-start | bytes 12296 | tf_op jit(solution)/shard_map/ppermute | solution.py:23
  90.8 6.8 %copy-start.8 = (bf16[1,64,64]{0,2,1:T(8,128)(2,1)S(1)}, bf16[1,64,64]{0,2,1:T(8,128)(2,1)}, u32[]{:S(2)}) copy-start(bf16[1,64,64]{0,2,1:T(8,128)(2,1)} %get-tuple-element.12) | copy-start | bytes 24580
  91.8 6.2 %copy-start.7 = (bf16[1,64,64]{0,2,1:T(8,128)(2,1)S(1)}, bf16[1,64,64]{0,2,1:T(8,128)(2,1)}, u32[]{:S(2)}) copy-start(bf16[1,64,64]{0,2,1:T(8,128)(2,1)} %get-tuple-element.7) | copy-start | bytes 24580
  95.9 10.5 %copy-start.16 = (f32[4,16,64]{2,1,0:T(8,128)S(1)}, f32[4,16,64]{2,1,0:T(8,128)}, u32[]{:S(2)}) copy-start(f32[4,16,64]{2,1,0:T(8,128)} %fusion.23) | copy-start | bytes 49156
  95.9 11.6 %copy-start.15 = (f32[8,16,64]{2,1,0:T(8,128)S(1)}, f32[8,16,64]{2,1,0:T(8,128)}, u32[]{:S(2)}) copy-start(f32[8,16,64]{2,1,0:T(8,128)} %fusion.18) | copy-start | bytes 98308
  98.1 10.7 %copy-start.11 = (bf16[62,64,64]{2,1,0:T(8,128)(2,1)S(1)}, bf16[62,64,64]{2,1,0:T(8,128)(2,1)}, u32[]{:S(2)}) copy-start(bf16[62,64,64]{2,1,0:T(8,128)(2,1)} %param.12) | copy-start | bytes 1523716
  98.6 12.7 %copy-start.12 = (bf16[16,8192]{1,0:T(8,128)(2,1)S(1)}, bf16[16,8192]{1,0:T(8,128)(2,1)}, u32[]{:S(2)}) copy-start(bf16[16,8192]{1,0:T(8,128)(2,1)} %param.8) | copy-start | bytes 786436
  (8 other events, 31.3 us)
where the time goes:
time: 124 us; the launch traced here: 122 us
  local copies, waits for them, and re-layouts  45.5 us (37%)
  matrix products  40.4 us (33%)
  starting transfers between devices  25.8 us (21%)
  waiting for transfers between devices  8.33 us (7%)
  other arithmetic  2.27 us (2%)
    unnamed x65, local copies, waits for them, and re-layouts  25.9 us
    ppermute x7, starting transfers between devices, swapped(): return lax.ppermute(value, axis, pairs)  22.3 us
    dot_general x10, matrix products, transfer_batch(): jnp.einsum('nrk,nkj->nrj', coefficients, matrices, precision=lax.Precisio...  14.5 us
    dot_general x25, matrix products, times_matrix(): jnp.dot(values, matrix.astype(jnp.float32), precision=lax.Precision.HIGHEST)  10.3 us
    ppermute x7, waiting for transfers between devices, swapped(): return lax.ppermute(value, axis, pairs)  8.32 us
    dot_general x1, matrix products, local(): jnp.einsum('lpij,rlpj->rli', near_tiles, sources, preferred_element_type=...  8.06 us
    dynamic_slice x1, local copies, waits for them, and re-layouts, local(): theirs = times_matrix(partner, upper_transfer[offset + (node_index ^ 1)])  7.01 us
    dot_general x5, matrix products, adjoint_batch(): jnp.einsum('nrj,nkj->nrk', fields, matrices, precision=lax.Precision.HIGH...  5.53 us
  transfers between devices with their start and end apart: 9, of which 5 were waited for; matrix products, arithmetic and copies ran while one was open for 62% of the time, Pallas kernels for 0%

commit v1 on v0

v1 whole, which is shorter than its diff:
```python
import functools

import jax
import jax.numpy as jnp
from jax import lax
from jax.experimental import pallas as pl
from jax.experimental.pallas import tpu as pltpu
from jax.sharding import PartitionSpec as P

F32 = jnp.float32
BF16 = jnp.bfloat16
ANY = pl.BlockSpec(memory_space=pl.ANY)
VMEM = pl.BlockSpec(memory_space=pltpu.VMEM)
SMEM = pl.BlockSpec(memory_space=pltpu.SMEM)
NEAR_CHUNKS = (4, 6, 6, 6, 6, 4)
LEAVES_PER_STEP = 2


def split_rows(value):
    high = value.astype(BF16)
    low = (value - high.astype(F32)).astype(BF16)
    return jnp.concatenate([high, low], axis=0)


def join_rows(value):
    half = value.shape[0] // 2
    return value[:half] + value[half:]


def times(value, matrix):
    return join_rows(jnp.dot(split_rows(value), matrix, preferred_element_type=F32))


def times_transposed(value, matrix):
    dims = (((1,), (1,)), ((), ()))
    return join_rows(
        lax.dot_general(split_rows(value), matrix, dims, preferred_element_type=F32)
    )


def left_half(shape):
    return lax.broadcasted_iota(jnp.int32, shape, 1) < 64


def apart(pair):
    left = left_half(pair.shape)
    return jnp.concatenate([jnp.where(left, pair, 0.0), jnp.where(left, 0.0, pair)], axis=0)


def pick_nodes(position, matrices, picked):
    nodes = matrices.shape[2]
    count = 2 * 128
    row = lax.broadcasted_iota(jnp.int32, (8, nodes), 0)
    lane = lax.broadcasted_iota(jnp.int32, (8, nodes), 1)
    start = count - lax.shift_right_logical(jnp.full_like(row, count), row)
    wanted = start + lax.shift_right_logical(jnp.full_like(row, position), row)
    chosen = jnp.where(lane == wanted, 1.0, 0.0).astype(BF16)
    dims = (((1,), (1,)), ((), ()))
    for group in range(16):
        block = matrices[4 * group : 4 * group + 4].reshape(256, nodes)
        rows = lax.dot_general(chosen, block, dims, preferred_element_type=F32)
        shifted = pltpu.roll(rows, 64, 1)
        for half in range(2):
            lanes = slice(128 * half, 128 * half + 128)
            picked[pl.ds(4 * group + 2 * half, 8, stride=64), :] = rows[:, lanes]
            other = slice(128 * (1 - half), 128 * (1 - half) + 128)
            del other
            place = (128 * (half + 1)) % 256
            picked[pl.ds(4 * group + 2 * half + 1, 8, stride=64), :] = shifted[:, place : place + 128]


def up_kernel(pos_ref, rhs_hbm, basis_hbm, trans_hbm, upper_hbm, coef_ref, path_ref, upper_ref,
              rhs, basis, trans, upper, picked, sems):
    copies = [
        pltpu.make_async_copy(source, target, sems.at[i])
        for i, (source, target) in enumerate(
            [(rhs_hbm, rhs), (basis_hbm, basis), (trans_hbm, trans), (upper_hbm, upper)]
        )
    ]
    for copy in copies:
        copy.start()
    copies[0].wait()
    copies[1].wait()
    dims = (((1,), (1,)), ((), ()))
    current = []
    for pair in range(16):
        first = rhs[:, 512 * pair : 512 * pair + 256]
        second = rhs[:, 512 * pair + 256 : 512 * pair + 512]
        sources = jnp.concatenate([first, second], axis=0)
        both = lax.dot_general(
            sources, basis[2 * pair : 2 * pair + 2].reshape(128, 256), dims, preferred_element_type=F32
        )
        value = jnp.where(left_half((16, 128)), both[:16], both[16:])
        coef_ref[pair] = value
        current.append(value)
    copies[2].wait()
    base = 0
    while True:
        parents = [
            times(value, trans[2 * (base + i) : 2 * (base + i) + 2].reshape(128, 64))
            for i, value in enumerate(current)
        ]
        base += len(current)
        if len(parents) == 1:
            break
        current = [
            jnp.concatenate([parents[2 * i], parents[2 * i + 1]], axis=1) for i in range(len(parents) // 2)
        ]
        for i, value in enumerate(current):
            coef_ref[base + i] = value
    copies[3].wait()
    pick_nodes(pos_ref[0], upper, picked)
    value = parents[0]
    path_ref[:, 384:448] = value
    for level in range(6):
        matrix = picked[64 * level : 64 * level + 64, 0:64].astype(BF16)
        upper_ref[level] = matrix
        value = times(value, matrix)
        start = 64 * (5 - level)
        path_ref[:, start : start + 64] = value


def up_sweep(position, rhs, basis_t, local_transfer, upper_transfer_t):
    return pl.pallas_call(
        up_kernel,
        out_shape=(
            jax.ShapeDtypeStruct((31, 16, 128), F32),
            jax.ShapeDtypeStruct((16, 448), F32),
            jax.ShapeDtypeStruct((6, 64, 64), BF16),
        ),
        in_specs=[SMEM, ANY, ANY, ANY, ANY],
        out_specs=(VMEM, VMEM, VMEM),
        scratch_shapes=[
            pltpu.VMEM(rhs.shape, BF16),
            pltpu.VMEM(basis_t.shape, BF16),
            pltpu.VMEM(local_transfer.shape, BF16),
            pltpu.VMEM(upper_transfer_t.shape, BF16),
            pltpu.VMEM((512, 128), F32),
            pltpu.SemaphoreType.DMA((4,)),
        ],
        compiler_params=pltpu.CompilerParams(vmem_limit_bytes=20 * 2**20),
        cost_estimate=pl.CostEstimate(flops=10**8, bytes_accessed=5 * 2**20, transcendentals=0),
        name="up_sweep",
    )(position, rhs, basis_t, local_transfer, upper_transfer_t)


def far_kernel(pos_ref, coef, coup_hbm, upper_hbm, far_ref, upper_ref, coup, upper, picked, sems):
    copies = [
        pltpu.make_async_copy(coup_hbm, coup, sems.at[0]),
        pltpu.make_async_copy(upper_hbm, upper, sems.at[1]),
    ]
    for copy in copies:
        copy.start()
    copies[0].wait()
    for pair in range(31):
        swapped = pltpu.roll(coef[pair], 64, 1)
        both = times(apart(swapped), coup[2 * pair : 2 * pair + 2].reshape(128, 64))
        far_ref[pair] = jnp.concatenate([both[:16], both[16:]], axis=1)
    copies[1].wait()
    pick_nodes(pos_ref[0], upper, picked)
    for level in range(7):
        upper_ref[level] = picked[64 * level : 64 * level + 64, 0:64].astype(BF16)


def far_fields(position, coef, local_coupling, upper_coupling_t):
    return pl.pallas_call(
        far_kernel,
        out_shape=(
            jax.ShapeDtypeStruct((31, 16, 128), F32),
            jax.ShapeDtypeStruct((7, 64, 64), BF16),
        ),
        in_specs=[SMEM, VMEM, ANY, ANY],
        out_specs=(VMEM, VMEM),
        scratch_shapes=[
            pltpu.VMEM(local_coupling.shape, BF16),
            pltpu.VMEM(upper_coupling_t.shape, BF16),
            pltpu.VMEM((512, 128), F32),
            pltpu.SemaphoreType.DMA((2,)),
        ],
        compiler_params=pltpu.CompilerParams(vmem_limit_bytes=20 * 2**20),
        cost_estimate=pl.CostEstimate(flops=10**8, bytes_accessed=5 * 2**20, transcendentals=0),
        name="far_fields",
    )(position, coef, local_coupling, upper_coupling_t)


def near_kernel(first, index_ref, before, own, after, order, tiles, out_ref):
    del order
    step = pl.program_id(0)
    dims = (((1,), (1,)), ((), ()))
    for i in range(LEAVES_PER_STEP):
        leaf = first + step * LEAVES_PER_STEP + i
        total = jnp.zeros((16, 256), F32)
        for k in range(4):
            index = index_ref[leaf, k]
            side = lax.shift_right_logical(index, 5)
            column = pl.ds(pl.multiple_of((index & 31) * 256, 256), 256)
            source = jnp.where(
                side == 0, before[:, column], jnp.where(side == 1, own[:, column], after[:, column])
            )
            total += lax.dot_general(source, tiles[i, k], dims, preferred_element_type=F32)
        out_ref[:, 256 * i : 256 * i + 256] = total


def near_field(first, count, index, before, own, after, order, tiles):
    steps = count // LEAVES_PER_STEP
    start = first // LEAVES_PER_STEP
    return pl.pallas_call(
        functools.partial(near_kernel, first),
        grid=(steps,),
        out_shape=jax.ShapeDtypeStruct((16, 256 * count), F32),
        in_specs=[
            SMEM,
            VMEM,
            VMEM,
            VMEM,
            ANY,
            pl.BlockSpec((LEAVES_PER_STEP, 4, 256, 256), lambda i: (start + i, 0, 0, 0)),
        ],
        out_specs=pl.BlockSpec((16, 256 * LEAVES_PER_STEP), lambda i: (0, i)),
        compiler_params=pltpu.CompilerParams(vmem_limit_bytes=20 * 2**20),
        cost_estimate=pl.CostEstimate(
            flops=count * 4 * 256 * 256 * 32, bytes_accessed=count * 4 * 2**17, transcendentals=0
        ),
        name="near_field",
    )(index, before, own, after, order, tiles)


def down_kernel(*refs):
    siblings = refs[:7]
    upper_trans, upper_coup, far, trans_hbm, basis_hbm = refs[7:12]
    nearby = refs[12 : 12 + len(NEAR_CHUNKS)]
    out_ref, trans, basis, sems = refs[12 + len(NEAR_CHUNKS) :]
    copies = [
        pltpu.make_async_copy(trans_hbm, trans, sems.at[0]),
        pltpu.make_async_copy(basis_hbm, basis, sems.at[1]),
    ]
    for copy in copies:
        copy.start()
    field = None
    for level in range(6, -1, -1):
        width = 64 * (7 - level)
        term = times(siblings[level][:, width - 64 : width], upper_coup[level])
        field = term if field is None else term + times_transposed(field, upper_trans[level])
    copies[0].wait()
    fields = [field]
    base = 31
    while len(fields) < 32:
        base -= len(fields)
        pairs = [
            far[base + i] + times_transposed(value, trans[2 * (base + i) : 2 * (base + i) + 2].reshape(128, 64))
            for i, value in enumerate(fields)
        ]
        if len(pairs) == 16:
            break
        fields = []
        for pair in pairs:
            fields += [pair[:, 0:64], pair[:, 64:128]]
    copies[1].wait()
    leaf = 0
    for nearby_ref, count in zip(nearby, NEAR_CHUNKS):
        for i in range(0, count, 2):
            both = times(apart(pairs[leaf // 2]), basis[leaf : leaf + 2].reshape(128, 256))
            for j in range(2):
                out_ref[:, 256 * (leaf + j) : 256 * (leaf + j) + 256] = (
                    both[16 * j : 16 * j + 16] + nearby_ref[:, 256 * (i + j) : 256 * (i + j) + 256]
                )
            leaf += 2


def down_sweep(siblings, upper_trans, upper_coup, far, local_transfer, basis_t, nearby):
    return pl.pallas_call(
        down_kernel,
        out_shape=jax.ShapeDtypeStruct((16, 8192), F32),
        in_specs=[VMEM] * 10 + [ANY, ANY] + [VMEM] * len(nearby),
        out_specs=VMEM,
        scratch_shapes=[
            pltpu.VMEM(local_transfer.shape, BF16),
            pltpu.VMEM(basis_t.shape, BF16),
            pltpu.SemaphoreType.DMA((2,)),
        ],
        compiler_params=pltpu.CompilerParams(vmem_limit_bytes=20 * 2**20),
        cost_estimate=pl.CostEstimate(flops=10**8, bytes_accessed=5 * 2**20, transcendentals=0),
        name="down_sweep",
    )(*siblings, upper_trans, upper_coup, far, local_transfer, basis_t, *nearby)


def local(rhs, leaf_basis, near_tiles, near_pairs, local_transfer, local_coupling, upper_transfer, upper_coupling):
    devices = lax.axis_size("leaf")
    position = lax.axis_index("leaf").astype(jnp.int32)
    up = [(i, i + 1) for i in range(devices - 1)]
    before = lax.ppermute(rhs, "leaf", up)
    after = lax.ppermute(rhs, "leaf", [(j, i) for i, j in up])
    index = near_pairs - (position * 32 - 32)
    basis_t = jnp.transpose(leaf_basis, (0, 2, 1))
    where = position.reshape(1)
    coef, path, upper_trans = up_sweep(
        where, rhs, basis_t, local_transfer, jnp.transpose(upper_transfer, (1, 2, 0))
    )
    nearby = []
    siblings = []
    first = 0
    for level in range(7):
        width = 64 * (7 - level)
        pairs = [(i, i ^ (1 << level)) for i in range(devices)]
        received = lax.ppermute(path, "leaf", pairs)
        if level == 0:
            far, upper_coup = far_fields(where, coef, local_coupling, jnp.transpose(upper_coupling, (1, 2, 0)))
            received, far = lax.optimization_barrier((received, far))
        else:
            count = NEAR_CHUNKS[level - 1]
            part = near_field(first, count, index, before, rhs, after, path, near_tiles)
            first += count
            received, part = lax.optimization_barrier((received, part))
            nearby.append(part)
        siblings.append(received)
        path = path[:, : width - 64] + received[:, : width - 64]
    return down_sweep(siblings, upper_trans, upper_coup, far, local_transfer, basis_t, nearby)


def solution(mesh):
    return jax.shard_map(
        local,
        mesh=mesh,
        in_specs=(
            P(None, "leaf"),
            P("leaf", None, None),
            P("leaf", None, None, None),
            P("leaf", None),
            P("leaf", None, None),
            P("leaf", None, None),
            P(),
            P(),
        ),
        out_specs=P(None, "leaf"),
        check_vma=False,
    )
```

time: 124 us -> 64.4 us (0.52)
  the two profiles are of different devices: /device:TPU:0 before, /device:TPU:24 now
where the time goes in v1:
time: 64.4 us; the launch traced here: 63.9 us
  Pallas kernels  21.5 us (33%)
  waiting for transfers between devices  15.1 us (23%)
  local copies, waits for them, and re-layouts  14.9 us (23%)
  starting transfers between devices  12.1 us (19%)
    unnamed x21, local copies, waits for them, and re-layouts  14.9 us
    pallas_call x6, Pallas kernels, near_field(): pl.pallas_call(functools.partial(near_kernel, first), grid=(steps,), out_...  12.3 us
    ppermute x1, starting transfers between devices, local(): after = lax.ppermute(rhs, 'leaf', [(j, i) for i, j in up])  8.41 us
    ppermute x7, waiting for transfers between devices, local(): received = lax.ppermute(path, 'leaf', pairs)  8.18 us
    ppermute x1, waiting for transfers between devices, local(): before = lax.ppermute(rhs, 'leaf', up)  6.93 us
    pallas_call x1, Pallas kernels, up_sweep(): pl.pallas_call(up_kernel, out_shape=(jax.ShapeDtypeStruct((31, 16, 128),...  4.07 us
    pallas_call x1, Pallas kernels, down_sweep(): pl.pallas_call(down_kernel, out_shape=jax.ShapeDtypeStruct((16, 8192), F3...  3.38 us
    ppermute x1, starting transfers between devices, local(): before = lax.ppermute(rhs, 'leaf', up)  1.92 us
  transfers between devices with their start and end apart: 9, of which 5 were waited for; matrix products, arithmetic and copies ran while one was open for 0% of the time, Pallas kernels for 22%

profile of v1, /device:TPU:24, one launch (start us, length us, event | category | flops | bytes accessed | tf_op | source)
XLA Modules:
  0.0 63.9 jit_solution(14050825755958549979)
XLA Ops:
  0.0 1.2 %copy-done.2 = bf16[32,256,64]{1,2,0:T(8,128)(2,1)S(1)} copy-done((bf16[32,256,64]{1,2,0:T(8,128)(2,1)S(1)}, bf16[32,256,64]{1,2,0:T(8,128)(2,1)}, u32[]{:S(2)}) %copy-start.2) | copy-done | bytes 1048600
  1.2 1.2 %copy-done.4 = bf16[62,64,64]{2,1,0:T(8,128)(2,1)S(1)} copy-done((bf16[62,64,64]{2,1,0:T(8,128)(2,1)S(1)}, bf16[62,64,64]{2,1,0:T(8,128)(2,1)}, u32[]{:S(2)}) %copy-start.4) | copy-done | bytes 507928
  2.4 1.6 %copy-done.6 = bf16[252,64,64]{0,2,1:T(8,128)(2,1)S(1)} copy-done((bf16[252,64,64]{0,2,1:T(8,128)(2,1)S(1)}, bf16[252,64,64]{0,2,1:T(8,128)(2,1)}, u32[]{:S(2)}) %copy-start.6) | copy-done | bytes 2064408
  4.0 4.1 %up_sweep.1 = (f32[31,16,128]{2,1,0:T(8,128)S(1)}, f32[16,448]{1,0:T(8,128)S(1)}, bf16[6,64,64]{2,1,0:T(8,128)(2,1)S(1)}) custom-call(s32[1]{0:T(128)} %bitcast.pos_ref, bf16[16,8192]{1,0:T(8,128)(2,1)} %own.11, bf16[32,64,256]{2,1,0:T(8,128)(2,1)S(1)} %bitcast.4, bf16[62,64,64]{2,1,0:T(8,128)(2,1)S(1)} %copy-done.4, bf16[64,64,252]{2,1,0:T(8,128)(2,1)S(1)} %bitcast.6), custom_call_target="tpu_custom_call" | custom-call | flops 100000000 | bytes 5242880 | tf_op jit(solution)/shard_map/up_sweep/pallas_call | solution.py:124
  8.2 8.4 %collective-permute-start.3 = (bf16[16,8192]{1,0:T(8,128)(2,1)}, bf16[16,8192]{1,0:T(8,128)(2,1)S(1)}, u32[]{:S(2)}, u32[]{:S(2)}) collective-permute-start(bf16[16,8192]{1,0:T(8,128)(2,1)} %own.11), channel_id=1, source_target_pairs={{1,0},{2,1},{3,2},{4,3},{5,4},{6,5},{7,6},{8,7},{9,8},{10,9},{11,1... | collective-permute-start | bytes 786440 | tf_op jit(solution)/shard_map/ppermute | solution.py:292
  16.6 1.9 %collective-permute-start.2 = (bf16[16,8192]{1,0:T(8,128)(2,1)}, bf16[16,8192]{1,0:T(8,128)(2,1)S(1)}, u32[]{:S(2)}, u32[]{:S(2)}) collective-permute-start(bf16[16,8192]{1,0:T(8,128)(2,1)} %own.11), channel_id=1, source_target_pairs={{0,1},{1,2},{2,3},{3,4},{4,5},{5,6},{6,7},{7,8},{8,9},{9,10},{10,1... | collective-permute-start | bytes 786440 | tf_op jit(solution)/shard_map/ppermute | solution.py:291
  18.7 1.2 %copy-done.8 = bf16[62,64,64]{2,1,0:T(8,128)(2,1)S(1)} copy-done((bf16[62,64,64]{2,1,0:T(8,128)(2,1)S(1)}, bf16[62,64,64]{2,1,0:T(8,128)(2,1)}, u32[]{:S(2)}) %copy-start.8) | copy-done | bytes 507928
  19.9 1.8 %far_fields.1 = (f32[31,16,128]{2,1,0:T(8,128)S(1)}, bf16[7,64,64]{2,1,0:T(8,128)(2,1)S(1)}) custom-call(s32[1]{0:T(128)} %bitcast.pos_ref, f32[31,16,128]{2,1,0:T(8,128)S(1)} %get-tuple-element.25.coef, bf16[62,64,64]{2,1,0:T(8,128)(2,1)S(1)} %copy-done.8, bf16[64,64,254]{2,1,0:T(8,128)(2,1)S(1)} %bitcast.7), custom_call_target="tpu_custom_call" | custom-call | flops 100000000 | bytes 5242880 | tf_op jit(solution)/shard_map/far_fields/pallas_call | solution.py:166
  21.8 6.9 %collective-permute-done.2.before = bf16[16,8192]{1,0:T(8,128)(2,1)S(1)} collective-permute-done((bf16[16,8192]{1,0:T(8,128)(2,1)}, bf16[16,8192]{1,0:T(8,128)(2,1)S(1)}, u32[]{:S(2)}, u32[]{:S(2)}) %collective-permute-start.2) | collective-permute-done | bytes 262176 | tf_op jit(solution)/shard_map/ppermute | solution.py:291
  28.8 5.8 %copy-done = bf16[32,4,256,256]{3,2,1,0:T(8,128)(2,1)S(1)} copy-done((bf16[32,4,256,256]{3,2,1,0:T(8,128)(2,1)S(1)}, bf16[32,4,256,256]{3,2,1,0:T(8,128)(2,1)}, u32[]{:S(2)}) %copy-start) | copy-done | bytes 16777240
  34.5 1.9 %near_field.6.refs_12_ = f32[16,1024]{1,0:T(8,128)S(1)} custom-call(s32[32,4]{1,0:T(8,128)S(1)} %broadcast_subtract_fusion.index_ref, bf16[16,8192]{1,0:T(8,128)(2,1)S(1)} %collective-permute-done.2.before, bf16[16,8192]{1,0:T(8,128)(2,1)} %own.11, bf16[16,8192]{1,0:T(8,128)(2,1)S(1)} %collective-permute-done.3.after, f32[16,384]{1,0:T(8,128)S(1)} %slice_add_fusion.1.order, ...), custom_call_target="tpu_custom_call" | custom-call | flops 33554432 | bytes 2097152 | tf_op jit(solution)/shard_map/near_field/pallas_call | solution.py:207
  36.5 3.8 %copy-done.1 = bf16[32,4,256,256]{3,2,1,0:T(8,128)(2,1)S(1)} copy-done((bf16[32,4,256,256]{3,2,1,0:T(8,128)(2,1)S(1)}, bf16[32,4,256,256]{3,2,1,0:T(8,128)(2,1)}, u32[]{:S(2)}) %copy-start.1) | copy-done | bytes 16777240
  40.4 2.1 %near_field.7.refs_13_ = f32[16,1536]{1,0:T(8,128)S(1)} custom-call(s32[32,4]{1,0:T(8,128)S(1)} %broadcast_subtract_fusion.index_ref, bf16[16,8192]{1,0:T(8,128)(2,1)S(1)} %collective-permute-done.2.before, bf16[16,8192]{1,0:T(8,128)(2,1)} %own.11, bf16[16,8192]{1,0:T(8,128)(2,1)S(1)} %collective-permute-done.3.after, f32[16,320]{1,0:T(8,128)S(1)} %slice_add_fusion.order, ...), custom_call_target="tpu_custom_call" | custom-call | flops 50331648 | bytes 3145728 | tf_op jit(solution)/shard_map/near_field/pallas_call | solution.py:207
  42.6 2.2 %near_field.8.refs_14_ = f32[16,1536]{1,0:T(8,128)S(1)} custom-call(s32[32,4]{1,0:T(8,128)S(1)} %broadcast_subtract_fusion.index_ref, bf16[16,8192]{1,0:T(8,128)(2,1)S(1)} %collective-permute-done.2.before, bf16[16,8192]{1,0:T(8,128)(2,1)} %own.11, bf16[16,8192]{1,0:T(8,128)(2,1)S(1)} %collective-permute-done.3.after, f32[16,256]{1,0:T(8,128)S(1)} %slice_add_fusion.3.order, ...), custom_call_target="tpu_custom_call" | custom-call | flops 50331648 | bytes 3145728 | tf_op jit(solution)/shard_map/near_field/pallas_call | solution.py:207
  44.8 1.6 %collective-permute-done.5.refs_3_ = f32[16,256]{1,0:T(8,128)S(1)} collective-permute-done((f32[16,256]{1,0:T(8,128)S(1)}, f32[16,256]{1,0:T(8,128)S(1)}, u32[]{:S(2)}, u32[]{:S(2)}) %collective-permute-start.5) | collective-permute-done | bytes 16416 | tf_op jit(solution)/shard_map/ppermute | solution.py:305
  46.4 2.2 %near_field.9.refs_15_ = f32[16,1536]{1,0:T(8,128)S(1)} custom-call(s32[32,4]{1,0:T(8,128)S(1)} %broadcast_subtract_fusion.index_ref, bf16[16,8192]{1,0:T(8,128)(2,1)S(1)} %collective-permute-done.2.before, bf16[16,8192]{1,0:T(8,128)(2,1)} %own.11, bf16[16,8192]{1,0:T(8,128)(2,1)S(1)} %collective-permute-done.3.after, f32[16,192]{1,0:T(8,128)S(1)} %slice_add_fusion.2.order, ...), custom_call_target="tpu_custom_call" | custom-call | flops 50331648 | bytes 3145728 | tf_op jit(solution)/shard_map/near_field/pallas_call | solution.py:207
  48.6 3.1 %collective-permute-done.6.refs_4_ = f32[16,192]{1,0:T(8,128)S(1)} collective-permute-done((f32[16,192]{1,0:T(8,128)S(1)}, f32[16,192]{1,0:T(8,128)S(1)}, u32[]{:S(2)}, u32[]{:S(2)}) %collective-permute-start.6) | collective-permute-done | bytes 12320 | tf_op jit(solution)/shard_map/ppermute | solution.py:305
  51.6 0.4 collective-permute-start.7
  52.1 2.1 %near_field.10.refs_16_ = f32[16,1536]{1,0:T(8,128)S(1)} custom-call(s32[32,4]{1,0:T(8,128)S(1)} %broadcast_subtract_fusion.index_ref, bf16[16,8192]{1,0:T(8,128)(2,1)S(1)} %collective-permute-done.2.before, bf16[16,8192]{1,0:T(8,128)(2,1)} %own.11, bf16[16,8192]{1,0:T(8,128)(2,1)S(1)} %collective-permute-done.3.after, f32[16,128]{1,0:T(8,128)S(1)} %slice_add_fusion.5.order, ...), custom_call_target="tpu_custom_call" | custom-call | flops 50331648 | bytes 3145728 | tf_op jit(solution)/shard_map/near_field/pallas_call | solution.py:207
  54.2 1.1 %collective-permute-done.7.refs_5_ = f32[16,128]{1,0:T(8,128)S(1)} collective-permute-done((f32[16,128]{1,0:T(8,128)S(1)}, f32[16,128]{1,0:T(8,128)S(1)}, u32[]{:S(2)}, u32[]{:S(2)}) %collective-permute-start.7) | collective-permute-done | bytes 8224 | tf_op jit(solution)/shard_map/ppermute | solution.py:305
  55.3 1.0 %collective-permute-start.8 = (f32[16,64]{1,0:T(8,128)S(1)}, f32[16,64]{1,0:T(8,128)S(1)}, u32[]{:S(2)}, u32[]{:S(2)}) collective-permute-start(f32[16,64]{1,0:T(8,128)S(1)} %slice_add_fusion.4.order), channel_id=1, source_target_pairs={{0,64},{1,65},{2,66},{3,67},{4,68},{5,69},{6,70},{7,71},{8,72},{9,... | collective-permute-start | bytes 12296 | tf_op jit(solution)/shard_map/ppermute | solution.py:305
  56.3 1.7 %near_field.11.refs_17_ = f32[16,1024]{1,0:T(8,128)S(1)} custom-call(s32[32,4]{1,0:T(8,128)S(1)} %broadcast_subtract_fusion.index_ref, bf16[16,8192]{1,0:T(8,128)(2,1)S(1)} %collective-permute-done.2.before, bf16[16,8192]{1,0:T(8,128)(2,1)} %own.11, bf16[16,8192]{1,0:T(8,128)(2,1)S(1)} %collective-permute-done.3.after, f32[16,64]{1,0:T(8,128)S(1)} %slice_add_fusion.4.order, ...), custom_call_target="tpu_custom_call" | custom-call | flops 33554432 | bytes 2097152 | tf_op jit(solution)/shard_map/near_field/pallas_call | solution.py:207
  58.0 2.5 %collective-permute-done.8.refs_6_ = f32[16,64]{1,0:T(8,128)S(1)} collective-permute-done((f32[16,64]{1,0:T(8,128)S(1)}, f32[16,64]{1,0:T(8,128)S(1)}, u32[]{:S(2)}, u32[]{:S(2)}) %collective-permute-start.8) | collective-permute-done | bytes 4128 | tf_op jit(solution)/shard_map/ppermute | solution.py:305
  60.5 3.4 %down_sweep.1 = f32[16,8192]{1,0:T(8,128)} custom-call(f32[16,448]{1,0:T(8,128)S(1)} %collective-permute-done.refs_0_, f32[16,384]{1,0:T(8,128)S(1)} %collective-permute-done.1.refs_1_, f32[16,320]{1,0:T(8,128)S(1)} %collective-permute-done.4.refs_2_, f32[16,256]{1,0:T(8,128)S(1)} %collective-permute-done.5.refs_3_, ...), custom_call_target="tpu_custom_call" | custom-call | flops 100000000 | bytes 5242880 | tf_op jit(solution)/shard_map/down_sweep/pallas_call | solution.py:271
  (31 shorter events, 0.5 us)
Async XLA Ops:
  0.0 1.2 %copy-start.2 = (bf16[32,256,64]{1,2,0:T(8,128)(2,1)S(1)}, bf16[32,256,64]{1,2,0:T(8,128)(2,1)}, u32[]{:S(2)}) copy-start(bf16[32,256,64]{1,2,0:T(8,128)(2,1)} %param.9) | copy-start | bytes 3145732
  1.2 1.2 %copy-start.4 = (bf16[62,64,64]{2,1,0:T(8,128)(2,1)S(1)}, bf16[62,64,64]{2,1,0:T(8,128)(2,1)}, u32[]{:S(2)}) copy-start(bf16[62,64,64]{2,1,0:T(8,128)(2,1)} %refs_10_.1) | copy-start | bytes 1523716
  2.4 1.6 %copy-start.6 = (bf16[252,64,64]{0,2,1:T(8,128)(2,1)S(1)}, bf16[252,64,64]{0,2,1:T(8,128)(2,1)}, u32[]{:S(2)}) copy-start(bf16[252,64,64]{0,2,1:T(8,128)(2,1)} %param.14) | copy-start | bytes 6193156
  4.0 14.5 %copy-start.9 = (s32[32,4]{0,1:T(4,128)S(1)}, s32[32,4]{0,1:T(4,128)}, u32[]{:S(2)}) copy-start(s32[32,4]{0,1:T(4,128)} %param.11) | copy-start | bytes 1540
  4.0 14.6 %copy-start.7 = (bf16[254,64,64]{0,2,1:T(8,128)(2,1)S(1)}, bf16[254,64,64]{0,2,1:T(8,128)(2,1)}, u32[]{:S(2)}) copy-start(bf16[254,64,64]{0,2,1:T(8,128)(2,1)} %param.15) | copy-start | bytes 6242308
  8.1 13.6 %collective-permute-start = (f32[16,448]{1,0:T(8,128)S(1)}, f32[16,448]{1,0:T(8,128)S(1)}, u32[]{:S(2)}, u32[]{:S(2)}) collective-permute-start(f32[16,448]{1,0:T(8,128)S(1)} %get-tuple-element.24), channel_id=1, source_target_pairs={{0,1},{1,0},{2,3},{3,2},{4,5},{5,4},{6,7},{7,6},{8,9},{9,8},{10,11... | collective-permute-start | bytes 86024 | tf_op jit(solution)/shard_map/ppermute | solution.py:305
  8.2 13.6 %collective-permute-start.3 = (bf16[16,8192]{1,0:T(8,128)(2,1)}, bf16[16,8192]{1,0:T(8,128)(2,1)S(1)}, u32[]{:S(2)}, u32[]{:S(2)}) collective-permute-start(bf16[16,8192]{1,0:T(8,128)(2,1)} %own.11), channel_id=1, source_target_pairs={{1,0},{2,1},{3,2},{4,3},{5,4},{6,5},{7,6},{8,7},{9,8},{10,9},{11,1... | collective-permute-start | bytes 786440 | tf_op jit(solution)/shard_map/ppermute | solution.py:292
  16.6 12.1 %collective-permute-start.2 = (bf16[16,8192]{1,0:T(8,128)(2,1)}, bf16[16,8192]{1,0:T(8,128)(2,1)S(1)}, u32[]{:S(2)}, u32[]{:S(2)}) collective-permute-start(bf16[16,8192]{1,0:T(8,128)(2,1)} %own.11), channel_id=1, source_target_pairs={{0,1},{1,2},{2,3},{3,4},{4,5},{5,6},{6,7},{7,8},{8,9},{9,10},{10,1... | collective-permute-start | bytes 786440 | tf_op jit(solution)/shard_map/ppermute | solution.py:291
  18.7 1.2 %copy-start.8 = (bf16[62,64,64]{2,1,0:T(8,128)(2,1)S(1)}, bf16[62,64,64]{2,1,0:T(8,128)(2,1)}, u32[]{:S(2)}) copy-start(bf16[62,64,64]{2,1,0:T(8,128)(2,1)} %coup_hbm.1) | copy-start | bytes 1523716
  21.7 14.7 %collective-permute-start.1 = (f32[16,384]{1,0:T(8,128)S(1)}, f32[16,384]{1,0:T(8,128)S(1)}, u32[]{:S(2)}, u32[]{:S(2)}) collective-permute-start(f32[16,384]{1,0:T(8,128)S(1)} %slice_add_fusion.1.order), channel_id=1, source_target_pairs={{0,2},{1,3},{2,0},{3,1},{4,6},{5,7},{6,4},{7,5},{8,10},{9,11},{10,... | collective-permute-start | bytes 73736 | tf_op jit(solution)/shard_map/ppermute | solution.py:305
  28.8 5.8 %copy-start = (bf16[32,4,256,256]{3,2,1,0:T(8,128)(2,1)S(1)}, bf16[32,4,256,256]{3,2,1,0:T(8,128)(2,1)}, u32[]{:S(2)}) copy-start(bf16[32,4,256,256]{3,2,1,0:T(8,128)(2,1)} %tiles.11) | copy-start | bytes 50331652
  34.5 5.8 %copy-start.1 = (bf16[32,4,256,256]{3,2,1,0:T(8,128)(2,1)S(1)}, bf16[32,4,256,256]{3,2,1,0:T(8,128)(2,1)}, u32[]{:S(2)}) copy-start(bf16[32,4,256,256]{3,2,1,0:T(8,128)(2,1)} %tiles.11) | copy-start | bytes 50331652
  36.5 6.1 %collective-permute-start.4 = (f32[16,320]{1,0:T(8,128)S(1)}, f32[16,320]{1,0:T(8,128)S(1)}, u32[]{:S(2)}, u32[]{:S(2)}) collective-permute-start(f32[16,320]{1,0:T(8,128)S(1)} %slice_add_fusion.order), channel_id=1, source_target_pairs={{0,4},{1,5},{2,6},{3,7},{4,0},{5,1},{6,2},{7,3},{8,12},{9,13},{10,... | collective-permute-start | bytes 61448 | tf_op jit(solution)/shard_map/ppermute | solution.py:305
  42.6 3.8 %collective-permute-start.5 = (f32[16,256]{1,0:T(8,128)S(1)}, f32[16,256]{1,0:T(8,128)S(1)}, u32[]{:S(2)}, u32[]{:S(2)}) collective-permute-start(f32[16,256]{1,0:T(8,128)S(1)} %slice_add_fusion.3.order), channel_id=1, source_target_pairs={{0,8},{1,9},{2,10},{3,11},{4,12},{5,13},{6,14},{7,15},{8,0},{9,1},... | collective-permute-start | bytes 49160 | tf_op jit(solution)/shard_map/ppermute | solution.py:305
  46.4 5.2 %collective-permute-start.6 = (f32[16,192]{1,0:T(8,128)S(1)}, f32[16,192]{1,0:T(8,128)S(1)}, u32[]{:S(2)}, u32[]{:S(2)}) collective-permute-start(f32[16,192]{1,0:T(8,128)S(1)} %slice_add_fusion.2.order), channel_id=1, source_target_pairs={{0,16},{1,17},{2,18},{3,19},{4,20},{5,21},{6,22},{7,23},{8,24},{9,... | collective-permute-start | bytes 36872 | tf_op jit(solution)/shard_map/ppermute | solution.py:305
  51.6 3.7 %collective-permute-start.7 = (f32[16,128]{1,0:T(8,128)S(1)}, f32[16,128]{1,0:T(8,128)S(1)}, u32[]{:S(2)}, u32[]{:S(2)}) collective-permute-start(f32[16,128]{1,0:T(8,128)S(1)} %slice_add_fusion.5.order), channel_id=1, source_target_pairs={{0,32},{1,33},{2,34},{3,35},{4,36},{5,37},{6,38},{7,39},{8,40},{9,... | collective-permute-start | bytes 24584 | tf_op jit(solution)/shard_map/ppermute | solution.py:305
  55.3 5.2 %copy-start.3 = (bf16[32,256,64]{1,2,0:T(8,128)(2,1)S(1)}, bf16[32,256,64]{1,2,0:T(8,128)(2,1)}, u32[]{:S(2)}) copy-start(bf16[32,256,64]{1,2,0:T(8,128)(2,1)} %param.9) | copy-start | bytes 3145732
  55.3 5.2 %copy-start.5 = (bf16[62,64,64]{2,1,0:T(8,128)(2,1)S(1)}, bf16[62,64,64]{2,1,0:T(8,128)(2,1)}, u32[]{:S(2)}) copy-start(bf16[62,64,64]{2,1,0:T(8,128)(2,1)} %refs_10_.1) | copy-start | bytes 1523716
  55.3 5.2 %collective-permute-start.8 = (f32[16,64]{1,0:T(8,128)S(1)}, f32[16,64]{1,0:T(8,128)S(1)}, u32[]{:S(2)}, u32[]{:S(2)}) collective-permute-start(f32[16,64]{1,0:T(8,128)S(1)} %slice_add_fusion.4.order), channel_id=1, source_target_pairs={{0,64},{1,65},{2,66},{3,67},{4,68},{5,69},{6,70},{7,71},{8,72},{9,... | collective-permute-start | bytes 12296 | tf_op jit(solution)/shard_map/ppermute | solution.py:305

commit v2 on v1

v2 whole, which is shorter than its diff:
```python
import functools

import jax
import jax.numpy as jnp
from jax import lax
from jax.experimental import pallas as pl
from jax.experimental.pallas import tpu as pltpu
from jax.sharding import PartitionSpec as P

F32 = jnp.float32
BF16 = jnp.bfloat16
ANY = pl.BlockSpec(memory_space=pl.ANY)
VMEM = pl.BlockSpec(memory_space=pltpu.VMEM)
HBM = pl.BlockSpec(memory_space=pltpu.HBM)
SMEM = pl.BlockSpec(memory_space=pltpu.SMEM)
NEAR_CHUNKS = (6, 6, 6, 6, 6, 2)
FETCH = (8, 4, 6, 7, 7)
MASKS = (1, 2, 6, 8, 24, 32, 96)


def split_rows(value):
    high = value.astype(BF16)
    low = (value - high.astype(F32)).astype(BF16)
    return jnp.concatenate([high, low], axis=0)


def join_rows(value):
    half = value.shape[0] // 2
    return value[:half] + value[half:]


def times(value, matrix):
    return join_rows(jnp.dot(split_rows(value), matrix, preferred_element_type=F32))


def times_transposed(value, matrix):
    dims = (((1,), (1,)), ((), ()))
    return join_rows(
        lax.dot_general(split_rows(value), matrix, dims, preferred_element_type=F32)
    )


def left_half(shape):
    return lax.broadcasted_iota(jnp.int32, shape, 1) < 64


def apart(pair):
    left = left_half(pair.shape)
    return jnp.concatenate([jnp.where(left, pair, 0.0), jnp.where(left, 0.0, pair)], axis=0)


def pick_nodes(position, matrices, picked):
    nodes = matrices.shape[2]
    count = 2 * 128
    row = lax.broadcasted_iota(jnp.int32, (8, nodes), 0)
    lane = lax.broadcasted_iota(jnp.int32, (8, nodes), 1)
    start = count - lax.shift_right_logical(jnp.full_like(row, count), row)
    wanted = start + lax.shift_right_logical(jnp.full_like(row, position), row)
    chosen = jnp.where(lane == wanted, 1.0, 0.0).astype(BF16)
    dims = (((1,), (1,)), ((), ()))
    for group in range(16):
        block = matrices[4 * group : 4 * group + 4].reshape(256, nodes)
        rows = lax.dot_general(chosen, block, dims, preferred_element_type=F32)
        shifted = pltpu.roll(rows, 64, 1)
        for half in range(2):
            lanes = slice(128 * half, 128 * half + 128)
            picked[pl.ds(4 * group + 2 * half, 8, stride=64), :] = rows[:, lanes]
            other = slice(128 * (1 - half), 128 * (1 - half) + 128)
            del other
            place = (128 * (half + 1)) % 256
            picked[pl.ds(4 * group + 2 * half + 1, 8, stride=64), :] = shifted[:, place : place + 128]


def in_hbm(*arrays):
    return [pltpu.with_memory_space_constraint(array, pltpu.HBM) for array in arrays]


def vmem(shape, dtype):
    return pltpu.VMEM(shape, dtype)


def vmem_like(array):
    return vmem(array.shape, array.dtype)


def tiles_like(tiles, count):
    return vmem((count,) + tiles.shape[1:], tiles.dtype)


def start_all(pairs, sems):
    copies = [pltpu.make_async_copy(source, target, sems.at[i]) for i, (source, target) in enumerate(pairs)]
    for copy in copies:
        copy.start()
    return copies


def params():
    return pltpu.CompilerParams(vmem_limit_bytes=24 * 2**20)


def cost(flops, size):
    return pl.CostEstimate(flops=flops, bytes_accessed=size, transcendentals=0)


def up_kernel(pos_ref, rhs_hbm, basis_hbm, trans_hbm, upper_hbm, upper_coup_hbm, coup_hbm, tiles_hbm,
              coef_ref, path_ref, upper_ref, rhs, basis, trans, upper_coup, coup, tiles,
              upper, picked, sems):
    copies = start_all(
        [
            (rhs_hbm, rhs),
            (basis_hbm, basis),
            (trans_hbm, trans),
            (upper_hbm, upper),
            (upper_coup_hbm, upper_coup),
            (tiles_hbm.at[: FETCH[0]], tiles),
            (coup_hbm, coup),
        ],
        sems,
    )
    copies[0].wait()
    copies[1].wait()
    dims = (((1,), (1,)), ((), ()))
    current = []
    for pair in range(16):
        first = rhs[:, 512 * pair : 512 * pair + 256]
        second = rhs[:, 512 * pair + 256 : 512 * pair + 512]
        sources = jnp.concatenate([first, second], axis=0)
        both = lax.dot_general(
            sources, basis[2 * pair : 2 * pair + 2].reshape(128, 256), dims, preferred_element_type=F32
        )
        value = jnp.where(left_half((16, 128)), both[:16], both[16:])
        coef_ref[pair] = value
        current.append(value)
    copies[2].wait()
    base = 0
    while True:
        parents = [
            times(value, trans[2 * (base + i) : 2 * (base + i) + 2].reshape(128, 64))
            for i, value in enumerate(current)
        ]
        base += len(current)
        if len(parents) == 1:
            break
        current = [
            jnp.concatenate([parents[2 * i], parents[2 * i + 1]], axis=1) for i in range(len(parents) // 2)
        ]
        for i, value in enumerate(current):
            coef_ref[base + i] = value
    copies[3].wait()
    pick_nodes(pos_ref[0], upper, picked)
    value = parents[0]
    path_ref[:, 384:448] = value
    for level in range(6):
        matrix = picked[64 * level : 64 * level + 64, 0:64].astype(BF16)
        upper_ref[level] = matrix
        value = times(value, matrix)
        start = 64 * (5 - level)
        path_ref[:, start : start + 64] = value
    for copy in copies[4:]:
        copy.wait()


def up_sweep(position, rhs, basis_t, local_transfer, upper_transfer_t, upper_coupling_t, local_coupling, tiles):
    return pl.pallas_call(
        up_kernel,
        out_shape=(
            vmem((31, 16, 128), F32),
            vmem((16, 448), F32),
            vmem((6, 64, 64), BF16),
            vmem_like(rhs),
            vmem_like(basis_t),
            vmem_like(local_transfer),
            vmem_like(upper_coupling_t),
            vmem_like(local_coupling),
            tiles_like(tiles, FETCH[0]),
        ),
        in_specs=[SMEM] + [HBM] * 7,
        out_specs=(VMEM,) * 9,
        scratch_shapes=[
            pltpu.VMEM(upper_transfer_t.shape, BF16),
            pltpu.VMEM((512, 128), F32),
            pltpu.SemaphoreType.DMA((7,)),
        ],
        compiler_params=params(),
        cost_estimate=cost(4 * 10**9, 12 * 2**20),
        name="up_sweep",
    )(
        position,
        *in_hbm(rhs, basis_t, local_transfer, upper_transfer_t, upper_coupling_t, local_coupling, tiles),
    )


def pick_kernel(pos_ref, order, upper, tiles_hbm, *refs):
    del order
    upper_ref, tiles, picked, sems = refs[-4:]
    copies = start_all([(tiles_hbm.at[FETCH[0] : FETCH[0] + FETCH[1]], tiles)], sems)
    pick_nodes(pos_ref[0], upper, picked)
    for level in range(7):
        upper_ref[level] = picked[64 * level : 64 * level + 64, 0:64].astype(BF16)
    copies[0].wait()


def pick_couplings(position, order, upper_coupling_t, tiles, keep):
    return pl.pallas_call(
        pick_kernel,
        out_shape=(vmem((7, 64, 64), BF16), tiles_like(tiles, FETCH[1])),
        in_specs=[SMEM, ANY, VMEM, HBM] + [VMEM] * len(keep),
        out_specs=(VMEM, VMEM),
        scratch_shapes=[pltpu.VMEM((512, 128), F32), pltpu.SemaphoreType.DMA((1,))],
        compiler_params=params(),
        cost_estimate=cost(10**9, 2**20),
        name="pick_couplings",
    )(position, order, upper_coupling_t, *in_hbm(tiles), *keep)


def near_kernel(first, count, fetched, fetch, with_far, *refs):
    pos_ref, pairs_ref, order, inner, own, outer = refs[:6]
    del order
    at = 6
    held = refs[at : at + fetched]
    at += fetched
    coef, coup = refs[at : at + 2]
    at += 4
    if fetch:
        tiles_hbm = refs[at]
        at += 1
    out_ref = refs[at]
    at += 1
    if with_far:
        far_ref = refs[at]
        at += 1
    if fetch:
        start = sum(FETCH[:fetch])
        copies = start_all([(tiles_hbm.at[start : start + FETCH[fetch]], refs[at])], refs[at + 1])
    dims = (((1,), (1,)), ((), ()))
    position = pos_ref[0]
    for i in range(count):
        total = None
        place = first + i
        box = 0
        while place >= FETCH[box]:
            place -= FETCH[box]
            box += 1
        for k in range(4):
            leaf = pairs_ref[k, first + i]
            holder = lax.shift_right_logical(leaf, 5)
            column = pl.ds(pl.multiple_of((leaf & 31) * 256, 256), 256)
            source = jnp.where(
                holder == position, own[:, column],
                jnp.where(holder == position ^ 1, inner[:, column], outer[:, column]),
            )
            part = lax.dot_general(source, held[box][place, k], dims, preferred_element_type=F32)
            total = part if total is None else total + part
        out_ref[:, 256 * i : 256 * i + 256] = total
    if with_far:
        for pair in range(31):
            swapped = pltpu.roll(coef[pair], 64, 1)
            both = times(apart(swapped), coup[2 * pair : 2 * pair + 2].reshape(128, 64))
            far_ref[pair] = jnp.concatenate([both[:16], both[16:]], axis=1)
    if fetch:
        copies[0].wait()


def near_field(first, count, position, near_pairs_t, order, inner, own, outer, held, keep, fetch, tiles, with_far):
    inputs = [position, near_pairs_t, order, inner, own, outer, *held, *keep]
    in_specs = [SMEM, SMEM, ANY] + [VMEM] * (len(inputs) - 3)
    outputs = [vmem((16, 256 * count), F32)]
    scratch = []
    if with_far:
        outputs.append(vmem((31, 16, 128), F32))
    if fetch:
        inputs += in_hbm(tiles)
        in_specs.append(HBM)
        outputs.append(tiles_like(tiles, FETCH[fetch]))
        scratch = [pltpu.SemaphoreType.DMA((1,))]
    return pl.pallas_call(
        functools.partial(near_kernel, first, count, len(held), fetch, with_far),
        out_shape=tuple(outputs),
        in_specs=in_specs,
        out_specs=(VMEM,) * len(outputs),
        scratch_shapes=scratch,
        compiler_params=params(),
        cost_estimate=cost(10**9, 2**20),
        name="near_field",
    )(*inputs)


def down_kernel(*refs):
    siblings = refs[:7]
    upper_trans, upper_coup, far, trans, basis = refs[7:12]
    nearby = refs[12 : 12 + len(NEAR_CHUNKS)]
    out_ref = refs[12 + len(NEAR_CHUNKS)]
    field = None
    for level in range(6, -1, -1):
        width = 64 * (7 - level)
        term = times(siblings[level][:, width - 64 : width], upper_coup[level])
        field = term if field is None else term + times_transposed(field, upper_trans[level])
    fields = [field]
    base = 31
    while len(fields) < 32:
        base -= len(fields)
        pairs = [
            far[base + i] + times_transposed(value, trans[2 * (base + i) : 2 * (base + i) + 2].reshape(128, 64))
            for i, value in enumerate(fields)
        ]
        if len(pairs) == 16:
            break
        fields = []
        for pair in pairs:
            fields += [pair[:, 0:64], pair[:, 64:128]]
    leaf = 0
    for nearby_ref, count in zip(nearby, NEAR_CHUNKS):
        for i in range(0, count, 2):
            both = times(apart(pairs[leaf // 2]), basis[leaf : leaf + 2].reshape(128, 256))
            for j in range(2):
                out_ref[:, 256 * (leaf + j) : 256 * (leaf + j) + 256] = (
                    both[16 * j : 16 * j + 16] + nearby_ref[:, 256 * (i + j) : 256 * (i + j) + 256]
                )
            leaf += 2


def down_sweep(siblings, upper_trans, upper_coup, far, local_transfer, basis_t, nearby):
    return pl.pallas_call(
        down_kernel,
        out_shape=jax.ShapeDtypeStruct((16, 8192), F32),
        in_specs=[VMEM] * (12 + len(nearby)),
        out_specs=VMEM,
        compiler_params=params(),
        cost_estimate=cost(3 * 10**9, 2**20),
        name="down_sweep",
    )(*siblings, upper_trans, upper_coup, far, local_transfer, basis_t, *nearby)


def local(rhs, leaf_basis, near_tiles, near_pairs, local_transfer, local_coupling, upper_transfer, upper_coupling):
    devices = lax.axis_size("leaf")
    position = lax.axis_index("leaf").astype(jnp.int32)
    last = devices - 1
    outward = [(i, min(max(i + 2 * (i & 1) - 1, 0), last)) for i in range(devices)]
    outer = lax.ppermute(rhs, "leaf", outward)
    inner = lax.ppermute(rhs, "leaf", [(i, i ^ 1) for i in range(devices)])
    near_pairs_t = jnp.transpose(near_pairs, (1, 0))
    basis_t = jnp.transpose(leaf_basis, (0, 2, 1))
    where = position.reshape(1)
    coef, path, upper_trans, own, basis, trans, upper_coup, coup, tiles = up_sweep(
        where,
        rhs,
        basis_t,
        local_transfer,
        jnp.transpose(upper_transfer, (1, 2, 0)),
        jnp.transpose(upper_coupling, (1, 2, 0)),
        local_coupling,
        near_tiles,
    )
    held = [tiles]
    keep = [coef, coup, trans, basis]
    nearby = []
    siblings = []
    first = 0
    for level in range(7):
        width = 64 * (7 - level)
        pairs = [(i, i ^ MASKS[level]) for i in range(devices)]
        received = lax.ppermute(path, "leaf", pairs)
        if level == 0:
            upper_coup, tiles = pick_couplings(where, path, upper_coup, near_tiles, held + keep)
            held.append(tiles)
            received, upper_coup = lax.optimization_barrier((received, upper_coup))
        else:
            count = NEAR_CHUNKS[level - 1]
            fetch = level + 1 if level + 1 < len(FETCH) else 0
            last_chunk = level == 6
            results = near_field(
                first, count, where, near_pairs_t, path, inner, own, outer, held, keep, fetch, near_tiles, last_chunk
            )
            part = results[0]
            if fetch:
                held.append(results[-1])
            if last_chunk:
                far = results[1]
            first += count
            received, part = lax.optimization_barrier((received, part))
            nearby.append(part)
        siblings.append(received)
        path = path[:, : width - 64] + received[:, : width - 64]
    return down_sweep(siblings, upper_trans, upper_coup, far, trans, basis, nearby)


def solution(mesh):
    return jax.shard_map(
        local,
        mesh=mesh,
        in_specs=(
            P(None, "leaf"),
            P("leaf", None, None),
            P("leaf", None, None, None),
            P("leaf", None),
            P("leaf", None, None),
            P("leaf", None, None),
            P(),
            P(),
        ),
        out_specs=P(None, "leaf"),
        check_vma=False,
    )
```

time: 64.4 us -> 44.2 us (0.69)
  local copies, waits for them, and re-layouts: 14.9 us -> 0.01 us
  waiting for transfers between devices: 15.1 us -> 11 us
  starting transfers between devices: 12.1 us -> 9.5 us
  Pallas kernels: 21.5 us -> 23.3 us
    unnamed x21 -> x2, local copies, waits for them, and re-layouts: 14.9 us -> 0.01 us
    ppermute x2, waiting for transfers between devices: 6.93 us -> 0.01 us  [the longest x1 0.01 us: local(): outer = lax.ppermute(rhs, 'leaf', outward)]
    ppermute x7, waiting for transfers between devices: 8.18 us -> 10.9 us  [local(): received = lax.ppermute(path, 'leaf', pairs)]
    ppermute x2, starting transfers between devices: 10.3 us -> 7.83 us  [the longest x1 7.75 us: local(): outer = lax.ppermute(rhs, 'leaf', outward)]
    pallas_call x8, Pallas kernels: 18.1 us -> 20.6 us  [the longest x6 14 us: near_field(): pl.pallas_call(functools.partial(near_kernel, first, count, len(held), fe...]
  transfers between devices with their start and end apart: 9 -> 9, of which waited for: 5 -> 6; matrix products, arithmetic and copies ran while one was open for 0% -> 0% of each run, Pallas kernels for 22% -> 47%
where the time goes in v2:
time: 44.2 us; the launch traced here: 43.9 us
  Pallas kernels  23.3 us (53%)
  waiting for transfers between devices  11 us (25%)
  starting transfers between devices  9.5 us (21%)
    pallas_call x6, Pallas kernels, near_field(): pl.pallas_call(functools.partial(near_kernel, first, count, len(held), fe...  14 us
    ppermute x7, waiting for transfers between devices, local(): received = lax.ppermute(path, 'leaf', pairs)  10.9 us
    ppermute x1, starting transfers between devices, local(): outer = lax.ppermute(rhs, 'leaf', outward)  7.75 us
    pallas_call x1, Pallas kernels, up_sweep(): pl.pallas_call(up_kernel, out_shape=(vmem((31, 16, 128), F32), vmem((16,...  4.42 us
    pallas_call x1, Pallas kernels, down_sweep(): pl.pallas_call(down_kernel, out_shape=jax.ShapeDtypeStruct((16, 8192), F3...  2.75 us
    pallas_call x1, Pallas kernels, pick_couplings(): pl.pallas_call(pick_kernel, out_shape=(vmem((7, 64, 64), BF16), tiles_lik...  2.13 us
    ppermute x7, starting transfers between devices, local(): received = lax.ppermute(path, 'leaf', pairs)  1.66 us
  transfers between devices with their start and end apart: 9, of which 6 were waited for; matrix products, arithmetic and copies ran while one was open for 0% of the time, Pallas kernels for 47%

profile of v2, /device:TPU:24, one launch (start us, length us, event | category | flops | bytes accessed | tf_op | source)
XLA Modules:
  0.0 43.9 jit_solution(4903423865176739484)
XLA Ops:
  0.0 7.7 %collective-permute-start.3 = (bf16[16,8192]{1,0:T(8,128)(2,1)}, bf16[16,8192]{1,0:T(8,128)(2,1)S(1)}, u32[]{:S(2)}, u32[]{:S(2)}) collective-permute-start(bf16[16,8192]{1,0:T(8,128)(2,1)} %rhs_hbm.1), channel_id=1, source_target_pairs={{0,0},{1,2},{2,1},{3,4},{4,3},{5,6},{6,5},{7,8},{8,7},{9,10},{10,9... | collective-permute-start | bytes 786440 | tf_op jit(solution)/shard_map/ppermute | solution.py:339
  7.8 0.1 collective-permute-start.2
  7.9 4.4 %up_sweep.1 = (f32[31,16,128]{2,1,0:T(8,128)S(1)}, f32[16,448]{1,0:T(8,128)S(1)}, bf16[6,64,64]{2,1,0:T(8,128)(2,1)S(1)}, bf16[16,8192]{1,0:T(8,128)(2,1)S(1)}, ...) custom-call(s32[1]{0:T(128)} %bitcast.pos_ref.refs_0_, ...), custom_call_target="tpu_custom_call" | custom-call | flops 4000000000 | bytes 12582912 | tf_op jit(solution)/shard_map/up_sweep/pallas_call | solution.py:164
  12.3 0.6 %collective-permute-start = (f32[16,448]{1,0:T(8,128)S(1)}, f32[16,448]{1,0:T(8,128)S(1)}, u32[]{:S(2)}, u32[]{:S(2)}) collective-permute-start(f32[16,448]{1,0:T(8,128)S(1)} %get-tuple-element.38.order), channel_id=1, source_target_pairs={{0,1},{1,0},{2,3},{3,2},{4,5},{5,4},{6,7},{7,6},{8,9},{9,8},{10,11... | collective-permute-start | bytes 86024 | tf_op jit(solution)/shard_map/ppermute | solution.py:362
  12.8 2.1 %pick_couplings.1 = (bf16[7,64,64]{2,1,0:T(8,128)(2,1)S(1)}, bf16[4,4,256,256]{3,2,1,0:T(8,128)(2,1)S(1)}) custom-call(s32[1]{0:T(128)} %bitcast.pos_ref.refs_0_, f32[16,448]{1,0:T(8,128)S(1)} %get-tuple-element.38.order, bf16[64,64,254]{2,1,0:T(8,128)(2,1)S(1)} %get-tuple-element.39.upper, bf16[32,4,256,256]{3,2,1,0:T(8,128)(2,1)} %refs_14_.1, ...), custom_call_target="tpu_custom_call" | custom-call | flops 1000000000 | bytes 1048576 | tf_op jit(solution)/shard_map/pick_couplings/pallas_call | solution.py:204
  15.0 0.1 collective-permute-start.1
  15.1 0.0 collective-permute-done.3.refs_5_
  15.1 3.2 %near_field.6 = (f32[16,1536]{1,0:T(8,128)S(1)}, bf16[6,4,256,256]{3,2,1,0:T(8,128)(2,1)S(1)}) custom-call(s32[1]{0:T(128)} %bitcast.pos_ref.refs_0_, s32[4,32]{1,0:T(4,128)S(1)} %bitcast.5, f32[16,384]{1,0:T(8,128)S(1)} %slice_add_fusion.1.refs_2_, bf16[16,8192]{1,0:T(8,128)(2,1)S(1)} %collective-permute-done.2.refs_3_, ...), custom_call_target="tpu_custom_call" | custom-call | flops 1000000000 | bytes 1048576 | tf_op jit(solution)/shard_map/near_field/pallas_call | solution.py:276
  18.3 0.6 %collective-permute-done.1.refs_1_ = f32[16,384]{1,0:T(8,128)S(1)} collective-permute-done((f32[16,384]{1,0:T(8,128)S(1)}, f32[16,384]{1,0:T(8,128)S(1)}, u32[]{:S(2)}, u32[]{:S(2)}) %collective-permute-start.1) | collective-permute-done | bytes 24608 | tf_op jit(solution)/shard_map/ppermute | solution.py:362
  18.9 3.3 %near_field.7 = (f32[16,1536]{1,0:T(8,128)S(1)}, bf16[7,4,256,256]{3,2,1,0:T(8,128)(2,1)S(1)}) custom-call(s32[1]{0:T(128)} %bitcast.pos_ref.refs_0_, s32[4,32]{1,0:T(4,128)S(1)} %bitcast.6, f32[16,320]{1,0:T(8,128)S(1)} %slice_add_fusion.refs_2_, bf16[16,8192]{1,0:T(8,128)(2,1)S(1)} %collective-permute-done.2.refs_3_, ...), custom_call_target="tpu_custom_call" | custom-call | flops 1000000000 | bytes 1048576 | tf_op jit(solution)/shard_map/near_field/pallas_call | solution.py:276
  22.2 1.7 %collective-permute-done.4.refs_2_ = f32[16,320]{1,0:T(8,128)S(1)} collective-permute-done((f32[16,320]{1,0:T(8,128)S(1)}, f32[16,320]{1,0:T(8,128)S(1)}, u32[]{:S(2)}, u32[]{:S(2)}) %collective-permute-start.4) | collective-permute-done | bytes 20512 | tf_op jit(solution)/shard_map/ppermute | solution.py:362
  24.0 0.0 collective-permute-start.5
  24.0 3.3 %near_field.8 = (f32[16,1536]{1,0:T(8,128)S(1)}, bf16[7,4,256,256]{3,2,1,0:T(8,128)(2,1)S(1)}) custom-call(s32[1]{0:T(128)} %bitcast.pos_ref.refs_0_, s32[4,32]{1,0:T(4,128)S(1)} %bitcast.7, f32[16,256]{1,0:T(8,128)S(1)} %slice_add_fusion.3.refs_2_, bf16[16,8192]{1,0:T(8,128)(2,1)S(1)} %collective-permute-done.2.refs_3_, ...), custom_call_target="tpu_custom_call" | custom-call | flops 1000000000 | bytes 1048576 | tf_op jit(solution)/shard_map/near_field/pallas_call | solution.py:276
  27.3 0.4 collective-permute-done.5.refs_3_
  27.7 0.6 %collective-permute-start.6 = (f32[16,192]{1,0:T(8,128)S(1)}, f32[16,192]{1,0:T(8,128)S(1)}, u32[]{:S(2)}, u32[]{:S(2)}) collective-permute-start(f32[16,192]{1,0:T(8,128)S(1)} %slice_add_fusion.2.refs_2_), channel_id=1, source_target_pairs={{0,24},{1,25},{2,26},{3,27},{4,28},{5,29},{6,30},{7,31},{8,16},{9,... | collective-permute-start | bytes 36872 | tf_op jit(solution)/shard_map/ppermute | solution.py:362
  28.3 1.5 %near_field.9.refs_15_ = f32[16,1536]{1,0:T(8,128)S(1)} custom-call(s32[1]{0:T(128)} %bitcast.pos_ref.refs_0_, s32[4,32]{1,0:T(4,128)S(1)} %bitcast.8, f32[16,192]{1,0:T(8,128)S(1)} %slice_add_fusion.2.refs_2_, bf16[16,8192]{1,0:T(8,128)(2,1)S(1)} %collective-permute-done.2.refs_3_, bf16[16,8192]{1,0:T(8,128)(2,1)S(1)} %get-tuple-element.47.refs_4_, ...), custom_call_target="tpu_custom_call" | custom-call | flops 1000000000 | bytes 1048576 | tf_op jit(solution)/shard_map/near_field/pallas_call | solution.py:276
  29.7 2.9 %collective-permute-done.6.refs_4_ = f32[16,192]{1,0:T(8,128)S(1)} collective-permute-done((f32[16,192]{1,0:T(8,128)S(1)}, f32[16,192]{1,0:T(8,128)S(1)}, u32[]{:S(2)}, u32[]{:S(2)}) %collective-permute-start.6) | collective-permute-done | bytes 12320 | tf_op jit(solution)/shard_map/ppermute | solution.py:362
  32.7 0.4 %collective-permute-start.7 = (f32[16,128]{1,0:T(8,128)S(1)}, f32[16,128]{1,0:T(8,128)S(1)}, u32[]{:S(2)}, u32[]{:S(2)}) collective-permute-start(f32[16,128]{1,0:T(8,128)S(1)} %slice_add_fusion.5.refs_2_), channel_id=1, source_target_pairs={{0,32},{1,33},{2,34},{3,35},{4,36},{5,37},{6,38},{7,39},{8,40},{9,... | collective-permute-start | bytes 24584 | tf_op jit(solution)/shard_map/ppermute | solution.py:362
  33.1 1.5 %near_field.10.refs_16_ = f32[16,1536]{1,0:T(8,128)S(1)} custom-call(s32[1]{0:T(128)} %bitcast.pos_ref.refs_0_, s32[4,32]{1,0:T(4,128)S(1)} %bitcast.9, f32[16,128]{1,0:T(8,128)S(1)} %slice_add_fusion.5.refs_2_, bf16[16,8192]{1,0:T(8,128)(2,1)S(1)} %collective-permute-done.2.refs_3_, bf16[16,8192]{1,0:T(8,128)(2,1)S(1)} %get-tuple-element.47.refs_4_, ...), custom_call_target="tpu_custom_call" | custom-call | flops 1000000000 | bytes 1048576 | tf_op jit(solution)/shard_map/near_field/pallas_call | solution.py:276
  34.6 1.7 %collective-permute-done.7.refs_5_ = f32[16,128]{1,0:T(8,128)S(1)} collective-permute-done((f32[16,128]{1,0:T(8,128)S(1)}, f32[16,128]{1,0:T(8,128)S(1)}, u32[]{:S(2)}, u32[]{:S(2)}) %collective-permute-start.7) | collective-permute-done | bytes 8224 | tf_op jit(solution)/shard_map/ppermute | solution.py:362
  36.3 0.0 collective-permute-start.8
  36.3 1.3 %near_field.11 = (f32[16,512]{1,0:T(8,128)S(1)}, f32[31,16,128]{2,1,0:T(8,128)S(1)}) custom-call(s32[1]{0:T(128)} %bitcast.pos_ref.refs_0_, s32[4,32]{1,0:T(4,128)S(1)} %bitcast.10, f32[16,64]{1,0:T(8,128)S(1)} %slice_add_fusion.4.refs_2_, bf16[16,8192]{1,0:T(8,128)(2,1)S(1)} %collective-permute-done.2.refs_3_, ...), custom_call_target="tpu_custom_call" | custom-call | flops 1000000000 | bytes 1048576 | tf_op jit(solution)/shard_map/near_field/pallas_call | solution.py:276
  37.6 3.6 %collective-permute-done.8.refs_6_ = f32[16,64]{1,0:T(8,128)S(1)} collective-permute-done((f32[16,64]{1,0:T(8,128)S(1)}, f32[16,64]{1,0:T(8,128)S(1)}, u32[]{:S(2)}, u32[]{:S(2)}) %collective-permute-start.8) | collective-permute-done | bytes 4128 | tf_op jit(solution)/shard_map/ppermute | solution.py:362
  41.2 2.7 %down_sweep.1 = f32[16,8192]{1,0:T(8,128)} custom-call(f32[16,448]{1,0:T(8,128)S(1)} %collective-permute-done.refs_0_, f32[16,384]{1,0:T(8,128)S(1)} %collective-permute-done.1.refs_1_, f32[16,320]{1,0:T(8,128)S(1)} %collective-permute-done.4.refs_2_, f32[16,256]{1,0:T(8,128)S(1)} %collective-permute-done.5.refs_3_, ...), custom_call_target="tpu_custom_call" | custom-call | flops 3000000000 | bytes 1048576 | tf_op jit(solution)/shard_map/down_sweep/pallas_call | solution.py:323
  (11 shorter events, 0.0 us)
Async XLA Ops:
  0.0 15.1 %collective-permute-start.3 = (bf16[16,8192]{1,0:T(8,128)(2,1)}, bf16[16,8192]{1,0:T(8,128)(2,1)S(1)}, u32[]{:S(2)}, u32[]{:S(2)}) collective-permute-start(bf16[16,8192]{1,0:T(8,128)(2,1)} %rhs_hbm.1), channel_id=1, source_target_pairs={{0,0},{1,2},{2,1},{3,4},{4,3},{5,6},{6,5},{7,8},{8,7},{9,10},{10,9... | collective-permute-start | bytes 786440 | tf_op jit(solution)/shard_map/ppermute | solution.py:339
  7.8 7.4 %collective-permute-start.2 = (bf16[16,8192]{1,0:T(8,128)(2,1)}, bf16[16,8192]{1,0:T(8,128)(2,1)S(1)}, u32[]{:S(2)}, u32[]{:S(2)}) collective-permute-start(bf16[16,8192]{1,0:T(8,128)(2,1)} %rhs_hbm.1), channel_id=1, source_target_pairs={{0,1},{1,0},{2,3},{3,2},{4,5},{5,4},{6,7},{7,6},{8,9},{9,8},{10,11... | collective-permute-start | bytes 786440 | tf_op jit(solution)/shard_map/ppermute | solution.py:340
  12.3 2.7 %collective-permute-start = (f32[16,448]{1,0:T(8,128)S(1)}, f32[16,448]{1,0:T(8,128)S(1)}, u32[]{:S(2)}, u32[]{:S(2)}) collective-permute-start(f32[16,448]{1,0:T(8,128)S(1)} %get-tuple-element.38.order), channel_id=1, source_target_pairs={{0,1},{1,0},{2,3},{3,2},{4,5},{5,4},{6,7},{7,6},{8,9},{9,8},{10,11... | collective-permute-start | bytes 86024 | tf_op jit(solution)/shard_map/ppermute | solution.py:362
  12.8 2.3 %copy-start = (s32[32,4]{0,1:T(4,128)S(1)}, s32[32,4]{0,1:T(4,128)}, u32[]{:S(2)}) copy-start(s32[32,4]{0,1:T(4,128)} %param.11) | copy-start | bytes 1540
  15.0 3.9 %collective-permute-start.1 = (f32[16,384]{1,0:T(8,128)S(1)}, f32[16,384]{1,0:T(8,128)S(1)}, u32[]{:S(2)}, u32[]{:S(2)}) collective-permute-start(f32[16,384]{1,0:T(8,128)S(1)} %slice_add_fusion.1.refs_2_), channel_id=1, source_target_pairs={{0,2},{1,3},{2,0},{3,1},{4,6},{5,7},{6,4},{7,5},{8,10},{9,11},{10,... | collective-permute-start | bytes 73736 | tf_op jit(solution)/shard_map/ppermute | solution.py:362
  18.9 5.0 %collective-permute-start.4 = (f32[16,320]{1,0:T(8,128)S(1)}, f32[16,320]{1,0:T(8,128)S(1)}, u32[]{:S(2)}, u32[]{:S(2)}) collective-permute-start(f32[16,320]{1,0:T(8,128)S(1)} %slice_add_fusion.refs_2_), channel_id=1, source_target_pairs={{0,6},{1,7},{2,4},{3,5},{4,2},{5,3},{6,0},{7,1},{8,14},{9,15},{10,... | collective-permute-start | bytes 61448 | tf_op jit(solution)/shard_map/ppermute | solution.py:362
  24.0 3.7 %collective-permute-start.5 = (f32[16,256]{1,0:T(8,128)S(1)}, f32[16,256]{1,0:T(8,128)S(1)}, u32[]{:S(2)}, u32[]{:S(2)}) collective-permute-start(f32[16,256]{1,0:T(8,128)S(1)} %slice_add_fusion.3.refs_2_), channel_id=1, source_target_pairs={{0,8},{1,9},{2,10},{3,11},{4,12},{5,13},{6,14},{7,15},{8,0},{9,1},... | collective-permute-start | bytes 49160 | tf_op jit(solution)/shard_map/ppermute | solution.py:362
  27.7 4.9 %collective-permute-start.6 = (f32[16,192]{1,0:T(8,128)S(1)}, f32[16,192]{1,0:T(8,128)S(1)}, u32[]{:S(2)}, u32[]{:S(2)}) collective-permute-start(f32[16,192]{1,0:T(8,128)S(1)} %slice_add_fusion.2.refs_2_), channel_id=1, source_target_pairs={{0,24},{1,25},{2,26},{3,27},{4,28},{5,29},{6,30},{7,31},{8,16},{9,... | collective-permute-start | bytes 36872 | tf_op jit(solution)/shard_map/ppermute | solution.py:362
  32.7 3.7 %collective-permute-start.7 = (f32[16,128]{1,0:T(8,128)S(1)}, f32[16,128]{1,0:T(8,128)S(1)}, u32[]{:S(2)}, u32[]{:S(2)}) collective-permute-start(f32[16,128]{1,0:T(8,128)S(1)} %slice_add_fusion.5.refs_2_), channel_id=1, source_target_pairs={{0,32},{1,33},{2,34},{3,35},{4,36},{5,37},{6,38},{7,39},{8,40},{9,... | collective-permute-start | bytes 24584 | tf_op jit(solution)/shard_map/ppermute | solution.py:362
  36.3 4.9 %collective-permute-start.8 = (f32[16,64]{1,0:T(8,128)S(1)}, f32[16,64]{1,0:T(8,128)S(1)}, u32[]{:S(2)}, u32[]{:S(2)}) collective-permute-start(f32[16,64]{1,0:T(8,128)S(1)} %slice_add_fusion.4.refs_2_), channel_id=1, source_target_pairs={{0,96},{1,97},{2,98},{3,99},{4,100},{5,101},{6,102},{7,103},{8,104... | collective-permute-start | bytes 12296 | tf_op jit(solution)/shard_map/ppermute | solution.py:362

commit v3 on v2

--- a/solution.py
+++ b/solution.py
@@ -13,9 +13,8 @@
 VMEM = pl.BlockSpec(memory_space=pltpu.VMEM)
 HBM = pl.BlockSpec(memory_space=pltpu.HBM)
 SMEM = pl.BlockSpec(memory_space=pltpu.SMEM)
-NEAR_CHUNKS = (6, 6, 6, 6, 6, 2)
-FETCH = (8, 4, 6, 7, 7)
-MASKS = (1, 2, 6, 8, 24, 32, 96)
+NEAR_CHUNKS = (6, 6, 6, 7, 7)
+MASKS = (1, 3, 7, 9, 25, 33, 97)
 
 
 def split_rows(value):
@@ -102,8 +101,8 @@
     return pl.CostEstimate(flops=flops, bytes_accessed=size, transcendentals=0)
 
 
-def up_kernel(pos_ref, rhs_hbm, basis_hbm, trans_hbm, upper_hbm, upper_coup_hbm, coup_hbm, tiles_hbm,
-              coef_ref, path_ref, upper_ref, rhs, basis, trans, upper_coup, coup, tiles,
+def up_kernel(pos_ref, rhs_hbm, basis_hbm, trans_hbm, upper_hbm, upper_coup_hbm, coup_hbm,
+              coef_ref, path_ref, upper_ref, rhs, basis, trans, upper_coup, coup,
               upper, picked, sems):
     copies = start_all(
         [
@@ -112,7 +111,6 @@
             (trans_hbm, trans),
             (upper_hbm, upper),
             (upper_coup_hbm, upper_coup),
-            (tiles_hbm.at[: FETCH[0]], tiles),
             (coup_hbm, coup),
         ],
         sems,
@@ -160,7 +158,7 @@
         copy.wait()
 
 
-def up_sweep(position, rhs, basis_t, local_transfer, upper_transfer_t, upper_coupling_t, local_coupling, tiles):
+def up_sweep(position, rhs, basis_t, local_transfer, upper_transfer_t, upper_coupling_t, local_coupling):
     return pl.pallas_call(
         up_kernel,
         out_shape=(
@@ -172,75 +170,72 @@
             vmem_like(local_transfer),
             vmem_like(upper_coupling_t),
             vmem_like(local_coupling),
-            tiles_like(tiles, FETCH[0]),
         ),
-        in_specs=[SMEM] + [HBM] * 7,
-        out_specs=(VMEM,) * 9,
+        in_specs=[SMEM] + [HBM] * 6,
+        out_specs=(VMEM,) * 8,
         scratch_shapes=[
             pltpu.VMEM(upper_transfer_t.shape, BF16),
             pltpu.VMEM((512, 128), F32),
-            pltpu.SemaphoreType.DMA((7,)),
+            pltpu.SemaphoreType.DMA((6,)),
         ],
         compiler_params=params(),
         cost_estimate=cost(4 * 10**9, 12 * 2**20),
         name="up_sweep",
     )(
         position,
-        *in_hbm(rhs, basis_t, local_transfer, upper_transfer_t, upper_coupling_t, local_coupling, tiles),
-    )
-
-
-def pick_kernel(pos_ref, order, upper, tiles_hbm, *refs):
+        *in_hbm(rhs, basis_t, local_transfer, upper_transfer_t, upper_coupling_t, local_coupling),
+    )
+
+
+def pick_kernel(pos_ref, order, upper, *refs):
     del order
-    upper_ref, tiles, picked, sems = refs[-4:]
-    copies = start_all([(tiles_hbm.at[FETCH[0] : FETCH[0] + FETCH[1]], tiles)], sems)
+    upper_ref, picked = refs[-2:]
     pick_nodes(pos_ref[0], upper, picked)
     for level in range(7):
         upper_ref[level] = picked[64 * level : 64 * level + 64, 0:64].astype(BF16)
-    copies[0].wait()
-
-
-def pick_couplings(position, order, upper_coupling_t, tiles, keep):
+
+
+def pick_couplings(position, order, upper_coupling_t, keep):
     return pl.pallas_call(
         pick_kernel,
-        out_shape=(vmem((7, 64, 64), BF16), tiles_like(tiles, FETCH[1])),
-        in_specs=[SMEM, ANY, VMEM, HBM] + [VMEM] * len(keep),
-        out_specs=(VMEM, VMEM),
-        scratch_shapes=[pltpu.VMEM((512, 128), F32), pltpu.SemaphoreType.DMA((1,))],
+        out_shape=vmem((7, 64, 64), BF16),
+        in_specs=[SMEM, ANY, VMEM] + [VMEM] * len(keep),
+        out_specs=VMEM,
+        scratch_shapes=[pltpu.VMEM((512, 128), F32)],
         compiler_params=params(),
         cost_estimate=cost(10**9, 2**20),
         name="pick_couplings",
-    )(position, order, upper_coupling_t, *in_hbm(tiles), *keep)
-
-
-def near_kernel(first, count, fetched, fetch, with_far, *refs):
-    pos_ref, pairs_ref, order, inner, own, outer = refs[:6]
+    )(position, order, upper_coupling_t, *keep)
+
+
+def far_kernel(order, coef, coup, *refs):
     del order
-    at = 6
-    held = refs[at : at + fetched]
-    at += fetched
-    coef, coup = refs[at : at + 2]
-    at += 4
-    if fetch:
-        tiles_hbm = refs[at]
-        at += 1
-    out_ref = refs[at]
-    at += 1
-    if with_far:
-        far_ref = refs[at]
-        at += 1
-    if fetch:
-        start = sum(FETCH[:fetch])
-        copies = start_all([(tiles_hbm.at[start : start + FETCH[fetch]], refs[at])], refs[at + 1])
+    far_ref = refs[-1]
+    for pair in range(31):
+        swapped = pltpu.roll(coef[pair], 64, 1)
+        both = times(apart(swapped), coup[2 * pair : 2 * pair + 2].reshape(128, 64))
+        far_ref[pair] = jnp.concatenate([both[:16], both[16:]], axis=1)
+
+
+def far_fields(order, coef, coup, keep):
+    return pl.pallas_call(
+        far_kernel,
+        out_shape=vmem((31, 16, 128), F32),
+        in_specs=[ANY] + [VMEM] * (2 + len(keep)),
+        out_specs=VMEM,
+        compiler_params=params(),
+        cost_estimate=cost(10**9, 2**20),
+        name="far_fields",
+    )(order, coef, coup, *keep)
+
+
+def near_kernel(first, count, pos_ref, pairs_ref, order, inner, own, outer, tiles, *refs):
+    del order
+    out_ref = refs[-1]
     dims = (((1,), (1,)), ((), ()))
     position = pos_ref[0]
     for i in range(count):
         total = None
-        place = first + i
-        box = 0
-        while place >= FETCH[box]:
-            place -= FETCH[box]
-            box += 1
         for k in range(4):
             leaf = pairs_ref[k, first + i]
             holder = lax.shift_right_logical(leaf, 5)
@@ -249,40 +244,21 @@
                 holder == position, own[:, column],
                 jnp.where(holder == position ^ 1, inner[:, column], outer[:, column]),
             )
-            part = lax.dot_general(source, held[box][place, k], dims, preferred_element_type=F32)
+            part = lax.dot_general(source, tiles[first + i, k], dims, preferred_element_type=F32)
             total = part if total is None else total + part
         out_ref[:, 256 * i : 256 * i + 256] = total
-    if with_far:
-        for pair in range(31):
-            swapped = pltpu.roll(coef[pair], 64, 1)
-            both = times(apart(swapped), coup[2 * pair : 2 * pair + 2].reshape(128, 64))
-            far_ref[pair] = jnp.concatenate([both[:16], both[16:]], axis=1)
-    if fetch:
-        copies[0].wait()
-
-
-def near_field(first, count, position, near_pairs_t, order, inner, own, outer, held, keep, fetch, tiles, with_far):
-    inputs = [position, near_pairs_t, order, inner, own, outer, *held, *keep]
-    in_specs = [SMEM, SMEM, ANY] + [VMEM] * (len(inputs) - 3)
-    outputs = [vmem((16, 256 * count), F32)]
-    scratch = []
-    if with_far:
-        outputs.append(vmem((31, 16, 128), F32))
-    if fetch:
-        inputs += in_hbm(tiles)
-        in_specs.append(HBM)
-        outputs.append(tiles_like(tiles, FETCH[fetch]))
-        scratch = [pltpu.SemaphoreType.DMA((1,))]
-    return pl.pallas_call(
-        functools.partial(near_kernel, first, count, len(held), fetch, with_far),
-        out_shape=tuple(outputs),
-        in_specs=in_specs,
-        out_specs=(VMEM,) * len(outputs),
-        scratch_shapes=scratch,
+
+
+def near_field(first, count, position, near_pairs_t, order, inner, own, outer, tiles, keep):
+    return pl.pallas_call(
+        functools.partial(near_kernel, first, count),
+        out_shape=vmem((16, 256 * count), F32),
+        in_specs=[SMEM, SMEM, ANY] + [VMEM] * (4 + len(keep)),
+        out_specs=VMEM,
         compiler_params=params(),
         cost_estimate=cost(10**9, 2**20),
         name="near_field",
-    )(*inputs)
+    )(position, near_pairs_t, order, inner, own, outer, tiles, *keep)
 
 
 def down_kernel(*refs):
@@ -308,15 +284,14 @@
         fields = []
         for pair in pairs:
             fields += [pair[:, 0:64], pair[:, 64:128]]
-    leaf = 0
-    for nearby_ref, count in zip(nearby, NEAR_CHUNKS):
-        for i in range(0, count, 2):
-            both = times(apart(pairs[leaf // 2]), basis[leaf : leaf + 2].reshape(128, 256))
-            for j in range(2):
-                out_ref[:, 256 * (leaf + j) : 256 * (leaf + j) + 256] = (
-                    both[16 * j : 16 * j + 16] + nearby_ref[:, 256 * (i + j) : 256 * (i + j) + 256]
-                )
-            leaf += 2
+    places = [(box, i) for box, count in enumerate(NEAR_CHUNKS) for i in range(count)]
+    for leaf in range(0, 32, 2):
+        both = times(apart(pairs[leaf // 2]), basis[leaf : leaf + 2].reshape(128, 256))
+        for j in range(2):
+            box, i = places[leaf + j]
+            out_ref[:, 256 * (leaf + j) : 256 * (leaf + j) + 256] = (
+                both[16 * j : 16 * j + 16] + nearby[box][:, 256 * i : 256 * i + 256]
+            )
 
 
 def down_sweep(siblings, upper_trans, upper_coup, far, local_transfer, basis_t, nearby):
@@ -334,25 +309,22 @@
 def local(rhs, leaf_basis, near_tiles, near_pairs, local_transfer, local_coupling, upper_transfer, upper_coupling):
     devices = lax.axis_size("leaf")
     position = lax.axis_index("leaf").astype(jnp.int32)
+    where = position.reshape(1)
     last = devices - 1
     outward = [(i, min(max(i + 2 * (i & 1) - 1, 0), last)) for i in range(devices)]
-    outer = lax.ppermute(rhs, "leaf", outward)
-    inner = lax.ppermute(rhs, "leaf", [(i, i ^ 1) for i in range(devices)])
+    inward = [(i, i ^ 1) for i in range(devices)]
     near_pairs_t = jnp.transpose(near_pairs, (1, 0))
-    basis_t = jnp.transpose(leaf_basis, (0, 2, 1))
-    where = position.reshape(1)
-    coef, path, upper_trans, own, basis, trans, upper_coup, coup, tiles = up_sweep(
+    coef, path, upper_trans, own, basis, trans, upper_coup, coup = up_sweep(
         where,
         rhs,
-        basis_t,
+        jnp.transpose(leaf_basis, (0, 2, 1)),
         local_transfer,
         jnp.transpose(upper_transfer, (1, 2, 0)),
         jnp.transpose(upper_coupling, (1, 2, 0)),
         local_coupling,
-        near_tiles,
-    )
-    held = [tiles]
-    keep = [coef, coup, trans, basis]
+    )
+    outer = lax.ppermute(own, "leaf", outward)
+    inner = lax.ppermute(own, "leaf", inward)
     nearby = []
     siblings = []
     first = 0
@@ -361,21 +333,16 @@
         pairs = [(i, i ^ MASKS[level]) for i in range(devices)]
         received = lax.ppermute(path, "leaf", pairs)
         if level == 0:
-            upper_coup, tiles = pick_couplings(where, path, upper_coup, near_tiles, held + keep)
-            held.append(tiles)
+            upper_coup = pick_couplings(where, path, upper_coup, [coef, coup, trans, basis])
             received, upper_coup = lax.optimization_barrier((received, upper_coup))
+        elif level == 1:
+            far = far_fields(path, coef, coup, [trans, basis])
+            received, far = lax.optimization_barrier((received, far))
         else:
-            count = NEAR_CHUNKS[level - 1]
-            fetch = level + 1 if level + 1 < len(FETCH) else 0
-            last_chunk = level == 6
-            results = near_field(
-                first, count, where, near_pairs_t, path, inner, own, outer, held, keep, fetch, near_tiles, last_chunk
+            count = NEAR_CHUNKS[level - 2]
+            part = near_field(
+                first, count, where, near_pairs_t, path, inner, own, outer, near_tiles, [far, trans, basis]
             )
-            part = results[0]
-            if fetch:
-                held.append(results[-1])
-            if last_chunk:
-                far = results[1]
             first += count
             received, part = lax.optimization_barrier((received, part))
             nearby.append(part)

time: 44.2 us -> 41.1 us (0.930)
  the two profiles are of different devices: /device:TPU:24 before, /device:TPU:1 now
where the time goes in v3:
time: 41.1 us; the launch traced here: 41 us
  starting transfers between devices  22.8 us (55%)
  Pallas kernels  16.2 us (39%)
  waiting for transfers between devices  1.87 us (5%)
    ppermute x7, starting transfers between devices, local(): received = lax.ppermute(path, 'leaf', pairs)  18 us
    pallas_call x5, Pallas kernels, near_field(): pl.pallas_call(functools.partial(near_kernel, first, count), out_shape=vm...  7.66 us
    ppermute x1, starting transfers between devices, local(): outer = lax.ppermute(own, 'leaf', outward)  4.77 us
    pallas_call x1, Pallas kernels, up_sweep(): pl.pallas_call(up_kernel, out_shape=(vmem((31, 16, 128), F32), vmem((16,...  4.44 us
    pallas_call x1, Pallas kernels, down_sweep(): pl.pallas_call(down_kernel, out_shape=jax.ShapeDtypeStruct((16, 8192), F3...  2.77 us
    ppermute x7, waiting for transfers between devices, local(): received = lax.ppermute(path, 'leaf', pairs)  1.87 us
  transfers between devices with their start and end apart: 9, of which 3 were waited for; matrix products, arithmetic and copies ran while one was open for 0% of the time, Pallas kernels for 22%

profile of v3, /device:TPU:1, one launch (start us, length us, event | category | flops | bytes accessed | tf_op | source)
XLA Modules:
  0.0 41.0 jit_solution(6748457214193356731)
XLA Ops:
  0.0 4.4 %up_sweep.1 = (f32[31,16,128]{2,1,0:T(8,128)S(1)}, f32[16,448]{1,0:T(8,128)S(1)}, bf16[6,64,64]{2,1,0:T(8,128)(2,1)S(1)}, bf16[16,8192]{1,0:T(8,128)(2,1)S(1)}, ...) custom-call(s32[1]{0:T(128)} %bitcast.pos_ref, ...), custom_call_target="tpu_custom_call" | custom-call | flops 4000000000 | bytes 12582912 | tf_op jit(solution)/shard_map/up_sweep/pallas_call | solution.py:162
  4.5 4.8 %collective-permute-start.4 = (bf16[16,8192]{1,0:T(8,128)(2,1)S(1)}, bf16[16,8192]{1,0:T(8,128)(2,1)S(1)}, u32[]{:S(2)}, u32[]{:S(2)}) collective-permute-start(bf16[16,8192]{1,0:T(8,128)(2,1)S(1)} %get-tuple-element.35.own), channel_id=1, source_target_pairs={{0,0},{1,2},{2,1},{3,4},{4,3},{5,6},{6,5},{7,8},{8,7},{9,10},{10,9... | collective-permute-start | bytes 786440 | tf_op jit(solution)/shard_map/ppermute | solution.py:326
  9.2 0.1 collective-permute-start.3
  9.3 0.5 %collective-permute-start = (f32[16,448]{1,0:T(8,128)S(1)}, f32[16,448]{1,0:T(8,128)S(1)}, u32[]{:S(2)}, u32[]{:S(2)}) collective-permute-start(f32[16,448]{1,0:T(8,128)S(1)} %get-tuple-element.27.order), channel_id=1, source_target_pairs={{0,1},{1,0},{2,3},{3,2},{4,5},{5,4},{6,7},{7,6},{8,9},{9,8},{10,11... | collective-permute-start | bytes 86024 | tf_op jit(solution)/shard_map/ppermute | solution.py:334
  9.8 0.8 %pick_couplings.1.refs_8_ = bf16[7,64,64]{2,1,0:T(8,128)(2,1)S(1)} custom-call(s32[1]{0:T(128)} %bitcast.pos_ref, f32[16,448]{1,0:T(8,128)S(1)} %get-tuple-element.27.order, bf16[64,64,254]{2,1,0:T(8,128)(2,1)S(1)} %get-tuple-element.28.upper, f32[31,16,128]{2,1,0:T(8,128)S(1)} %get-tuple-element.29.refs_0_.coef, ...), custom_call_target="tpu_custom_call" | custom-call | flops 1000000000 | bytes 1048576 | tf_op jit(solution)/shard_map/pick_couplings/pallas_call | solution.py:199
  10.6 0.0 copy-start.1
  10.6 0.3 collective-permute-done.refs_0_
  10.9 1.2 %collective-permute-start.1 = (f32[16,384]{1,0:T(8,128)S(1)}, f32[16,384]{1,0:T(8,128)S(1)}, u32[]{:S(2)}, u32[]{:S(2)}) collective-permute-start(f32[16,384]{1,0:T(8,128)S(1)} %slice_add_fusion.1.order), channel_id=1, source_target_pairs={{0,3},{1,2},{2,1},{3,0},{4,7},{5,6},{6,5},{7,4},{8,11},{9,10},{10,... | collective-permute-start | bytes 73736 | tf_op jit(solution)/shard_map/ppermute | solution.py:334
  12.2 0.5 %far_fields.1.refs_0_.refs_9_ = f32[31,16,128]{2,1,0:T(8,128)S(1)} custom-call(f32[16,384]{1,0:T(8,128)S(1)} %slice_add_fusion.1.order, f32[31,16,128]{2,1,0:T(8,128)S(1)} %get-tuple-element.29.refs_0_.coef, bf16[62,64,64]{2,1,0:T(8,128)(2,1)S(1)} %get-tuple-element.30.refs_1_.coup, ...), custom_call_target="tpu_custom_call" | custom-call | flops 1000000000 | bytes 1048576 | tf_op jit(solution)/shard_map/far_fields/pallas_call | solution.py:221
  12.7 1.5 %collective-permute-done.1.refs_1_ = f32[16,384]{1,0:T(8,128)S(1)} collective-permute-done((f32[16,384]{1,0:T(8,128)S(1)}, f32[16,384]{1,0:T(8,128)S(1)}, u32[]{:S(2)}, u32[]{:S(2)}) %collective-permute-start.1) | collective-permute-done | bytes 24608 | tf_op jit(solution)/shard_map/ppermute | solution.py:334
  14.2 2.9 %collective-permute-start.2 = (f32[16,320]{1,0:T(8,128)S(1)}, f32[16,320]{1,0:T(8,128)S(1)}, u32[]{:S(2)}, u32[]{:S(2)}) collective-permute-start(f32[16,320]{1,0:T(8,128)S(1)} %slice_add_fusion.order), channel_id=1, source_target_pairs={{0,7},{1,6},{2,5},{3,4},{4,3},{5,2},{6,1},{7,0},{8,15},{9,14},{10,... | collective-permute-start | bytes 61448 | tf_op jit(solution)/shard_map/ppermute | solution.py:334
  17.0 0.0 collective-permute-done.4.outer
  17.0 0.0 collective-permute-done.3.inner
  17.1 1.5 %near_field.5.refs_12_ = f32[16,1536]{1,0:T(8,128)S(1)} custom-call(s32[1]{0:T(128)} %bitcast.pos_ref, s32[4,32]{1,0:T(4,128)S(1)} %bitcast.5, f32[16,320]{1,0:T(8,128)S(1)} %slice_add_fusion.order, bf16[16,8192]{1,0:T(8,128)(2,1)S(1)} %collective-permute-done.3.inner, bf16[16,8192]{1,0:T(8,128)(2,1)S(1)} %get-tuple-element.35.own, ...), custom_call_target="tpu_custom_call" | custom-call | flops 1000000000 | bytes 1048576 | tf_op jit(solution)/shard_map/near_field/pallas_call | solution.py:253
  18.5 0.1 collective-permute-done.2.refs_2_
  18.6 2.2 %collective-permute-start.5 = (f32[16,256]{1,0:T(8,128)S(1)}, f32[16,256]{1,0:T(8,128)S(1)}, u32[]{:S(2)}, u32[]{:S(2)}) collective-permute-start(f32[16,256]{1,0:T(8,128)S(1)} %slice_add_fusion.3.order), channel_id=1, source_target_pairs={{0,9},{1,8},{2,11},{3,10},{4,13},{5,12},{6,15},{7,14},{8,1},{9,0},... | collective-permute-start | bytes 49160 | tf_op jit(solution)/shard_map/ppermute | solution.py:334
  20.8 1.5 %near_field.6.refs_13_ = f32[16,1536]{1,0:T(8,128)S(1)} custom-call(s32[1]{0:T(128)} %bitcast.pos_ref, s32[4,32]{1,0:T(4,128)S(1)} %bitcast.6, f32[16,256]{1,0:T(8,128)S(1)} %slice_add_fusion.3.order, bf16[16,8192]{1,0:T(8,128)(2,1)S(1)} %collective-permute-done.3.inner, bf16[16,8192]{1,0:T(8,128)(2,1)S(1)} %get-tuple-element.35.own, ...), custom_call_target="tpu_custom_call" | custom-call | flops 1000000000 | bytes 1048576 | tf_op jit(solution)/shard_map/near_field/pallas_call | solution.py:253
  22.3 4.1 %collective-permute-start.6 = (f32[16,192]{1,0:T(8,128)S(1)}, f32[16,192]{1,0:T(8,128)S(1)}, u32[]{:S(2)}, u32[]{:S(2)}) collective-permute-start(f32[16,192]{1,0:T(8,128)S(1)} %slice_add_fusion.2.order), channel_id=1, source_target_pairs={{0,25},{1,24},{2,27},{3,26},{4,29},{5,28},{6,31},{7,30},{8,17},{9,... | collective-permute-start | bytes 36872 | tf_op jit(solution)/shard_map/ppermute | solution.py:334
  26.4 1.5 %near_field.7.refs_14_ = f32[16,1536]{1,0:T(8,128)S(1)} custom-call(s32[1]{0:T(128)} %bitcast.pos_ref, s32[4,32]{1,0:T(4,128)S(1)} %bitcast.7, f32[16,192]{1,0:T(8,128)S(1)} %slice_add_fusion.2.order, bf16[16,8192]{1,0:T(8,128)(2,1)S(1)} %collective-permute-done.3.inner, bf16[16,8192]{1,0:T(8,128)(2,1)S(1)} %get-tuple-element.35.own, ...), custom_call_target="tpu_custom_call" | custom-call | flops 1000000000 | bytes 1048576 | tf_op jit(solution)/shard_map/near_field/pallas_call | solution.py:253
  27.9 3.9 %collective-permute-start.7 = (f32[16,128]{1,0:T(8,128)S(1)}, f32[16,128]{1,0:T(8,128)S(1)}, u32[]{:S(2)}, u32[]{:S(2)}) collective-permute-start(f32[16,128]{1,0:T(8,128)S(1)} %slice_add_fusion.5.order), channel_id=1, source_target_pairs={{0,33},{1,32},{2,35},{3,34},{4,37},{5,36},{6,39},{7,38},{8,41},{9,... | collective-permute-start | bytes 24584 | tf_op jit(solution)/shard_map/ppermute | solution.py:334
  31.8 1.6 %near_field.8.refs_15_ = f32[16,1792]{1,0:T(8,128)S(1)} custom-call(s32[1]{0:T(128)} %bitcast.pos_ref, s32[4,32]{1,0:T(4,128)S(1)} %bitcast.8, f32[16,128]{1,0:T(8,128)S(1)} %slice_add_fusion.5.order, bf16[16,8192]{1,0:T(8,128)(2,1)S(1)} %collective-permute-done.3.inner, bf16[16,8192]{1,0:T(8,128)(2,1)S(1)} %get-tuple-element.35.own, ...), custom_call_target="tpu_custom_call" | custom-call | flops 1000000000 | bytes 1048576 | tf_op jit(solution)/shard_map/near_field/pallas_call | solution.py:253
  33.5 3.2 %collective-permute-start.8 = (f32[16,64]{1,0:T(8,128)S(1)}, f32[16,64]{1,0:T(8,128)S(1)}, u32[]{:S(2)}, u32[]{:S(2)}) collective-permute-start(f32[16,64]{1,0:T(8,128)S(1)} %slice_add_fusion.4.order), channel_id=1, source_target_pairs={{0,97},{1,96},{2,99},{3,98},{4,101},{5,100},{6,103},{7,102},{8,105... | collective-permute-start | bytes 12296 | tf_op jit(solution)/shard_map/ppermute | solution.py:334
  36.6 1.6 %near_field.9.refs_16_ = f32[16,1792]{1,0:T(8,128)S(1)} custom-call(s32[1]{0:T(128)} %bitcast.pos_ref, s32[4,32]{1,0:T(4,128)S(1)} %bitcast.9, f32[16,64]{1,0:T(8,128)S(1)} %slice_add_fusion.4.order, bf16[16,8192]{1,0:T(8,128)(2,1)S(1)} %collective-permute-done.3.inner, bf16[16,8192]{1,0:T(8,128)(2,1)S(1)} %get-tuple-element.35.own, ...), custom_call_target="tpu_custom_call" | custom-call | flops 1000000000 | bytes 1048576 | tf_op jit(solution)/shard_map/near_field/pallas_call | solution.py:253
  38.3 2.8 %down_sweep.1 = f32[16,8192]{1,0:T(8,128)} custom-call(f32[16,448]{1,0:T(8,128)S(1)} %collective-permute-done.refs_0_, f32[16,384]{1,0:T(8,128)S(1)} %collective-permute-done.1.refs_1_, f32[16,320]{1,0:T(8,128)S(1)} %collective-permute-done.2.refs_2_, f32[16,256]{1,0:T(8,128)S(1)} %collective-permute-done.5.refs_3_, ...), custom_call_target="tpu_custom_call" | custom-call | flops 3000000000 | bytes 1048576 | tf_op jit(solution)/shard_map/down_sweep/pallas_call | solution.py:298
  (13 shorter events, 0.1 us)
Async XLA Ops:
  0.0 17.0 %copy-start = (bf16[32,4,256,256]{3,2,1,0:T(8,128)(2,1)S(1)}, bf16[32,4,256,256]{3,2,1,0:T(8,128)(2,1)}, u32[]{:S(2)}) copy-start(bf16[32,4,256,256]{3,2,1,0:T(8,128)(2,1)} %tiles.9) | copy-start | bytes 50331652
  4.5 12.6 %collective-permute-start.4 = (bf16[16,8192]{1,0:T(8,128)(2,1)S(1)}, bf16[16,8192]{1,0:T(8,128)(2,1)S(1)}, u32[]{:S(2)}, u32[]{:S(2)}) collective-permute-start(bf16[16,8192]{1,0:T(8,128)(2,1)S(1)} %get-tuple-element.35.own), channel_id=1, source_target_pairs={{0,0},{1,2},{2,1},{3,4},{4,3},{5,6},{6,5},{7,8},{8,7},{9,10},{10,9... | collective-permute-start | bytes 786440 | tf_op jit(solution)/shard_map/ppermute | solution.py:326
  9.2 7.8 %collective-permute-start.3 = (bf16[16,8192]{1,0:T(8,128)(2,1)S(1)}, bf16[16,8192]{1,0:T(8,128)(2,1)S(1)}, u32[]{:S(2)}, u32[]{:S(2)}) collective-permute-start(bf16[16,8192]{1,0:T(8,128)(2,1)S(1)} %get-tuple-element.35.own), channel_id=1, source_target_pairs={{0,1},{1,0},{2,3},{3,2},{4,5},{5,4},{6,7},{7,6},{8,9},{9,8},{10,11... | collective-permute-start | bytes 786440 | tf_op jit(solution)/shard_map/ppermute | solution.py:327
  9.3 1.6 %collective-permute-start = (f32[16,448]{1,0:T(8,128)S(1)}, f32[16,448]{1,0:T(8,128)S(1)}, u32[]{:S(2)}, u32[]{:S(2)}) collective-permute-start(f32[16,448]{1,0:T(8,128)S(1)} %get-tuple-element.27.order), channel_id=1, source_target_pairs={{0,1},{1,0},{2,3},{3,2},{4,5},{5,4},{6,7},{7,6},{8,9},{9,8},{10,11... | collective-permute-start | bytes 86024 | tf_op jit(solution)/shard_map/ppermute | solution.py:334
  10.6 6.5 %copy-start.1 = (s32[32,4]{0,1:T(4,128)S(1)}, s32[32,4]{0,1:T(4,128)}, u32[]{:S(2)}) copy-start(s32[32,4]{0,1:T(4,128)} %param.11) | copy-start | bytes 1540
  10.9 3.3 %collective-permute-start.1 = (f32[16,384]{1,0:T(8,128)S(1)}, f32[16,384]{1,0:T(8,128)S(1)}, u32[]{:S(2)}, u32[]{:S(2)}) collective-permute-start(f32[16,384]{1,0:T(8,128)S(1)} %slice_add_fusion.1.order), channel_id=1, source_target_pairs={{0,3},{1,2},{2,1},{3,0},{4,7},{5,6},{6,5},{7,4},{8,11},{9,10},{10,... | collective-permute-start | bytes 73736 | tf_op jit(solution)/shard_map/ppermute | solution.py:334
  14.2 4.5 %collective-permute-start.2 = (f32[16,320]{1,0:T(8,128)S(1)}, f32[16,320]{1,0:T(8,128)S(1)}, u32[]{:S(2)}, u32[]{:S(2)}) collective-permute-start(f32[16,320]{1,0:T(8,128)S(1)} %slice_add_fusion.order), channel_id=1, source_target_pairs={{0,7},{1,6},{2,5},{3,4},{4,3},{5,2},{6,1},{7,0},{8,15},{9,14},{10,... | collective-permute-start | bytes 61448 | tf_op jit(solution)/shard_map/ppermute | solution.py:334
  18.6 3.6 %collective-permute-start.5 = (f32[16,256]{1,0:T(8,128)S(1)}, f32[16,256]{1,0:T(8,128)S(1)}, u32[]{:S(2)}, u32[]{:S(2)}) collective-permute-start(f32[16,256]{1,0:T(8,128)S(1)} %slice_add_fusion.3.order), channel_id=1, source_target_pairs={{0,9},{1,8},{2,11},{3,10},{4,13},{5,12},{6,15},{7,14},{8,1},{9,0},... | collective-permute-start | bytes 49160 | tf_op jit(solution)/shard_map/ppermute | solution.py:334
  22.3 5.6 %collective-permute-start.6 = (f32[16,192]{1,0:T(8,128)S(1)}, f32[16,192]{1,0:T(8,128)S(1)}, u32[]{:S(2)}, u32[]{:S(2)}) collective-permute-start(f32[16,192]{1,0:T(8,128)S(1)} %slice_add_fusion.2.order), channel_id=1, source_target_pairs={{0,25},{1,24},{2,27},{3,26},{4,29},{5,28},{6,31},{7,30},{8,17},{9,... | collective-permute-start | bytes 36872 | tf_op jit(solution)/shard_map/ppermute | solution.py:334
  27.9 5.6 %collective-permute-start.7 = (f32[16,128]{1,0:T(8,128)S(1)}, f32[16,128]{1,0:T(8,128)S(1)}, u32[]{:S(2)}, u32[]{:S(2)}) collective-permute-start(f32[16,128]{1,0:T(8,128)S(1)} %slice_add_fusion.5.order), channel_id=1, source_target_pairs={{0,33},{1,32},{2,35},{3,34},{4,37},{5,36},{6,39},{7,38},{8,41},{9,... | collective-permute-start | bytes 24584 | tf_op jit(solution)/shard_map/ppermute | solution.py:334
  33.5 4.8 %collective-permute-start.8 = (f32[16,64]{1,0:T(8,128)S(1)}, f32[16,64]{1,0:T(8,128)S(1)}, u32[]{:S(2)}, u32[]{:S(2)}) collective-permute-start(f32[16,64]{1,0:T(8,128)S(1)} %slice_add_fusion.4.order), channel_id=1, source_target_pairs={{0,97},{1,96},{2,99},{3,98},{4,101},{5,100},{6,103},{7,102},{8,105... | collective-permute-start | bytes 12296 | tf_op jit(solution)/shard_map/ppermute | solution.py:334

commit v4 on v3

--- a/solution.py
+++ b/solution.py
@@ -103,20 +103,31 @@
 
 def up_kernel(pos_ref, rhs_hbm, basis_hbm, trans_hbm, upper_hbm, upper_coup_hbm, coup_hbm,
               coef_ref, path_ref, upper_ref, rhs, basis, trans, upper_coup, coup,
-              upper, picked, sems):
+              upper, picked, high, low, sems):
     copies = start_all(
         [
+            (upper_hbm, upper),
             (rhs_hbm, rhs),
             (basis_hbm, basis),
             (trans_hbm, trans),
-            (upper_hbm, upper),
             (upper_coup_hbm, upper_coup),
             (coup_hbm, coup),
         ],
         sems,
     )
     copies[0].wait()
-    copies[1].wait()
+    pick_nodes(pos_ref[0], upper, picked)
+    for copy in copies[1:4]:
+        copy.wait()
+    maps = None
+    for level in range(6):
+        matrix = picked[64 * level : 64 * level + 64, 0:64].astype(BF16)
+        upper_ref[level] = matrix
+        maps = matrix.astype(F32) if level == 0 else times(maps, matrix)
+        lanes = slice(64 * (5 - level), 64 * (6 - level))
+        head = maps.astype(BF16)
+        high[:, lanes] = head
+        low[:, lanes] = (maps - head.astype(F32)).astype(BF16)
     dims = (((1,), (1,)), ((), ()))
     current = []
     for pair in range(16):
@@ -129,7 +140,6 @@
         value = jnp.where(left_half((16, 128)), both[:16], both[16:])
         coef_ref[pair] = value
         current.append(value)
-    copies[2].wait()
     base = 0
     while True:
         parents = [
@@ -144,16 +154,11 @@
         ]
         for i, value in enumerate(current):
             coef_ref[base + i] = value
-    copies[3].wait()
-    pick_nodes(pos_ref[0], upper, picked)
-    value = parents[0]
-    path_ref[:, 384:448] = value
-    for level in range(6):
-        matrix = picked[64 * level : 64 * level + 64, 0:64].astype(BF16)
-        upper_ref[level] = matrix
-        value = times(value, matrix)
-        start = 64 * (5 - level)
-        path_ref[:, start : start + 64] = value
+    root = parents[0]
+    path_ref[:, 384:448] = root
+    path_ref[:, 0:384] = times(root, high[...]) + jnp.dot(
+        root.astype(BF16), low[...], preferred_element_type=F32
+    )
     for copy in copies[4:]:
         copy.wait()
 
@@ -176,10 +181,12 @@
         scratch_shapes=[
             pltpu.VMEM(upper_transfer_t.shape, BF16),
             pltpu.VMEM((512, 128), F32),
+            pltpu.VMEM((64, 384), BF16),
+            pltpu.VMEM((64, 384), BF16),
             pltpu.SemaphoreType.DMA((6,)),
         ],
         compiler_params=params(),
-        cost_estimate=cost(4 * 10**9, 12 * 2**20),
+        cost_estimate=cost(4 * 10**9, 2**20),
         name="up_sweep",
     )(
         position,
@@ -203,37 +210,45 @@
         out_specs=VMEM,
         scratch_shapes=[pltpu.VMEM((512, 128), F32)],
         compiler_params=params(),
-        cost_estimate=cost(10**9, 2**20),
+        cost_estimate=cost(6 * 10**9, 2**20),
         name="pick_couplings",
     )(position, order, upper_coupling_t, *keep)
 
 
-def far_kernel(order, coef, coup, *refs):
+def far_kernel(order, coef, coup, upper_trans, upper_coup, *refs):
     del order
-    far_ref = refs[-1]
+    far_ref, high_ref, low_ref = refs[-3:]
+    maps = upper_coup[6].astype(F32)
+    for level in range(5, -1, -1):
+        maps = times_transposed(maps, upper_trans[level])
+        maps = jnp.concatenate([maps, upper_coup[level].astype(F32)], axis=0)
+    high = maps.astype(BF16)
+    high_ref[...] = high
+    low_ref[...] = (maps - high.astype(F32)).astype(BF16)
     for pair in range(31):
         swapped = pltpu.roll(coef[pair], 64, 1)
         both = times(apart(swapped), coup[2 * pair : 2 * pair + 2].reshape(128, 64))
         far_ref[pair] = jnp.concatenate([both[:16], both[16:]], axis=1)
 
 
-def far_fields(order, coef, coup, keep):
+def far_fields(order, coef, coup, upper_trans, upper_coup, keep):
     return pl.pallas_call(
         far_kernel,
-        out_shape=vmem((31, 16, 128), F32),
-        in_specs=[ANY] + [VMEM] * (2 + len(keep)),
-        out_specs=VMEM,
+        out_shape=(vmem((31, 16, 128), F32), vmem((448, 64), BF16), vmem((448, 64), BF16)),
+        in_specs=[ANY] + [VMEM] * (4 + len(keep)),
+        out_specs=(VMEM,) * 3,
         compiler_params=params(),
-        cost_estimate=cost(10**9, 2**20),
+        cost_estimate=cost(6 * 10**9, 2**20),
         name="far_fields",
-    )(order, coef, coup, *keep)
-
-
-def near_kernel(first, count, pos_ref, pairs_ref, order, inner, own, outer, tiles, *refs):
+    )(order, coef, coup, upper_trans, upper_coup, *keep)
+
+
+def near_kernel(first, count, pos_ref, pairs_ref, order, inner, own, outer, across, tiles, *refs):
     del order
     out_ref = refs[-1]
     dims = (((1,), (1,)), ((), ()))
     position = pos_ref[0]
+    row = lax.shift_right_logical(position, 3)
     for i in range(count):
         total = None
         for k in range(4):
@@ -242,35 +257,40 @@
             column = pl.ds(pl.multiple_of((leaf & 31) * 256, 256), 256)
             source = jnp.where(
                 holder == position, own[:, column],
-                jnp.where(holder == position ^ 1, inner[:, column], outer[:, column]),
+                jnp.where(
+                    holder == position ^ 1, inner[:, column],
+                    jnp.where(lax.shift_right_logical(holder, 3) == row, outer[:, column], across[:, column]),
+                ),
             )
             part = lax.dot_general(source, tiles[first + i, k], dims, preferred_element_type=F32)
             total = part if total is None else total + part
         out_ref[:, 256 * i : 256 * i + 256] = total
 
 
-def near_field(first, count, position, near_pairs_t, order, inner, own, outer, tiles, keep):
+def near_field(first, count, position, near_pairs_t, order, inner, own, outer, across, tiles, keep):
     return pl.pallas_call(
         functools.partial(near_kernel, first, count),
         out_shape=vmem((16, 256 * count), F32),
-        in_specs=[SMEM, SMEM, ANY] + [VMEM] * (4 + len(keep)),
+        in_specs=[SMEM, SMEM, ANY] + [VMEM] * (5 + len(keep)),
         out_specs=VMEM,
         compiler_params=params(),
         cost_estimate=cost(10**9, 2**20),
         name="near_field",
-    )(position, near_pairs_t, order, inner, own, outer, tiles, *keep)
+    )(position, near_pairs_t, order, inner, own, outer, across, tiles, *keep)
 
 
 def down_kernel(*refs):
     siblings = refs[:7]
-    upper_trans, upper_coup, far, trans, basis = refs[7:12]
+    high, low, far, trans, basis = refs[7:12]
     nearby = refs[12 : 12 + len(NEAR_CHUNKS)]
     out_ref = refs[12 + len(NEAR_CHUNKS)]
-    field = None
-    for level in range(6, -1, -1):
+    field = jnp.zeros((16, 64), F32)
+    for level in range(7):
         width = 64 * (7 - level)
-        term = times(siblings[level][:, width - 64 : width], upper_coup[level])
-        field = term if field is None else term + times_transposed(field, upper_trans[level])
+        value = siblings[level][:, width - 64 : width]
+        rows = slice(64 * (6 - level), 64 * (7 - level))
+        field += times(value, high[rows])
+        field += jnp.dot(value.astype(BF16), low[rows], preferred_element_type=F32)
     fields = [field]
     base = 31
     while len(fields) < 32:
@@ -294,7 +314,7 @@
             )
 
 
-def down_sweep(siblings, upper_trans, upper_coup, far, local_transfer, basis_t, nearby):
+def down_sweep(siblings, high, low, far, local_transfer, basis_t, nearby):
     return pl.pallas_call(
         down_kernel,
         out_shape=jax.ShapeDtypeStruct((16, 8192), F32),
@@ -303,17 +323,27 @@
         compiler_params=params(),
         cost_estimate=cost(3 * 10**9, 2**20),
         name="down_sweep",
-    )(*siblings, upper_trans, upper_coup, far, local_transfer, basis_t, *nearby)
+    )(*siblings, high, low, far, local_transfer, basis_t, *nearby)
+
+
+def onward(i, devices):
+    if i % 8 == 0:
+        return i + 8 if i + 8 < devices else i + 7
+    if i % 8 == 7:
+        return i - 8 if i >= 8 else i - 7
+    return i + 1 if i % 2 else i - 1
 
 
 def local(rhs, leaf_basis, near_tiles, near_pairs, local_transfer, local_coupling, upper_transfer, upper_coupling):
     devices = lax.axis_size("leaf")
     position = lax.axis_index("leaf").astype(jnp.int32)
     where = position.reshape(1)
-    last = devices - 1
-    outward = [(i, min(max(i + 2 * (i & 1) - 1, 0), last)) for i in range(devices)]
     inward = [(i, i ^ 1) for i in range(devices)]
+    outward = [(i, i // 8 * 8 + (i % 8 + 2 * (i % 2) - 1) % 8) for i in range(devices)]
+    rows = [(i, onward(i, devices)) for i in range(devices)]
     near_pairs_t = jnp.transpose(near_pairs, (1, 0))
+    outer = lax.ppermute(rhs, "leaf", outward)
+    inner = lax.ppermute(rhs, "leaf", inward)
     coef, path, upper_trans, own, basis, trans, upper_coup, coup = up_sweep(
         where,
         rhs,
@@ -323,8 +353,7 @@
         jnp.transpose(upper_coupling, (1, 2, 0)),
         local_coupling,
     )
-    outer = lax.ppermute(own, "leaf", outward)
-    inner = lax.ppermute(own, "leaf", inward)
+
     nearby = []
     siblings = []
     first = 0
@@ -336,19 +365,22 @@
             upper_coup = pick_couplings(where, path, upper_coup, [coef, coup, trans, basis])
             received, upper_coup = lax.optimization_barrier((received, upper_coup))
         elif level == 1:
-            far = far_fields(path, coef, coup, [trans, basis])
+            far, high, low = far_fields(path, coef, coup, upper_trans, upper_coup, [trans, basis])
             received, far = lax.optimization_barrier((received, far))
         else:
             count = NEAR_CHUNKS[level - 2]
             part = near_field(
-                first, count, where, near_pairs_t, path, inner, own, outer, near_tiles, [far, trans, basis]
+                first, count, where, near_pairs_t, path, inner, own, outer, across, near_tiles, [far, trans, basis, high, low]
             )
             first += count
             received, part = lax.optimization_barrier((received, part))
             nearby.append(part)
         siblings.append(received)
         path = path[:, : width - 64] + received[:, : width - 64]
-    return down_sweep(siblings, upper_trans, upper_coup, far, trans, basis, nearby)
+        if level == 0:
+            outer, path = lax.optimization_barrier((outer, path))
+            across = lax.ppermute(outer, "leaf", rows)
+    return down_sweep(siblings, high, low, far, trans, basis, nearby)
 
 
 def solution(mesh):

time: 41.1 us -> 37.4 us (0.910)
  starting transfers between devices: 22.8 us -> 17.2 us
  waiting for transfers between devices: 1.87 us -> 3.72 us
    ppermute x7, starting transfers between devices: 18 us -> 12.3 us  [local(): received = lax.ppermute(path, 'leaf', pairs)]
    ppermute x2 -> x3, waiting for transfers between devices: 0.01 us -> 2.67 us  [the longest x1 2.66 us: local(): across = lax.ppermute(outer, 'leaf', rows)]
    ppermute x7, waiting for transfers between devices: 1.87 us -> 1.05 us  [local(): received = lax.ppermute(path, 'leaf', pairs)]
    pallas_call x1, Pallas kernels: 0.53 us -> 1.26 us  [far_fields(): pl.pallas_call(far_kernel, out_shape=(vmem((31, 16, 128), F32), vmem((448...]
    pallas_call x1, Pallas kernels: 2.77 us -> 2.15 us  [down_sweep(): pl.pallas_call(down_kernel, out_shape=jax.ShapeDtypeStruct((16, 8192), F3...]
    ppermute x2 -> x3, starting transfers between devices: 4.86 us -> 4.94 us  [the longest x1 2.6 us: local(): outer = lax.ppermute(rhs, 'leaf', outward)]
  transfers between devices with their start and end apart: 9 -> 10, of which waited for: 3 -> 5; matrix products, arithmetic and copies ran while one was open for 0% -> 0% of each run, Pallas kernels for 22% -> 38%
where the time goes in v4:
time: 37.4 us; the launch traced here: 37.3 us
  starting transfers between devices  17.2 us (46%)
  Pallas kernels  16.1 us (43%)
  waiting for transfers between devices  3.72 us (10%)
    ppermute x7, starting transfers between devices, local(): received = lax.ppermute(path, 'leaf', pairs)  12.3 us
    pallas_call x5, Pallas kernels, near_field(): pl.pallas_call(functools.partial(near_kernel, first, count), out_shape=vm...  7.66 us
    pallas_call x1, Pallas kernels, up_sweep(): pl.pallas_call(up_kernel, out_shape=(vmem((31, 16, 128), F32), vmem((16,...  4.31 us
    ppermute x1, waiting for transfers between devices, local(): across = lax.ppermute(outer, 'leaf', rows)  2.66 us
    ppermute x1, starting transfers between devices, local(): outer = lax.ppermute(rhs, 'leaf', outward)  2.6 us
    pallas_call x1, Pallas kernels, down_sweep(): pl.pallas_call(down_kernel, out_shape=jax.ShapeDtypeStruct((16, 8192), F3...  2.15 us
    pallas_call x1, Pallas kernels, far_fields(): pl.pallas_call(far_kernel, out_shape=(vmem((31, 16, 128), F32), vmem((448...  1.26 us
    ppermute x1, starting transfers between devices, local(): across = lax.ppermute(outer, 'leaf', rows)  1.24 us
  transfers between devices with their start and end apart: 10, of which 5 were waited for; matrix products, arithmetic and copies ran while one was open for 0% of the time, Pallas kernels for 38%

profile of v4, /device:TPU:1, one launch (start us, length us, event | category | flops | bytes accessed | tf_op | source)
XLA Modules:
  0.0 37.3 jit_solution(4945924354856157586)
XLA Ops:
  0.0 2.6 %collective-permute-start.1 = (bf16[16,8192]{1,0:T(8,128)(2,1)}, bf16[16,8192]{1,0:T(8,128)(2,1)S(1)}, u32[]{:S(2)}, u32[]{:S(2)}) collective-permute-start(bf16[16,8192]{1,0:T(8,128)(2,1)} %rhs_hbm.1), channel_id=1, source_target_pairs={{0,7},{1,2},{2,1},{3,4},{4,3},{5,6},{6,5},{7,0},{8,15},{9,10},{10,... | collective-permute-start | bytes 786440 | tf_op jit(solution)/shard_map/ppermute | solution.py:345
  2.6 1.1 %collective-permute-start.4 = (bf16[16,8192]{1,0:T(8,128)(2,1)}, bf16[16,8192]{1,0:T(8,128)(2,1)S(1)}, u32[]{:S(2)}, u32[]{:S(2)}) collective-permute-start(bf16[16,8192]{1,0:T(8,128)(2,1)} %rhs_hbm.1), channel_id=1, source_target_pairs={{0,1},{1,0},{2,3},{3,2},{4,5},{5,4},{6,7},{7,6},{8,9},{9,8},{10,11... | collective-permute-start | bytes 786440 | tf_op jit(solution)/shard_map/ppermute | solution.py:346
  3.7 4.3 %up_sweep.1 = (f32[31,16,128]{2,1,0:T(8,128)S(1)}, f32[16,448]{1,0:T(8,128)S(1)}, bf16[6,64,64]{2,1,0:T(8,128)(2,1)S(1)}, bf16[16,8192]{1,0:T(8,128)(2,1)S(1)}, ...) custom-call(s32[1]{0:T(128)} %bitcast.pos_ref, ...), custom_call_target="tpu_custom_call" | custom-call | flops 4000000000 | bytes 1048576 | tf_op jit(solution)/shard_map/up_sweep/pallas_call | solution.py:167
  8.0 0.1 collective-permute-start
  8.1 0.8 %pick_couplings.1.upper_coup = bf16[7,64,64]{2,1,0:T(8,128)(2,1)S(1)} custom-call(s32[1]{0:T(128)} %bitcast.pos_ref, f32[16,448]{1,0:T(8,128)S(1)} %get-tuple-element.32.order, bf16[64,64,254]{2,1,0:T(8,128)(2,1)S(1)} %get-tuple-element.33.upper, f32[31,16,128]{2,1,0:T(8,128)S(1)} %get-tuple-element.34.refs_0_.coef, ...), custom_call_target="tpu_custom_call" | custom-call | flops 6000000000 | bytes 1048576 | tf_op jit(solution)/shard_map/pick_couplings/pallas_call | solution.py:206
  8.9 0.4 %collective-permute-done.refs_0_ = f32[16,448]{1,0:T(8,128)S(1)} collective-permute-done((f32[16,448]{1,0:T(8,128)S(1)}, f32[16,448]{1,0:T(8,128)S(1)}, u32[]{:S(2)}, u32[]{:S(2)}) %collective-permute-start) | collective-permute-done | bytes 28704 | tf_op jit(solution)/shard_map/ppermute | solution.py:363
  9.3 0.6 %collective-permute-start.2 = (f32[16,384]{1,0:T(8,128)S(1)}, f32[16,384]{1,0:T(8,128)S(1)}, u32[]{:S(2)}, u32[]{:S(2)}) collective-permute-start(f32[16,384]{1,0:T(8,128)S(1)} %slice_add_fusion.1.order), channel_id=1, source_target_pairs={{0,3},{1,2},{2,1},{3,0},{4,7},{5,6},{6,5},{7,4},{8,11},{9,10},{10,... | collective-permute-start | bytes 73736 | tf_op jit(solution)/shard_map/ppermute | solution.py:363
  9.9 1.2 %collective-permute-start.5 = (bf16[16,8192]{1,0:T(8,128)(2,1)S(1)}, bf16[16,8192]{1,0:T(8,128)(2,1)S(1)}, u32[]{:S(2)}, u32[]{:S(2)}) collective-permute-start(bf16[16,8192]{1,0:T(8,128)(2,1)S(1)} %collective-permute-done.1.outer), channel_id=1, source_target_pairs={{0,8},{1,2},{2,1},{3,4},{4,3},{5,6},{6,5},{7,0},{8,16},{9,10},{10,... | collective-permute-start | bytes 786440 | tf_op jit(solution)/shard_map/ppermute | solution.py:382
  11.2 1.3 %far_fields.1 = (f32[31,16,128]{2,1,0:T(8,128)S(1)}, bf16[448,64]{1,0:T(8,128)(2,1)S(1)}, bf16[448,64]{1,0:T(8,128)(2,1)S(1)}) custom-call(f32[16,384]{1,0:T(8,128)S(1)} %slice_add_fusion.1.order, f32[31,16,128]{2,1,0:T(8,128)S(1)} %get-tuple-element.34.refs_0_.coef, bf16[62,64,64]{2,1,0:T(8,128)(2,1)S(1)} %get-tuple-element.35.refs_1_.coup, ...), custom_call_target="tpu_custom_call" | custom-call | flops 6000000000 | bytes 1048576 | tf_op jit(solution)/shard_map/far_fields/pallas_call | solution.py:235
  12.4 0.2 collective-permute-done.2.refs_1_
  12.7 0.7 %collective-permute-start.3 = (f32[16,320]{1,0:T(8,128)S(1)}, f32[16,320]{1,0:T(8,128)S(1)}, u32[]{:S(2)}, u32[]{:S(2)}) collective-permute-start(f32[16,320]{1,0:T(8,128)S(1)} %slice_add_fusion.order), channel_id=1, source_target_pairs={{0,7},{1,6},{2,5},{3,4},{4,3},{5,2},{6,1},{7,0},{8,15},{9,14},{10,... | collective-permute-start | bytes 61448 | tf_op jit(solution)/shard_map/ppermute | solution.py:363
  13.3 2.7 %collective-permute-done.5.across = bf16[16,8192]{1,0:T(8,128)(2,1)S(1)} collective-permute-done((bf16[16,8192]{1,0:T(8,128)(2,1)S(1)}, bf16[16,8192]{1,0:T(8,128)(2,1)S(1)}, u32[]{:S(2)}, u32[]{:S(2)}) %collective-permute-start.5) | collective-permute-done | bytes 262176 | tf_op jit(solution)/shard_map/ppermute | solution.py:382
  16.0 1.5 %near_field.5.refs_12_ = f32[16,1536]{1,0:T(8,128)S(1)} custom-call(s32[1]{0:T(128)} %bitcast.pos_ref, s32[4,32]{1,0:T(4,128)S(1)} %bitcast.7, f32[16,320]{1,0:T(8,128)S(1)} %slice_add_fusion.order, bf16[16,8192]{1,0:T(8,128)(2,1)S(1)} %collective-permute-done.4.inner, bf16[16,8192]{1,0:T(8,128)(2,1)S(1)} %get-tuple-element.44.own, ...), custom_call_target="tpu_custom_call" | custom-call | flops 1000000000 | bytes 1048576 | tf_op jit(solution)/shard_map/near_field/pallas_call | solution.py:271
  17.5 0.2 collective-permute-done.3.refs_2_
  17.7 1.9 %collective-permute-start.6 = (f32[16,256]{1,0:T(8,128)S(1)}, f32[16,256]{1,0:T(8,128)S(1)}, u32[]{:S(2)}, u32[]{:S(2)}) collective-permute-start(f32[16,256]{1,0:T(8,128)S(1)} %slice_add_fusion.3.order), channel_id=1, source_target_pairs={{0,9},{1,8},{2,11},{3,10},{4,13},{5,12},{6,15},{7,14},{8,1},{9,0},... | collective-permute-start | bytes 49160 | tf_op jit(solution)/shard_map/ppermute | solution.py:363
  19.6 1.5 %near_field.6.refs_13_ = f32[16,1536]{1,0:T(8,128)S(1)} custom-call(s32[1]{0:T(128)} %bitcast.pos_ref, s32[4,32]{1,0:T(4,128)S(1)} %bitcast.8, f32[16,256]{1,0:T(8,128)S(1)} %slice_add_fusion.3.order, bf16[16,8192]{1,0:T(8,128)(2,1)S(1)} %collective-permute-done.4.inner, bf16[16,8192]{1,0:T(8,128)(2,1)S(1)} %get-tuple-element.44.own, ...), custom_call_target="tpu_custom_call" | custom-call | flops 1000000000 | bytes 1048576 | tf_op jit(solution)/shard_map/near_field/pallas_call | solution.py:271
  21.1 0.3 collective-permute-done.6.refs_3_
  21.3 3.5 %collective-permute-start.7 = (f32[16,192]{1,0:T(8,128)S(1)}, f32[16,192]{1,0:T(8,128)S(1)}, u32[]{:S(2)}, u32[]{:S(2)}) collective-permute-start(f32[16,192]{1,0:T(8,128)S(1)} %slice_add_fusion.2.order), channel_id=1, source_target_pairs={{0,25},{1,24},{2,27},{3,26},{4,29},{5,28},{6,31},{7,30},{8,17},{9,... | collective-permute-start | bytes 36872 | tf_op jit(solution)/shard_map/ppermute | solution.py:363
  24.9 1.5 %near_field.7.refs_14_ = f32[16,1536]{1,0:T(8,128)S(1)} custom-call(s32[1]{0:T(128)} %bitcast.pos_ref, s32[4,32]{1,0:T(4,128)S(1)} %bitcast.9, f32[16,192]{1,0:T(8,128)S(1)} %slice_add_fusion.2.order, bf16[16,8192]{1,0:T(8,128)(2,1)S(1)} %collective-permute-done.4.inner, bf16[16,8192]{1,0:T(8,128)(2,1)S(1)} %get-tuple-element.44.own, ...), custom_call_target="tpu_custom_call" | custom-call | flops 1000000000 | bytes 1048576 | tf_op jit(solution)/shard_map/near_field/pallas_call | solution.py:271
  26.4 2.5 %collective-permute-start.8 = (f32[16,128]{1,0:T(8,128)S(1)}, f32[16,128]{1,0:T(8,128)S(1)}, u32[]{:S(2)}, u32[]{:S(2)}) collective-permute-start(f32[16,128]{1,0:T(8,128)S(1)} %slice_add_fusion.5.order), channel_id=1, source_target_pairs={{0,33},{1,32},{2,35},{3,34},{4,37},{5,36},{6,39},{7,38},{8,41},{9,... | collective-permute-start | bytes 24584 | tf_op jit(solution)/shard_map/ppermute | solution.py:363
  28.9 1.6 %near_field.8.refs_15_ = f32[16,1792]{1,0:T(8,128)S(1)} custom-call(s32[1]{0:T(128)} %bitcast.pos_ref, s32[4,32]{1,0:T(4,128)S(1)} %bitcast.10, f32[16,128]{1,0:T(8,128)S(1)} %slice_add_fusion.5.order, bf16[16,8192]{1,0:T(8,128)(2,1)S(1)} %collective-permute-done.4.inner, bf16[16,8192]{1,0:T(8,128)(2,1)S(1)} %get-tuple-element.44.own, ...), custom_call_target="tpu_custom_call" | custom-call | flops 1000000000 | bytes 1048576 | tf_op jit(solution)/shard_map/near_field/pallas_call | solution.py:271
  30.5 3.0 %collective-permute-start.9 = (f32[16,64]{1,0:T(8,128)S(1)}, f32[16,64]{1,0:T(8,128)S(1)}, u32[]{:S(2)}, u32[]{:S(2)}) collective-permute-start(f32[16,64]{1,0:T(8,128)S(1)} %slice_add_fusion.4.order), channel_id=1, source_target_pairs={{0,97},{1,96},{2,99},{3,98},{4,101},{5,100},{6,103},{7,102},{8,105... | collective-permute-start | bytes 12296 | tf_op jit(solution)/shard_map/ppermute | solution.py:363
  33.5 1.6 %near_field.9.refs_16_ = f32[16,1792]{1,0:T(8,128)S(1)} custom-call(s32[1]{0:T(128)} %bitcast.pos_ref, s32[4,32]{1,0:T(4,128)S(1)} %bitcast.11, f32[16,64]{1,0:T(8,128)S(1)} %slice_add_fusion.4.order, bf16[16,8192]{1,0:T(8,128)(2,1)S(1)} %collective-permute-done.4.inner, bf16[16,8192]{1,0:T(8,128)(2,1)S(1)} %get-tuple-element.44.own, ...), custom_call_target="tpu_custom_call" | custom-call | flops 1000000000 | bytes 1048576 | tf_op jit(solution)/shard_map/near_field/pallas_call | solution.py:271
  35.1 2.2 %down_sweep.1 = f32[16,8192]{1,0:T(8,128)} custom-call(f32[16,448]{1,0:T(8,128)S(1)} %collective-permute-done.refs_0_, f32[16,384]{1,0:T(8,128)S(1)} %collective-permute-done.2.refs_1_, f32[16,320]{1,0:T(8,128)S(1)} %collective-permute-done.3.refs_2_, f32[16,256]{1,0:T(8,128)S(1)} %collective-permute-done.6.refs_3_, ...), custom_call_target="tpu_custom_call" | custom-call | flops 3000000000 | bytes 1048576 | tf_op jit(solution)/shard_map/down_sweep/pallas_call | solution.py:318
  (22 shorter events, 0.1 us)
Async XLA Ops:
  0.0 9.3 %collective-permute-start.1 = (bf16[16,8192]{1,0:T(8,128)(2,1)}, bf16[16,8192]{1,0:T(8,128)(2,1)S(1)}, u32[]{:S(2)}, u32[]{:S(2)}) collective-permute-start(bf16[16,8192]{1,0:T(8,128)(2,1)} %rhs_hbm.1), channel_id=1, source_target_pairs={{0,7},{1,2},{2,1},{3,4},{4,3},{5,6},{6,5},{7,0},{8,15},{9,10},{10,... | collective-permute-start | bytes 786440 | tf_op jit(solution)/shard_map/ppermute | solution.py:345
  2.6 10.7 %collective-permute-start.4 = (bf16[16,8192]{1,0:T(8,128)(2,1)}, bf16[16,8192]{1,0:T(8,128)(2,1)S(1)}, u32[]{:S(2)}, u32[]{:S(2)}) collective-permute-start(bf16[16,8192]{1,0:T(8,128)(2,1)} %rhs_hbm.1), channel_id=1, source_target_pairs={{0,1},{1,0},{2,3},{3,2},{4,5},{5,4},{6,7},{7,6},{8,9},{9,8},{10,11... | collective-permute-start | bytes 786440 | tf_op jit(solution)/shard_map/ppermute | solution.py:346
  8.0 1.3 %collective-permute-start = (f32[16,448]{1,0:T(8,128)S(1)}, f32[16,448]{1,0:T(8,128)S(1)}, u32[]{:S(2)}, u32[]{:S(2)}) collective-permute-start(f32[16,448]{1,0:T(8,128)S(1)} %get-tuple-element.32.order), channel_id=1, source_target_pairs={{0,1},{1,0},{2,3},{3,2},{4,5},{5,4},{6,7},{7,6},{8,9},{9,8},{10,11... | collective-permute-start | bytes 86024 | tf_op jit(solution)/shard_map/ppermute | solution.py:363
  8.1 7.9 %slice-start = ((s8[16777216]{0:T(1024)(128)(4,1)}), s8[4194304]{0:T(1024)(128)(4,1)S(1)}, s32[]{:S(2)}) async-start(s8[16777216]{0:T(1024)(128)(4,1)} %bitcast.5), calls=%async_computation | async-start | bytes 8388608
  8.1 7.9 %slice-start.1 = ((s8[16777216]{0:T(1024)(128)(4,1)}), s8[4194304]{0:T(1024)(128)(4,1)S(1)}, s32[]{:S(2)}) async-start(s8[16777216]{0:T(1024)(128)(4,1)} %bitcast.5), calls=%async_computation.1 | async-start | bytes 8388608
  9.3 3.3 %collective-permute-start.2 = (f32[16,384]{1,0:T(8,128)S(1)}, f32[16,384]{1,0:T(8,128)S(1)}, u32[]{:S(2)}, u32[]{:S(2)}) collective-permute-start(f32[16,384]{1,0:T(8,128)S(1)} %slice_add_fusion.1.order), channel_id=1, source_target_pairs={{0,3},{1,2},{2,1},{3,0},{4,7},{5,6},{6,5},{7,4},{8,11},{9,10},{10,... | collective-permute-start | bytes 73736 | tf_op jit(solution)/shard_map/ppermute | solution.py:363
  9.9 6.1 %collective-permute-start.5 = (bf16[16,8192]{1,0:T(8,128)(2,1)S(1)}, bf16[16,8192]{1,0:T(8,128)(2,1)S(1)}, u32[]{:S(2)}, u32[]{:S(2)}) collective-permute-start(bf16[16,8192]{1,0:T(8,128)(2,1)S(1)} %collective-permute-done.1.outer), channel_id=1, source_target_pairs={{0,8},{1,2},{2,1},{3,4},{4,3},{5,6},{6,5},{7,0},{8,16},{9,10},{10,... | collective-permute-start | bytes 786440 | tf_op jit(solution)/shard_map/ppermute | solution.py:382
  11.1 4.9 %slice-start.2 = ((s8[16777216]{0:T(1024)(128)(4,1)}), s8[4194304]{0:T(1024)(128)(4,1)S(1)}, s32[]{:S(2)}) async-start(s8[16777216]{0:T(1024)(128)(4,1)} %bitcast.5), calls=%async_computation.2 | async-start | bytes 8388608
  11.1 4.9 %slice-start.3 = ((s8[16777216]{0:T(1024)(128)(4,1)}), s8[4194304]{0:T(1024)(128)(4,1)S(1)}, s32[]{:S(2)}) async-start(s8[16777216]{0:T(1024)(128)(4,1)} %bitcast.5), calls=%async_computation.3 | async-start | bytes 8388608
  11.2 4.9 %copy-start = (s32[32,4]{0,1:T(4,128)S(1)}, s32[32,4]{0,1:T(4,128)}, u32[]{:S(2)}) copy-start(s32[32,4]{0,1:T(4,128)} %param.11) | copy-start | bytes 1540
  12.7 5.0 %collective-permute-start.3 = (f32[16,320]{1,0:T(8,128)S(1)}, f32[16,320]{1,0:T(8,128)S(1)}, u32[]{:S(2)}, u32[]{:S(2)}) collective-permute-start(f32[16,320]{1,0:T(8,128)S(1)} %slice_add_fusion.order), channel_id=1, source_target_pairs={{0,7},{1,6},{2,5},{3,4},{4,3},{5,2},{6,1},{7,0},{8,15},{9,14},{10,... | collective-permute-start | bytes 61448 | tf_op jit(solution)/shard_map/ppermute | solution.py:363
  17.7 3.6 %collective-permute-start.6 = (f32[16,256]{1,0:T(8,128)S(1)}, f32[16,256]{1,0:T(8,128)S(1)}, u32[]{:S(2)}, u32[]{:S(2)}) collective-permute-start(f32[16,256]{1,0:T(8,128)S(1)} %slice_add_fusion.3.order), channel_id=1, source_target_pairs={{0,9},{1,8},{2,11},{3,10},{4,13},{5,12},{6,15},{7,14},{8,1},{9,0},... | collective-permute-start | bytes 49160 | tf_op jit(solution)/shard_map/ppermute | solution.py:363
  21.3 5.0 %collective-permute-start.7 = (f32[16,192]{1,0:T(8,128)S(1)}, f32[16,192]{1,0:T(8,128)S(1)}, u32[]{:S(2)}, u32[]{:S(2)}) collective-permute-start(f32[16,192]{1,0:T(8,128)S(1)} %slice_add_fusion.2.order), channel_id=1, source_target_pairs={{0,25},{1,24},{2,27},{3,26},{4,29},{5,28},{6,31},{7,30},{8,17},{9,... | collective-permute-start | bytes 36872 | tf_op jit(solution)/shard_map/ppermute | solution.py:363
  26.4 4.1 %collective-permute-start.8 = (f32[16,128]{1,0:T(8,128)S(1)}, f32[16,128]{1,0:T(8,128)S(1)}, u32[]{:S(2)}, u32[]{:S(2)}) collective-permute-start(f32[16,128]{1,0:T(8,128)S(1)} %slice_add_fusion.5.order), channel_id=1, source_target_pairs={{0,33},{1,32},{2,35},{3,34},{4,37},{5,36},{6,39},{7,38},{8,41},{9,... | collective-permute-start | bytes 24584 | tf_op jit(solution)/shard_map/ppermute | solution.py:363
  30.5 4.6 %collective-permute-start.9 = (f32[16,64]{1,0:T(8,128)S(1)}, f32[16,64]{1,0:T(8,128)S(1)}, u32[]{:S(2)}, u32[]{:S(2)}) collective-permute-start(f32[16,64]{1,0:T(8,128)S(1)} %slice_add_fusion.4.order), channel_id=1, source_target_pairs={{0,97},{1,96},{2,99},{3,98},{4,101},{5,100},{6,103},{7,102},{8,105... | collective-permute-start | bytes 12296 | tf_op jit(solution)/shard_map/ppermute | solution.py:363

commit v5 on v4

--- a/solution.py
+++ b/solution.py
@@ -13,7 +13,8 @@
 VMEM = pl.BlockSpec(memory_space=pltpu.VMEM)
 HBM = pl.BlockSpec(memory_space=pltpu.HBM)
 SMEM = pl.BlockSpec(memory_space=pltpu.SMEM)
-NEAR_CHUNKS = (6, 6, 6, 7, 7)
+NEAR_CHUNKS = (8, 8, 8, 8)
+FAR_LEVEL = 2
 MASKS = (1, 3, 7, 9, 25, 33, 97)
 
 
@@ -86,11 +87,26 @@
     return vmem((count,) + tiles.shape[1:], tiles.dtype)
 
 
-def start_all(pairs, sems):
-    copies = [pltpu.make_async_copy(source, target, sems.at[i]) for i, (source, target) in enumerate(pairs)]
-    for copy in copies:
-        copy.start()
-    return copies
+def start_pieces(pairs, sems):
+    started = []
+    at = 0
+    for source, target, pieces in pairs:
+        size = source.shape[0] // pieces
+        group = []
+        for i in range(pieces):
+            span = slice(size * i, size * (i + 1) if i + 1 < pieces else source.shape[0])
+            group.append(pltpu.make_async_copy(source.at[span], target.at[span], sems.at[at]))
+            at += 1
+        for copy in group:
+            copy.start()
+        started.append(group)
+    return started
+
+
+def finish(groups):
+    for group in groups:
+        for copy in group:
+            copy.wait()
 
 
 def params():
@@ -101,24 +117,21 @@
     return pl.CostEstimate(flops=flops, bytes_accessed=size, transcendentals=0)
 
 
-def up_kernel(pos_ref, rhs_hbm, basis_hbm, trans_hbm, upper_hbm, upper_coup_hbm, coup_hbm,
-              coef_ref, path_ref, upper_ref, rhs, basis, trans, upper_coup, coup,
+def up_kernel(rhs_hbm, basis_hbm, trans_hbm, upper_hbm,
+              coef_ref, path_ref, upper_ref, rhs, basis, trans,
               upper, picked, high, low, sems):
-    copies = start_all(
+    copies = start_pieces(
         [
-            (upper_hbm, upper),
-            (rhs_hbm, rhs),
-            (basis_hbm, basis),
-            (trans_hbm, trans),
-            (upper_coup_hbm, upper_coup),
-            (coup_hbm, coup),
+            (upper_hbm, upper, 8),
+            (rhs_hbm, rhs, 1),
+            (basis_hbm, basis, 4),
+            (trans_hbm, trans, 4),
         ],
         sems,
     )
-    copies[0].wait()
-    pick_nodes(pos_ref[0], upper, picked)
-    for copy in copies[1:4]:
-        copy.wait()
+    finish(copies[:1])
+    pick_nodes(lax.axis_index("leaf"), upper, picked)
+    finish(copies[1:4])
     maps = None
     for level in range(6):
         matrix = picked[64 * level : 64 * level + 64, 0:64].astype(BF16)
@@ -159,11 +172,9 @@
     path_ref[:, 0:384] = times(root, high[...]) + jnp.dot(
         root.astype(BF16), low[...], preferred_element_type=F32
     )
-    for copy in copies[4:]:
-        copy.wait()
-
-
-def up_sweep(position, rhs, basis_t, local_transfer, upper_transfer_t, upper_coupling_t, local_coupling):
+
+
+def up_sweep(rhs, basis_t, local_transfer, upper_transfer_t):
     return pl.pallas_call(
         up_kernel,
         out_shape=(
@@ -173,46 +184,43 @@
             vmem_like(rhs),
             vmem_like(basis_t),
             vmem_like(local_transfer),
-            vmem_like(upper_coupling_t),
-            vmem_like(local_coupling),
         ),
-        in_specs=[SMEM] + [HBM] * 6,
-        out_specs=(VMEM,) * 8,
+        in_specs=[HBM] * 4,
+        out_specs=(VMEM,) * 6,
         scratch_shapes=[
             pltpu.VMEM(upper_transfer_t.shape, BF16),
             pltpu.VMEM((512, 128), F32),
             pltpu.VMEM((64, 384), BF16),
             pltpu.VMEM((64, 384), BF16),
-            pltpu.SemaphoreType.DMA((6,)),
+            pltpu.SemaphoreType.DMA((17,)),
         ],
         compiler_params=params(),
         cost_estimate=cost(4 * 10**9, 2**20),
         name="up_sweep",
     )(
-        position,
-        *in_hbm(rhs, basis_t, local_transfer, upper_transfer_t, upper_coupling_t, local_coupling),
-    )
-
-
-def pick_kernel(pos_ref, order, upper, *refs):
+        *in_hbm(rhs, basis_t, local_transfer, upper_transfer_t),
+    )
+
+
+def pick_kernel(order, upper, *refs):
     del order
     upper_ref, picked = refs[-2:]
-    pick_nodes(pos_ref[0], upper, picked)
+    pick_nodes(lax.axis_index("leaf"), upper, picked)
     for level in range(7):
         upper_ref[level] = picked[64 * level : 64 * level + 64, 0:64].astype(BF16)
 
 
-def pick_couplings(position, order, upper_coupling_t, keep):
+def pick_couplings(order, upper_coupling_t, keep):
     return pl.pallas_call(
         pick_kernel,
         out_shape=vmem((7, 64, 64), BF16),
-        in_specs=[SMEM, ANY, VMEM] + [VMEM] * len(keep),
+        in_specs=[ANY, VMEM] + [VMEM] * len(keep),
         out_specs=VMEM,
         scratch_shapes=[pltpu.VMEM((512, 128), F32)],
         compiler_params=params(),
         cost_estimate=cost(6 * 10**9, 2**20),
         name="pick_couplings",
-    )(position, order, upper_coupling_t, *keep)
+    )(order, upper_coupling_t, *keep)
 
 
 def far_kernel(order, coef, coup, upper_trans, upper_coup, *refs):
@@ -243,11 +251,11 @@
     )(order, coef, coup, upper_trans, upper_coup, *keep)
 
 
-def near_kernel(first, count, pos_ref, pairs_ref, order, inner, own, outer, across, tiles, *refs):
+def near_kernel(first, count, pairs_ref, order, inner, own, outer, across, tiles, *refs):
     del order
     out_ref = refs[-1]
     dims = (((1,), (1,)), ((), ()))
-    position = pos_ref[0]
+    position = lax.axis_index("leaf")
     row = lax.shift_right_logical(position, 3)
     for i in range(count):
         total = None
@@ -267,23 +275,23 @@
         out_ref[:, 256 * i : 256 * i + 256] = total
 
 
-def near_field(first, count, position, near_pairs_t, order, inner, own, outer, across, tiles, keep):
+def near_field(first, count, near_pairs_t, order, inner, own, outer, across, tiles, keep):
     return pl.pallas_call(
         functools.partial(near_kernel, first, count),
         out_shape=vmem((16, 256 * count), F32),
-        in_specs=[SMEM, SMEM, ANY] + [VMEM] * (5 + len(keep)),
+        in_specs=[SMEM, ANY] + [VMEM] * (5 + len(keep)),
         out_specs=VMEM,
         compiler_params=params(),
         cost_estimate=cost(10**9, 2**20),
         name="near_field",
-    )(position, near_pairs_t, order, inner, own, outer, across, tiles, *keep)
+    )(near_pairs_t, order, inner, own, outer, across, tiles, *keep)
 
 
 def down_kernel(*refs):
     siblings = refs[:7]
     high, low, far, trans, basis = refs[7:12]
     nearby = refs[12 : 12 + len(NEAR_CHUNKS)]
-    out_ref = refs[12 + len(NEAR_CHUNKS)]
+    out_hbm, out_ref, sems = refs[12 + len(NEAR_CHUNKS) :]
     field = jnp.zeros((16, 64), F32)
     for level in range(7):
         width = 64 * (7 - level)
@@ -305,6 +313,7 @@
         for pair in pairs:
             fields += [pair[:, 0:64], pair[:, 64:128]]
     places = [(box, i) for box, count in enumerate(NEAR_CHUNKS) for i in range(count)]
+    copies = []
     for leaf in range(0, 32, 2):
         both = times(apart(pairs[leaf // 2]), basis[leaf : leaf + 2].reshape(128, 256))
         for j in range(2):
@@ -312,6 +321,12 @@
             out_ref[:, 256 * (leaf + j) : 256 * (leaf + j) + 256] = (
                 both[16 * j : 16 * j + 16] + nearby[box][:, 256 * i : 256 * i + 256]
             )
+        if leaf % 8 == 6:
+            lanes = pl.ds(256 * (leaf - 6), 2048)
+            copies.append(pltpu.make_async_copy(out_ref.at[:, lanes], out_hbm.at[:, lanes], sems.at[leaf // 8]))
+            copies[-1].start()
+    for copy in copies:
+        copy.wait()
 
 
 def down_sweep(siblings, high, low, far, local_transfer, basis_t, nearby):
@@ -319,7 +334,8 @@
         down_kernel,
         out_shape=jax.ShapeDtypeStruct((16, 8192), F32),
         in_specs=[VMEM] * (12 + len(nearby)),
-        out_specs=VMEM,
+        out_specs=HBM,
+        scratch_shapes=[pltpu.VMEM((16, 8192), F32), pltpu.SemaphoreType.DMA((4,))],
         compiler_params=params(),
         cost_estimate=cost(3 * 10**9, 2**20),
         name="down_sweep",
@@ -336,23 +352,20 @@
 
 def local(rhs, leaf_basis, near_tiles, near_pairs, local_transfer, local_coupling, upper_transfer, upper_coupling):
     devices = lax.axis_size("leaf")
-    position = lax.axis_index("leaf").astype(jnp.int32)
-    where = position.reshape(1)
     inward = [(i, i ^ 1) for i in range(devices)]
     outward = [(i, i // 8 * 8 + (i % 8 + 2 * (i % 2) - 1) % 8) for i in range(devices)]
     rows = [(i, onward(i, devices)) for i in range(devices)]
     near_pairs_t = jnp.transpose(near_pairs, (1, 0))
     outer = lax.ppermute(rhs, "leaf", outward)
     inner = lax.ppermute(rhs, "leaf", inward)
-    coef, path, upper_trans, own, basis, trans, upper_coup, coup = up_sweep(
-        where,
+    coef, path, upper_trans, own, basis, trans = up_sweep(
         rhs,
         jnp.transpose(leaf_basis, (0, 2, 1)),
         local_transfer,
         jnp.transpose(upper_transfer, (1, 2, 0)),
-        jnp.transpose(upper_coupling, (1, 2, 0)),
-        local_coupling,
-    )
+    )
+    upper_coup = jnp.transpose(upper_coupling, (1, 2, 0))
+    coup = local_coupling
 
     nearby = []
     siblings = []
@@ -361,16 +374,16 @@
         width = 64 * (7 - level)
         pairs = [(i, i ^ MASKS[level]) for i in range(devices)]
         received = lax.ppermute(path, "leaf", pairs)
-        if level == 0:
-            upper_coup = pick_couplings(where, path, upper_coup, [coef, coup, trans, basis])
+        if level == 1:
+            upper_coup = pick_couplings(path, upper_coup, [coef, trans, basis])
             received, upper_coup = lax.optimization_barrier((received, upper_coup))
-        elif level == 1:
+        elif level == FAR_LEVEL:
             far, high, low = far_fields(path, coef, coup, upper_trans, upper_coup, [trans, basis])
             received, far = lax.optimization_barrier((received, far))
-        else:
-            count = NEAR_CHUNKS[level - 2]
+        elif level > FAR_LEVEL:
+            count = NEAR_CHUNKS[level - FAR_LEVEL - 1]
             part = near_field(
-                first, count, where, near_pairs_t, path, inner, own, outer, across, near_tiles, [far, trans, basis, high, low]
+                first, count, near_pairs_t, path, inner, own, outer, across, near_tiles, [far, trans, basis, high, low]
             )
             first += count
             received, part = lax.optimization_barrier((received, part))

time: 37.4 us -> 35.7 us (0.955)
  starting transfers between devices: 17.2 us -> 16 us
  Pallas kernels: 16.1 us -> 15.6 us
    ppermute x7, waiting for transfers between devices: 1.05 us -> 3.91 us  [local(): received = lax.ppermute(path, 'leaf', pairs)]
    ppermute x1, waiting for transfers between devices: 2.66 us -> 0.01 us  [local(): across = lax.ppermute(outer, 'leaf', rows)]
    ppermute x1, starting transfers between devices: 1.1 us -> 0.1 us  [local(): inner = lax.ppermute(rhs, 'leaf', inward)]
    pallas_call x5 -> x4, Pallas kernels: 7.66 us -> 7 us  [near_field(): pl.pallas_call(functools.partial(near_kernel, first, count), out_shape=vm...]
  transfers between devices with their start and end apart: 10 -> 10, of which waited for: 5 -> 3; matrix products, arithmetic and copies ran while one was open for 0% -> 0% of each run, Pallas kernels for 38% -> 38%
where the time goes in v5:
time: 35.7 us; the launch traced here: 35.6 us
  starting transfers between devices  16 us (45%)
  Pallas kernels  15.6 us (44%)
  waiting for transfers between devices  3.92 us (11%)
    ppermute x7, starting transfers between devices, local(): received = lax.ppermute(path, 'leaf', pairs)  12 us
    pallas_call x4, Pallas kernels, near_field(): pl.pallas_call(functools.partial(near_kernel, first, count), out_shape=vm...  7 us
    pallas_call x1, Pallas kernels, up_sweep(): pl.pallas_call(up_kernel, out_shape=(vmem((31, 16, 128), F32), vmem((16,...  4.47 us
    ppermute x7, waiting for transfers between devices, local(): received = lax.ppermute(path, 'leaf', pairs)  3.91 us
    ppermute x1, starting transfers between devices, local(): outer = lax.ppermute(rhs, 'leaf', outward)  2.6 us
    pallas_call x1, Pallas kernels, down_sweep(): pl.pallas_call(down_kernel, out_shape=jax.ShapeDtypeStruct((16, 8192), F3...  2.08 us
    pallas_call x1, Pallas kernels, far_fields(): pl.pallas_call(far_kernel, out_shape=(vmem((31, 16, 128), F32), vmem((448...  1.26 us
    ppermute x1, starting transfers between devices, local(): across = lax.ppermute(outer, 'leaf', rows)  1.24 us
  transfers between devices with their start and end apart: 10, of which 3 were waited for; matrix products, arithmetic and copies ran while one was open for 0% of the time, Pallas kernels for 38%

profile of v5, /device:TPU:1, one launch (start us, length us, event | category | flops | bytes accessed | tf_op | source)
XLA Modules:
  0.0 35.6 jit_solution(9633033727785822722)
XLA Ops:
  0.0 2.6 %collective-permute-start.1 = (bf16[16,8192]{1,0:T(8,128)(2,1)}, bf16[16,8192]{1,0:T(8,128)(2,1)S(1)}, u32[]{:S(2)}, u32[]{:S(2)}) collective-permute-start(bf16[16,8192]{1,0:T(8,128)(2,1)} %rhs_hbm.1), channel_id=1, source_target_pairs={{0,7},{1,2},{2,1},{3,4},{4,3},{5,6},{6,5},{7,0},{8,15},{9,10},{10,... | collective-permute-start | bytes 786440 | tf_op jit(solution)/shard_map/ppermute | solution.py:359
  2.6 4.5 %up_sweep.1 = (f32[31,16,128]{2,1,0:T(8,128)S(1)}, f32[16,448]{1,0:T(8,128)S(1)}, bf16[6,64,64]{2,1,0:T(8,128)(2,1)S(1)}, bf16[16,8192]{1,0:T(8,128)(2,1)S(1)}, ...) custom-call(bf16[16,8192]{1,0:T(8,128)(2,1)} %rhs_hbm.1, bf16[32,64,256]{2,1,0:T(8,128)(2,1)} %bitcast.12, ...), custom_call_target="tpu_custom_call" | custom-call | flops 4000000000 | bytes 1048576 | tf_op jit(solution)/shard_map/up_sweep/pallas_call | solution.py:178
  7.1 1.2 %collective-permute-start = (f32[16,448]{1,0:T(8,128)S(1)}, f32[16,448]{1,0:T(8,128)S(1)}, u32[]{:S(2)}, u32[]{:S(2)}) collective-permute-start(f32[16,448]{1,0:T(8,128)S(1)} %get-tuple-element.28), channel_id=1, source_target_pairs={{0,1},{1,0},{2,3},{3,2},{4,5},{5,4},{6,7},{7,6},{8,9},{9,8},{10,11... | collective-permute-start | bytes 86024 | tf_op jit(solution)/shard_map/ppermute | solution.py:376
  8.3 0.1 collective-permute-start.5
  8.4 0.8 %collective-permute-done.refs_0_ = f32[16,448]{1,0:T(8,128)S(1)} collective-permute-done((f32[16,448]{1,0:T(8,128)S(1)}, f32[16,448]{1,0:T(8,128)S(1)}, u32[]{:S(2)}, u32[]{:S(2)}) %collective-permute-start) | collective-permute-done | bytes 28704 | tf_op jit(solution)/shard_map/ppermute | solution.py:376
  9.1 0.0 collective-permute-done.1.outer
  9.1 0.6 %collective-permute-start.2 = (f32[16,384]{1,0:T(8,128)S(1)}, f32[16,384]{1,0:T(8,128)S(1)}, u32[]{:S(2)}, u32[]{:S(2)}) collective-permute-start(f32[16,384]{1,0:T(8,128)S(1)} %slice_add_fusion.order), channel_id=1, source_target_pairs={{0,3},{1,2},{2,1},{3,0},{4,7},{5,6},{6,5},{7,4},{8,11},{9,10},{10,... | collective-permute-start | bytes 73736 | tf_op jit(solution)/shard_map/ppermute | solution.py:376
  9.7 1.2 %collective-permute-start.6 = (bf16[16,8192]{1,0:T(8,128)(2,1)S(1)}, bf16[16,8192]{1,0:T(8,128)(2,1)S(1)}, u32[]{:S(2)}, u32[]{:S(2)}) collective-permute-start(bf16[16,8192]{1,0:T(8,128)(2,1)S(1)} %collective-permute-done.1.outer), channel_id=1, source_target_pairs={{0,8},{1,2},{2,1},{3,4},{4,3},{5,6},{6,5},{7,0},{8,16},{9,10},{10,... | collective-permute-start | bytes 786440 | tf_op jit(solution)/shard_map/ppermute | solution.py:395
  11.0 0.8 %pick_couplings.1.upper_coup = bf16[7,64,64]{2,1,0:T(8,128)(2,1)S(1)} custom-call(f32[16,384]{1,0:T(8,128)S(1)} %slice_add_fusion.order, bf16[64,64,254]{2,1,0:T(8,128)(2,1)S(1)} %bitcast.10, f32[31,16,128]{2,1,0:T(8,128)S(1)} %get-tuple-element.30.refs_0_.coef, bf16[62,64,64]{2,1,0:T(8,128)(2,1)S(1)} %get-tuple-element.31.refs_1_.refs_0_.refs_10_, ...), custom_call_target="tpu_custom_call" | custom-call | flops 6000000000 | bytes 1048576 | tf_op jit(solution)/shard_map/pick_couplings/pallas_call | solution.py:214
  11.7 0.0 slice-start.2
  11.8 0.7 %collective-permute-done.2.refs_1_ = f32[16,384]{1,0:T(8,128)S(1)} collective-permute-done((f32[16,384]{1,0:T(8,128)S(1)}, f32[16,384]{1,0:T(8,128)S(1)}, u32[]{:S(2)}, u32[]{:S(2)}) %collective-permute-start.2) | collective-permute-done | bytes 24608 | tf_op jit(solution)/shard_map/ppermute | solution.py:376
  12.5 0.8 %collective-permute-start.3 = (f32[16,320]{1,0:T(8,128)S(1)}, f32[16,320]{1,0:T(8,128)S(1)}, u32[]{:S(2)}, u32[]{:S(2)}) collective-permute-start(f32[16,320]{1,0:T(8,128)S(1)} %slice_add_fusion.1.order), channel_id=1, source_target_pairs={{0,7},{1,6},{2,5},{3,4},{4,3},{5,2},{6,1},{7,0},{8,15},{9,14},{10,... | collective-permute-start | bytes 61448 | tf_op jit(solution)/shard_map/ppermute | solution.py:376
  13.3 1.3 %far_fields.1 = (f32[31,16,128]{2,1,0:T(8,128)S(1)}, bf16[448,64]{1,0:T(8,128)(2,1)S(1)}, bf16[448,64]{1,0:T(8,128)(2,1)S(1)}) custom-call(f32[16,320]{1,0:T(8,128)S(1)} %slice_add_fusion.1.order, f32[31,16,128]{2,1,0:T(8,128)S(1)} %get-tuple-element.30.refs_0_.coef, bf16[62,64,64]{2,1,0:T(8,128)(2,1)S(1)} %copy-done.2, ...), custom_call_target="tpu_custom_call" | custom-call | flops 6000000000 | bytes 1048576 | tf_op jit(solution)/shard_map/far_fields/pallas_call | solution.py:243
  14.5 2.4 %collective-permute-done.3.refs_2_ = f32[16,320]{1,0:T(8,128)S(1)} collective-permute-done((f32[16,320]{1,0:T(8,128)S(1)}, f32[16,320]{1,0:T(8,128)S(1)}, u32[]{:S(2)}, u32[]{:S(2)}) %collective-permute-start.3) | collective-permute-done | bytes 20512 | tf_op jit(solution)/shard_map/ppermute | solution.py:376
  17.0 1.9 %collective-permute-start.4 = (f32[16,256]{1,0:T(8,128)S(1)}, f32[16,256]{1,0:T(8,128)S(1)}, u32[]{:S(2)}, u32[]{:S(2)}) collective-permute-start(f32[16,256]{1,0:T(8,128)S(1)} %slice_add_fusion.3.order), channel_id=1, source_target_pairs={{0,9},{1,8},{2,11},{3,10},{4,13},{5,12},{6,15},{7,14},{8,1},{9,0},... | collective-permute-start | bytes 49160 | tf_op jit(solution)/shard_map/ppermute | solution.py:376
  18.9 0.0 collective-permute-done.5.inner
  18.9 1.8 %near_field.4.refs_12_ = f32[16,2048]{1,0:T(8,128)S(1)} custom-call(s32[4,32]{1,0:T(4,128)S(1)} %bitcast.6, f32[16,256]{1,0:T(8,128)S(1)} %slice_add_fusion.3.order, bf16[16,8192]{1,0:T(8,128)(2,1)S(1)} %collective-permute-done.5.inner, bf16[16,8192]{1,0:T(8,128)(2,1)S(1)} %get-tuple-element.38.own, bf16[16,8192]{1,0:T(8,128)(2,1)S(1)} %collective-permute-done.1.outer, ...), custom_call_target="tpu_custom_call" | custom-call | flops 1000000000 | bytes 1048576 | tf_op jit(solution)/shard_map/near_field/pallas_call | solution.py:279
  20.7 3.4 %collective-permute-start.7 = (f32[16,192]{1,0:T(8,128)S(1)}, f32[16,192]{1,0:T(8,128)S(1)}, u32[]{:S(2)}, u32[]{:S(2)}) collective-permute-start(f32[16,192]{1,0:T(8,128)S(1)} %slice_add_fusion.2.order), channel_id=1, source_target_pairs={{0,25},{1,24},{2,27},{3,26},{4,29},{5,28},{6,31},{7,30},{8,17},{9,... | collective-permute-start | bytes 36872 | tf_op jit(solution)/shard_map/ppermute | solution.py:376
  24.1 1.7 %near_field.5.refs_13_ = f32[16,2048]{1,0:T(8,128)S(1)} custom-call(s32[4,32]{1,0:T(4,128)S(1)} %bitcast.7, f32[16,192]{1,0:T(8,128)S(1)} %slice_add_fusion.2.order, bf16[16,8192]{1,0:T(8,128)(2,1)S(1)} %collective-permute-done.5.inner, bf16[16,8192]{1,0:T(8,128)(2,1)S(1)} %get-tuple-element.38.own, bf16[16,8192]{1,0:T(8,128)(2,1)S(1)} %collective-permute-done.1.outer, ...), custom_call_target="tpu_custom_call" | custom-call | flops 1000000000 | bytes 1048576 | tf_op jit(solution)/shard_map/near_field/pallas_call | solution.py:279
  25.9 1.4 %collective-permute-start.8 = (f32[16,128]{1,0:T(8,128)S(1)}, f32[16,128]{1,0:T(8,128)S(1)}, u32[]{:S(2)}, u32[]{:S(2)}) collective-permute-start(f32[16,128]{1,0:T(8,128)S(1)} %slice_add_fusion.5.order), channel_id=1, source_target_pairs={{0,33},{1,32},{2,35},{3,34},{4,37},{5,36},{6,39},{7,38},{8,41},{9,... | collective-permute-start | bytes 24584 | tf_op jit(solution)/shard_map/ppermute | solution.py:376
  27.3 1.7 %near_field.6.refs_14_ = f32[16,2048]{1,0:T(8,128)S(1)} custom-call(s32[4,32]{1,0:T(4,128)S(1)} %bitcast.8, f32[16,128]{1,0:T(8,128)S(1)} %slice_add_fusion.5.order, bf16[16,8192]{1,0:T(8,128)(2,1)S(1)} %collective-permute-done.5.inner, bf16[16,8192]{1,0:T(8,128)(2,1)S(1)} %get-tuple-element.38.own, bf16[16,8192]{1,0:T(8,128)(2,1)S(1)} %collective-permute-done.1.outer, ...), custom_call_target="tpu_custom_call" | custom-call | flops 1000000000 | bytes 1048576 | tf_op jit(solution)/shard_map/near_field/pallas_call | solution.py:279
  29.1 2.7 %collective-permute-start.9 = (f32[16,64]{1,0:T(8,128)S(1)}, f32[16,64]{1,0:T(8,128)S(1)}, u32[]{:S(2)}, u32[]{:S(2)}) collective-permute-start(f32[16,64]{1,0:T(8,128)S(1)} %slice_add_fusion.4.order), channel_id=1, source_target_pairs={{0,97},{1,96},{2,99},{3,98},{4,101},{5,100},{6,103},{7,102},{8,105... | collective-permute-start | bytes 12296 | tf_op jit(solution)/shard_map/ppermute | solution.py:376
  31.8 1.7 %near_field.7.refs_15_ = f32[16,2048]{1,0:T(8,128)S(1)} custom-call(s32[4,32]{1,0:T(4,128)S(1)} %bitcast.9, f32[16,64]{1,0:T(8,128)S(1)} %slice_add_fusion.4.order, bf16[16,8192]{1,0:T(8,128)(2,1)S(1)} %collective-permute-done.5.inner, bf16[16,8192]{1,0:T(8,128)(2,1)S(1)} %get-tuple-element.38.own, bf16[16,8192]{1,0:T(8,128)(2,1)S(1)} %collective-permute-done.1.outer, ...), custom_call_target="tpu_custom_call" | custom-call | flops 1000000000 | bytes 1048576 | tf_op jit(solution)/shard_map/near_field/pallas_call | solution.py:279
  33.6 2.1 %down_sweep.1 = f32[16,8192]{1,0:T(8,128)} custom-call(f32[16,448]{1,0:T(8,128)S(1)} %collective-permute-done.refs_0_, f32[16,384]{1,0:T(8,128)S(1)} %collective-permute-done.2.refs_1_, f32[16,320]{1,0:T(8,128)S(1)} %collective-permute-done.3.refs_2_, f32[16,256]{1,0:T(8,128)S(1)} %collective-permute-done.4.refs_3_, ...), custom_call_target="tpu_custom_call" | custom-call | flops 3000000000 | bytes 1048576 | tf_op jit(solution)/shard_map/down_sweep/pallas_call | solution.py:333
  (27 shorter events, 0.1 us)
Async XLA Ops:
  0.0 9.1 %collective-permute-start.1 = (bf16[16,8192]{1,0:T(8,128)(2,1)}, bf16[16,8192]{1,0:T(8,128)(2,1)S(1)}, u32[]{:S(2)}, u32[]{:S(2)}) collective-permute-start(bf16[16,8192]{1,0:T(8,128)(2,1)} %rhs_hbm.1), channel_id=1, source_target_pairs={{0,7},{1,2},{2,1},{3,4},{4,3},{5,6},{6,5},{7,0},{8,15},{9,10},{10,... | collective-permute-start | bytes 786440 | tf_op jit(solution)/shard_map/ppermute | solution.py:359
  2.6 5.7 %copy-start.3 = (bf16[16,8192]{1,0:T(8,128)(2,1)S(1)}, bf16[16,8192]{1,0:T(8,128)(2,1)}, u32[]{:S(2)}) copy-start(bf16[16,8192]{1,0:T(8,128)(2,1)} %rhs_hbm.1) | copy-start | bytes 786436
  2.6 8.4 %copy-start.1 = (bf16[254,64,64]{0,2,1:T(8,128)(2,1)S(1)}, bf16[254,64,64]{0,2,1:T(8,128)(2,1)}, u32[]{:S(2)}) copy-start(bf16[254,64,64]{0,2,1:T(8,128)(2,1)} %param.15) | copy-start | bytes 6242308
  7.1 2.0 %collective-permute-start = (f32[16,448]{1,0:T(8,128)S(1)}, f32[16,448]{1,0:T(8,128)S(1)}, u32[]{:S(2)}, u32[]{:S(2)}) collective-permute-start(f32[16,448]{1,0:T(8,128)S(1)} %get-tuple-element.28), channel_id=1, source_target_pairs={{0,1},{1,0},{2,3},{3,2},{4,5},{5,4},{6,7},{7,6},{8,9},{9,8},{10,11... | collective-permute-start | bytes 86024 | tf_op jit(solution)/shard_map/ppermute | solution.py:376
  8.3 10.6 %collective-permute-start.5 = (bf16[16,8192]{1,0:T(8,128)(2,1)S(1)}, bf16[16,8192]{1,0:T(8,128)(2,1)S(1)}, u32[]{:S(2)}, u32[]{:S(2)}) collective-permute-start(bf16[16,8192]{1,0:T(8,128)(2,1)S(1)} %copy-done.3), channel_id=1, source_target_pairs={{0,1},{1,0},{2,3},{3,2},{4,5},{5,4},{6,7},{7,6},{8,9},{9,8},{10,11... | collective-permute-start | bytes 786440 | tf_op jit(solution)/shard_map/ppermute | solution.py:360
  9.1 3.3 %collective-permute-start.2 = (f32[16,384]{1,0:T(8,128)S(1)}, f32[16,384]{1,0:T(8,128)S(1)}, u32[]{:S(2)}, u32[]{:S(2)}) collective-permute-start(f32[16,384]{1,0:T(8,128)S(1)} %slice_add_fusion.order), channel_id=1, source_target_pairs={{0,3},{1,2},{2,1},{3,0},{4,7},{5,6},{6,5},{7,4},{8,11},{9,10},{10,... | collective-permute-start | bytes 73736 | tf_op jit(solution)/shard_map/ppermute | solution.py:376
  9.7 9.2 %collective-permute-start.6 = (bf16[16,8192]{1,0:T(8,128)(2,1)S(1)}, bf16[16,8192]{1,0:T(8,128)(2,1)S(1)}, u32[]{:S(2)}, u32[]{:S(2)}) collective-permute-start(bf16[16,8192]{1,0:T(8,128)(2,1)S(1)} %collective-permute-done.1.outer), channel_id=1, source_target_pairs={{0,8},{1,2},{2,1},{3,4},{4,3},{5,6},{6,5},{7,0},{8,16},{9,10},{10,... | collective-permute-start | bytes 786440 | tf_op jit(solution)/shard_map/ppermute | solution.py:395
  11.0 2.3 %copy-start.2 = (bf16[62,64,64]{2,1,0:T(8,128)(2,1)S(1)}, bf16[62,64,64]{2,1,0:T(8,128)(2,1)}, u32[]{:S(2)}) copy-start(bf16[62,64,64]{2,1,0:T(8,128)(2,1)} %coup.1) | copy-start | bytes 1523716
  11.0 7.9 %slice-start = ((s8[16777216]{0:T(1024)(128)(4,1)}), s8[4194304]{0:T(1024)(128)(4,1)S(1)}, s32[]{:S(2)}) async-start(s8[16777216]{0:T(1024)(128)(4,1)} %bitcast.4), calls=%async_computation | async-start | bytes 8388608
  11.0 7.9 %slice-start.1 = ((s8[16777216]{0:T(1024)(128)(4,1)}), s8[4194304]{0:T(1024)(128)(4,1)S(1)}, s32[]{:S(2)}) async-start(s8[16777216]{0:T(1024)(128)(4,1)} %bitcast.4), calls=%async_computation.1 | async-start | bytes 8388608
  11.7 7.2 %slice-start.2 = ((s8[16777216]{0:T(1024)(128)(4,1)}), s8[4194304]{0:T(1024)(128)(4,1)S(1)}, s32[]{:S(2)}) async-start(s8[16777216]{0:T(1024)(128)(4,1)} %bitcast.4), calls=%async_computation.2 | async-start | bytes 8388608
  12.5 4.5 %collective-permute-start.3 = (f32[16,320]{1,0:T(8,128)S(1)}, f32[16,320]{1,0:T(8,128)S(1)}, u32[]{:S(2)}, u32[]{:S(2)}) collective-permute-start(f32[16,320]{1,0:T(8,128)S(1)} %slice_add_fusion.1.order), channel_id=1, source_target_pairs={{0,7},{1,6},{2,5},{3,4},{4,3},{5,2},{6,1},{7,0},{8,15},{9,14},{10,... | collective-permute-start | bytes 61448 | tf_op jit(solution)/shard_map/ppermute | solution.py:376
  13.3 5.6 %slice-start.3 = ((s8[16777216]{0:T(1024)(128)(4,1)}), s8[4194304]{0:T(1024)(128)(4,1)S(1)}, s32[]{:S(2)}) async-start(s8[16777216]{0:T(1024)(128)(4,1)} %bitcast.4), calls=%async_computation.3 | async-start | bytes 8388608
  13.3 5.7 %copy-start = (s32[32,4]{0,1:T(4,128)S(1)}, s32[32,4]{0,1:T(4,128)}, u32[]{:S(2)}) copy-start(s32[32,4]{0,1:T(4,128)} %param.11) | copy-start | bytes 1540
  17.0 3.7 %collective-permute-start.4 = (f32[16,256]{1,0:T(8,128)S(1)}, f32[16,256]{1,0:T(8,128)S(1)}, u32[]{:S(2)}, u32[]{:S(2)}) collective-permute-start(f32[16,256]{1,0:T(8,128)S(1)} %slice_add_fusion.3.order), channel_id=1, source_target_pairs={{0,9},{1,8},{2,11},{3,10},{4,13},{5,12},{6,15},{7,14},{8,1},{9,0},... | collective-permute-start | bytes 49160 | tf_op jit(solution)/shard_map/ppermute | solution.py:376
  20.7 5.1 %collective-permute-start.7 = (f32[16,192]{1,0:T(8,128)S(1)}, f32[16,192]{1,0:T(8,128)S(1)}, u32[]{:S(2)}, u32[]{:S(2)}) collective-permute-start(f32[16,192]{1,0:T(8,128)S(1)} %slice_add_fusion.2.order), channel_id=1, source_target_pairs={{0,25},{1,24},{2,27},{3,26},{4,29},{5,28},{6,31},{7,30},{8,17},{9,... | collective-permute-start | bytes 36872 | tf_op jit(solution)/shard_map/ppermute | solution.py:376
  25.9 3.2 %collective-permute-start.8 = (f32[16,128]{1,0:T(8,128)S(1)}, f32[16,128]{1,0:T(8,128)S(1)}, u32[]{:S(2)}, u32[]{:S(2)}) collective-permute-start(f32[16,128]{1,0:T(8,128)S(1)} %slice_add_fusion.5.order), channel_id=1, source_target_pairs={{0,33},{1,32},{2,35},{3,34},{4,37},{5,36},{6,39},{7,38},{8,41},{9,... | collective-permute-start | bytes 24584 | tf_op jit(solution)/shard_map/ppermute | solution.py:376
  29.1 4.5 %collective-permute-start.9 = (f32[16,64]{1,0:T(8,128)S(1)}, f32[16,64]{1,0:T(8,128)S(1)}, u32[]{:S(2)}, u32[]{:S(2)}) collective-permute-start(f32[16,64]{1,0:T(8,128)S(1)} %slice_add_fusion.4.order), channel_id=1, source_target_pairs={{0,97},{1,96},{2,99},{3,98},{4,101},{5,100},{6,103},{7,102},{8,105... | collective-permute-start | bytes 12296 | tf_op jit(solution)/shard_map/ppermute | solution.py:376
